TPU v7x, 256 devices: a whole 4x4x8 slice. The times are simulated.
256 devices in a mesh: cal: 4 (over x_lo, core), row: 8 (over x_hi, y), col: 8 (over z).
Axes of the slice: x: 4 (x_hi: 2, x_lo: 2; x = x_hi * 2 + x_lo), y: 4, z: 8, core: 2. Of those that a mesh axis runs over, the one named last changes fastest.
Arguments:
- acts_one: bfloat16 [3072, 16384], P('cal', ('row', 'col')), may hold values from -40 to 40, as said below
- acts_two: bfloat16 [3072, 16384], P('cal', ('row', 'col')), may hold values from -40 to 40, as said below
Outputs:
- gram_reg: float32 [8, 2048, 8, 8, 256], P('row', 'cal', None, 'col')
- lead_panel: float32 [8, 2048, 512], P('row', 'cal', 'col')
Inputs may be any that keep to these rules, and one draw needn't show every extreme that they name: `acts_one`: calibration activations. `acts_two`: calibration activations.
All inputs are finite; a program needn't handle non-finite values.
Results may differ from a plain program's by a relative error of at most 0.0003.
Values may be sent and summed in bfloat16 or wider, within the bound.
No kernel may reach another device: no remote copies, remote signals or barrier semaphores. Data moves between devices by JAX's collectives and lax.ppermute only.
A program may use at most 128 MiB of HBM per device.

v0:
```python
import jax
import jax.numpy as jnp
from jax import lax
from jax.sharding import PartitionSpec as P

PANEL = 512


reg_alpha = 0.9


def from_root(block, axis, source):
    block = jnp.where(lax.axis_index(axis) == source, block, jnp.zeros_like(block))
    return lax.psum(block, axis)


def per_device(acts_one, acts_two):
    n_row = lax.axis_size("row")
    n_col = lax.axis_size("col")
    n_cal = lax.axis_size("cal")
    piece_width = acts_one.shape[1]
    local = jnp.concatenate([acts_one, acts_two], axis=0)
    total_tokens = local.shape[0] * n_cal
    columns = lax.all_gather(local, "row", axis=1, tiled=True)
    term = lax.dot_general(
        lax.all_gather(local, "col", axis=1, tiled=True),
        columns,
        (((0,), (0,)), ((), ())),
        preferred_element_type=jnp.float32,
    )
    block = lax.psum_scatter(term, "cal", scatter_dimension=0, tiled=True)
    block = block / (1.0 * total_tokens)
    quarter = block.shape[0]
    panel_rows = quarter * n_cal
    row_ids = (
        lax.axis_index("row") * panel_rows
        + lax.axis_index("cal") * quarter
        + jnp.arange(quarter, dtype=jnp.int32)
    )
    outer = jnp.arange(n_row, dtype=jnp.int32)[:, None] * (n_col * piece_width)
    inner = lax.axis_index("col") * piece_width + jnp.arange(piece_width, dtype=jnp.int32)[None, :]
    col_ids = (outer + inner).reshape(-1)
    reg = jnp.where(row_ids[:, None] == col_ids[None, :], block, reg_alpha * block)
    gram_reg = reg.reshape(1, quarter, n_row, 1, piece_width)
    first = lax.all_gather(reg[:, :piece_width], "col", axis=1, tiled=True)[:, :PANEL]
    diag = from_root(first, ("cal", "row"), 0)
    factor = jnp.linalg.cholesky(diag)
    solved = lax.linalg.triangular_solve(
        factor, first, left_side=False, lower=True, transpose_a=True
    )
    padded = jnp.concatenate([factor, jnp.zeros((quarter - PANEL, PANEL), jnp.float32)], axis=0)
    lead = jnp.where(row_ids[:, None] < PANEL, padded, solved)
    col_share = PANEL // n_col
    lead_part = lax.dynamic_slice_in_dim(lead, lax.axis_index("col") * col_share, col_share, 1)
    return (gram_reg, lead_part.reshape(1, quarter, col_share))


def solution(mesh):
    return jax.shard_map(
        per_device,
        mesh=mesh,
        in_specs=(P("cal", ("row", "col")), P("cal", ("row", "col"))),
        out_specs=(P("row", "cal", None, "col", None), P("row", "cal", "col")),
        check_vma=False,
    )
```

profile of v0, /device:TPU:1, one launch (start us, length us, event | category | flops | bytes accessed | tf_op | source)
XLA Modules:
  0.0 691.5 jit_solution(5115819217307622098)
XLA Ops:
  7.2 1.0 constant_dynamic-update-slice_fusion.1
  8.2 1.0 constant_dynamic-update-slice_fusion
  9.3 0.9 copy-done.1
  10.2 0.7 all-gather.6.cloned.1.call-update
  11.0 81.2 %all-gather.4.cloned.1.call-done = bf16[1536,2048]{1,0:T(8,128)(2,1)} async-done(((bf16[1536,256]{1,0:T(8,128)(2,1)}), bf16[1536,2048]{1,0:T(8,128)(2,1)}) %all-gather.4.cloned.1.call-update) | async-done | bytes 6291472 | tf_op jit(solution)/shard_map/all_gather | solution.py:26
  92.2 102.8 %all-gather.6.cloned.1.call-done = bf16[1536,2048]{1,0:T(8,128)(2,1)} async-done(((bf16[1536,256]{1,0:T(8,128)(2,1)}), bf16[1536,2048]{1,0:T(8,128)(2,1)}) %all-gather.6.cloned.1.call-update) | async-done | bytes 6291472 | tf_op jit(solution)/shard_map/all_gather | solution.py:24
  194.9 20.4 %fusion.37 = f32[2048,2048]{0,1:T(8,128)} fusion(bf16[1536,2048]{1,0:T(8,128)(2,1)} %all-gather.4.cloned.1.call-done, bf16[1536,2048]{1,0:T(8,128)(2,1)} %all-gather.6.cloned.1.call-done), kind=kOutput, calls=%fused_computation.85 | convolution fusion | flops 12884901888 | bytes 29360128 | tf_op jit(solution)/shard_map/dot_general | solution.py:25
  215.6 147.6 %reduce-scatter.2.cloned.1.call-done = f32[512,2048]{0,1:T(8,128)} async-done(((f32[2048,2048]{0,1:T(8,128)}), f32[512,2048]{0,1:T(8,128)}) %reduce-scatter.2.cloned.1.call-update) | async-done | bytes 4194320 | tf_op jit(solution)/shard_map/reduce_scatter | solution.py:31
  363.2 2.6 multiply_select_fusion
  365.8 2.0 copy-done
  367.8 0.8 slice.126
  368.7 55.6 %all-gather.8.cloned.1.call-done = f32[512,2048]{0,1:T(8,128)} async-done(((f32[512,256]{0,1:T(8,128)}), f32[512,2048]{0,1:T(8,128)}) %all-gather.8.cloned.1.call-update) | async-done | bytes 4194320 | tf_op jit(solution)/shard_map/all_gather | solution.py:45
  424.3 2.3 slice_select_fusion
  426.7 11.0 %copy.11 = f32[1,512,8,1,256]{4,3,2,1,0:T(1,128)} copy(f32[1,512,8,1,256]{1,4,2,3,0:T(8,128)} %bitcast.56) | data formatting | bytes 8388608
  437.7 103.5 %all-reduce.3.cloned.1.call-done = f32[512,512]{0,1:T(8,128)} async-done(((f32[512,512]{0,1:T(8,128)}), f32[512,512]{0,1:T(8,128)}) %all-reduce.3.cloned.1.call-update) | async-done | bytes 1048592 | tf_op jit(solution)/shard_map/psum | solution.py:14
  541.2 1.6 copy.5
  542.8 1.4 fusion
  544.2 11.7 %cholesky.103 = f32[128,128]{1,0:T(8,128)S(1)} custom-call(f32[128,128]{1,0:T(8,128)S(1)} %cholesky.263), custom_call_target="Cholesky" | custom-call | tf_op jit(solution)/shard_map/jit(cholesky)/cholesky | solution.py:47
  556.1 9.8 %custom-call.30 = f32[1,128,128]{1,2,0:T(8,128)S(1)} custom-call(f32[1,128,128]{2,1,0:T(8,128)S(1)} %get-tuple-element.33), custom_call_target="InvertDiagBlocksLowerTriangular" | custom-call | tf_op jit(solution)/shard_map/jit(cholesky)/cholesky | solution.py:47
  566.0 0.4 constant_dynamic-update-slice_fusion.2
  566.4 0.5 convolution_subtract_fusion.3
  567.0 11.7 %cholesky.215 = f32[128,128]{1,0:T(8,128)S(1)} custom-call(f32[128,128]{1,0:T(8,128)S(1)} %cholesky.267), custom_call_target="Cholesky" | custom-call | tf_op jit(solution)/shard_map/jit(cholesky)/cholesky | solution.py:47
  578.8 10.0 %custom-call.31 = f32[1,128,128]{1,2,0:T(8,128)S(1)} custom-call(f32[1,128,128]{2,1,0:T(8,128)S(1)} %get-tuple-element.31), custom_call_target="InvertDiagBlocksLowerTriangular" | custom-call | tf_op jit(solution)/shard_map/jit(cholesky)/cholesky | solution.py:47
  589.1 0.6 convolution_subtract_fusion.4
  589.8 11.7 %cholesky.236 = f32[128,128]{1,0:T(8,128)S(1)} custom-call(f32[128,128]{1,0:T(8,128)S(1)} %cholesky.272), custom_call_target="Cholesky" | custom-call | tf_op jit(solution)/shard_map/jit(cholesky)/cholesky | solution.py:47
  601.6 9.8 %custom-call.32 = f32[1,128,128]{1,2,0:T(8,128)S(1)} custom-call(f32[1,128,128]{2,1,0:T(8,128)S(1)} %get-tuple-element.29), custom_call_target="InvertDiagBlocksLowerTriangular" | custom-call | tf_op jit(solution)/shard_map/jit(cholesky)/cholesky | solution.py:47
  611.7 0.5 convolution_subtract_fusion.5
  612.2 12.0 %cholesky.253 = f32[128,128]{1,0:T(8,128)S(1)} custom-call(f32[128,128]{1,0:T(8,128)S(1)} %convolution_subtract_fusion.5), custom_call_target="Cholesky" | custom-call | tf_op jit(solution)/shard_map/jit(cholesky)/cholesky | solution.py:47
  624.3 0.6 compare_reduce_fusion.1
  625.0 0.7 compare_reduce_fusion
  625.6 0.7 compare_reduce_fusion.2
  629.1 8.3 %while.1 = (s32[]{:T(128)}, f32[512,512]{0,1:T(8,128)S(1)}, s32[4,2]{0,1:T(2,128)S(1)}, f32[4,128,128]{2,1,0:T(8,128)S(1)}, s32[]{:T(128)}) while((s32[]{:T(128)}, f32[512,512]{0,1:T(8,128)S(1)}, s32[4,2]{0,1:T(2,128)S(1)}, f32[4,128,128]{2,1,0:T(8,128)S(1)}, s32[]{:T(128)}) %tuple.31), condition=%wide.while_cond, body=%wide.while_body.sunk | while | flops 2 | bytes 393329 | solution.py:48
  629.2 0.5 fusion.46
  629.7 1.3 dynamic-slice.7
  631.3 0.5 fusion.46
  631.8 1.3 dynamic-slice.7
  633.3 0.5 fusion.46
  633.9 1.3 dynamic-slice.7
  635.4 0.5 fusion.46
  636.0 1.3 dynamic-slice.7
  637.4 39.3 %custom-call.33 = f32[4,128,128]{1,2,0:T(8,128)S(1)} custom-call(f32[4,128,128]{2,1,0:T(8,128)S(1)} %get-tuple-element.9), custom_call_target="InvertDiagBlocksLowerTriangular" | custom-call | tf_op jit(solution)/shard_map/triangular_solve | solution.py:48
  676.7 1.4 fusion.10
  678.1 1.4 convolution_subtract_fusion.1
  679.5 0.4 fusion.27
  679.9 1.4 convolution_subtract_fusion
  681.3 0.4 fusion.26
  681.7 1.6 convolution_subtract_fusion.2
  683.8 0.7 fusion.21
  (51 shorter events, 3.0 us)
Async XLA Ops:
  7.2 85.0 %all-gather.4.cloned.1.call-start = ((), (), s32[]{:S(2)}) async-start(), calls=%async_computation.1 | async-start | bytes 7077888 | tf_op jit(solution)/shard_map/all_gather | solution.py:26
  9.3 0.9 copy-start.1
  10.2 184.8 %all-gather.6.cloned.1.call-start = ((), (), s32[]{:S(2)}) async-start(), calls=%async_computation.2 | async-start | bytes 7077888 | tf_op jit(solution)/shard_map/all_gather | solution.py:24
  10.9 352.3 %reduce-scatter.2.cloned.1.call-start = ((), (), s32[]{:S(2)}) async-start(), calls=%async_computation.3 | async-start | bytes 20971520 | tf_op jit(solution)/shard_map/reduce_scatter | solution.py:31
  215.4 208.9 %all-gather.8.cloned.1.call-start = ((), (), s32[]{:S(2)}) async-start(), calls=%async_computation.4 | async-start | bytes 4718592 | tf_op jit(solution)/shard_map/all_gather | solution.py:45
  365.8 2.0 copy-start
  368.6 172.6 %all-reduce.3.cloned.1.call-start = ((), (), s32[]{:S(2)}) async-start(), calls=%async_computation.5 | async-start | bytes 2097152 | tf_op jit(solution)/shard_map/psum | solution.py:14
Sparse Core Ops, SparseCore 0:
  10.3 81.8 all-gather.3
  95.2 99.6 all-gather.5
  215.5 147.6 reduce-scatter.1
  368.7 55.5 all-gather.7
  427.7 113.4 all-reduce.2
where the time goes:
time: 698 us; the launch traced here: 691 us
  waiting for transfers between devices  492 us (70%)
  other arithmetic  126 us (18%)
  matrix products  30 us (4%)
  local copies, waits for them, and re-layouts  27 us (4%)
  between operations  17 us (2%)
    reduce_scatter x1, waiting for transfers between devices, per_device(): block = lax.psum_scatter(term, 'cal', scatter_dimension=0, tiled=True)  148 us
    psum x1, waiting for transfers between devices, from_root(): return lax.psum(block, axis)  104 us
    all_gather x1, waiting for transfers between devices, per_device(): columns = lax.all_gather(local, 'row', axis=1, tiled=True)  103 us
    all_gather x1, waiting for transfers between devices, per_device(): lax.all_gather(local, 'col', axis=1, tiled=True)  81.2 us
    another operation x14, other arithmetic, per_device(): factor = jnp.linalg.cholesky(diag)  78.9 us
    all_gather x1, waiting for transfers between devices, per_device(): lax.all_gather(reg[:, :piece_width], 'col', axis=1, tiled=True)[:, :PANEL]  55.6 us
    another operation x3, other arithmetic, per_device(): lax.linalg.triangular_solve(factor, first, left_side=False, lower=True, t...  39.6 us
    dot_general x1, matrix products, per_device(): lax.dot_general(lax.all_gather(local, 'col', axis=1, tiled=True), columns...  20.4 us
  transfers between devices with their start and end apart: 5, of which 5 were waited for; matrix products, arithmetic and copies ran while one was open for 2% of the time, Pallas kernels for 0%

commit v1 on v0

v1 whole, which is shorter than its diff:
```python
import functools

import jax
import jax.numpy as jnp
import numpy as np
from jax import lax
from jax.experimental import pallas as pl
from jax.experimental.pallas import tpu as pltpu
from jax.sharding import PartitionSpec as P

PANEL = 512
reg_alpha = 0.9
AXES = ("cal", "row", "col")
NX, NY, NZ = 4, 4, 8
HIGHEST = lax.Precision.HIGHEST


def flat(x, y, z, core):
    return (((x % 2) * 2 + core) * 8 + (x // 2) * 4 + y) * 8 + z


def devices():
    for x in range(NX):
        for y in range(NY):
            for z in range(NZ):
                for core in range(2):
                    yield x, y, z, core


def move(value, target):
    pairs = []
    for device in devices():
        to = target(*device)
        if to is not None:
            pairs.append((flat(*device), flat(*to)))
    return lax.ppermute(value, AXES, sorted(pairs))


def near(i, size, phase):
    return i ^ 1 if phase == 0 else (i + 1 if i % 2 else i - 1) % size


def x_step(s):
    return lambda x, y, z, c: (near(x, NX, (s + c) % 2), y, z, c)


def y_step(s):
    return lambda x, y, z, c: (x, near(y, NY, (s + c) % 2), z, c)


def z_step(s):
    return lambda x, y, z, c: (x, y, near(z, NZ, (s + c) % 2), c)


def core_swap(x, y, z, c):
    return x, y, z, 1 - c


def row_home(x, y, z, c):
    return (x, y, z, c) if z // 4 == x % 2 else (x ^ 1, y, 7 - z, c)


def tables():
    table = np.zeros((256, 32), np.int32)
    for x, y, z, c in devices():
        def ring4(i):
            p1 = lambda v: near(v, 4, c % 2)
            p2 = lambda v: near(v, 4, (1 + c) % 2)
            return [i, p1(i), p2(i), p1(p2(i))]

        step = lambda v, s: near(v, NZ, (s + c) % 2)
        first = lambda v: [v, step(v, 0)]
        third = lambda v: first(step(step(v, 2), 1))
        slots = first(z) + first(step(z, 1)) + third(z) + third(step(z, 3))
        assert sorted(slots) == list(range(8))
        low = x % 2
        blocks = [(p if p // 4 == low else 7 - p) - 4 * low for p in slots]
        halves = [low if p // 4 == low else 1 - low for p in slots]
        table[flat(x, y, z, c)] = ring4(x) + ring4(y) + blocks + halves + [c, low] + [0] * 6
    return table


TABLE = tables()


def gram_kernel(own, meta, *refs):
    row_refs, first_refs, second_refs = refs[:5], refs[5:9], refs[9:13]
    out_ref, rows, cols, acc, row_sem, col_sem, out_sem = refs[13:]
    tokens = row_refs[0].shape[2]
    half = tokens // 2
    core = meta[24]
    wanted = core if own else 1 - core
    sizes = [r.shape[0] for r in row_refs]
    row_copies = []
    slot = 0
    for ref, size in zip(row_refs, sizes):
        for i in range(size):
            block, side = meta[8 + slot], meta[16 + slot]
            dst = rows.at[
                pl.ds(pl.multiple_of((block % 2) * 256, 256), 256),
                pl.ds(pl.multiple_of(side * tokens, tokens), tokens),
            ]
            row_copies.append(
                (block // 2 == wanted, pltpu.make_async_copy(ref.at[i], dst, row_sem.at[slot]))
            )
            slot += 1
    for want, copy in row_copies:
        pl.when(want)(copy.start)
    col_copies = []
    for j in range(4):
        group = []
        for i in range(4):
            pair = jnp.where(core == 0, i // 2, i % 2)
            side = meta[i] % 2
            for which, ref in ((0, first_refs[j].at[i]), (1, second_refs[i].at[j])):
                dst = cols.at[
                    2 * j + pair,
                    pl.ds(pl.multiple_of(side * tokens + which * half, half), half),
                ]
                copy = pltpu.make_async_copy(ref, dst, col_sem.at[j, i, which])
                copy.start()
                group.append(copy)
        col_copies.append(group)
    for want, copy in row_copies:
        pl.when(want)(copy.wait)
    out_copies = []
    for j in range(4):
        for copy in col_copies[j]:
            copy.wait()
        for pair in range(2):
            x = jnp.where(core == 0, meta[2 * pair], meta[pair])
            a = (x // 2) * 4 + meta[4 + j]
            k = 2 * j + pair
            acc[k] = jnp.dot(rows[...], cols[k], preferred_element_type=jnp.float32)
            copy = pltpu.make_async_copy(acc.at[k], out_ref.at[a], out_sem.at[k])
            copy.start()
            out_copies.append(copy)
    for copy in out_copies:
        copy.wait()


def gram_part(own, meta, row_bufs, first_bufs, second_bufs):
    tokens = row_bufs[0].shape[2]
    any_spec = pl.BlockSpec(memory_space=pl.ANY)
    return pl.pallas_call(
        functools.partial(gram_kernel, own),
        out_shape=jax.ShapeDtypeStruct((8, 512, 256), jnp.float32),
        in_specs=[pl.BlockSpec(memory_space=pltpu.SMEM)] + [any_spec] * 13,
        out_specs=any_spec,
        scratch_shapes=[
            pltpu.VMEM((512, 2 * tokens), jnp.bfloat16),
            pltpu.VMEM((8, 2 * tokens, 256), jnp.bfloat16),
            pltpu.VMEM((8, 512, 256), jnp.float32),
            pltpu.SemaphoreType.DMA((8,)),
            pltpu.SemaphoreType.DMA((4, 4, 2)),
            pltpu.SemaphoreType.DMA((8,)),
        ],
        compiler_params=pltpu.CompilerParams(vmem_limit_bytes=40 * 2**20),
        cost_estimate=pl.CostEstimate(
            flops=2 * 512 * 2048 * 2 * tokens, bytes_accessed=24 * 2**20, transcendentals=0
        ),
    )(meta, *row_bufs, *first_bufs, *second_bufs)


def finish_kernel(scale, rows, where_ref, a_ref, b_ref, out_ref):
    start = where_ref[0] + pl.program_id(0) * rows
    row_ids = start + lax.broadcasted_iota(jnp.int32, (rows, 128), 0)
    lane = lax.broadcasted_iota(jnp.int32, (rows, 128), 1)
    for a in range(8):
        for h in range(2):
            total = a_ref[a, :, h * 128:(h + 1) * 128] + b_ref[a, :, h * 128:(h + 1) * 128]
            total = total * scale
            col_ids = a * 2048 + where_ref[1] + h * 128 + lane
            value = jnp.where(row_ids == col_ids, total, reg_alpha * total)
            out_ref[pl.ds(2 * a + h, rows, stride=16), :] = value


def finish(where, mine, theirs, scale):
    rows = 128
    block = pl.BlockSpec((8, rows, 256), lambda i: (0, i, 0))
    return pl.pallas_call(
        functools.partial(finish_kernel, scale, rows),
        grid=(512 // rows,),
        out_shape=jax.ShapeDtypeStruct((512 * 16, 128), jnp.float32),
        in_specs=[pl.BlockSpec(memory_space=pltpu.SMEM), block, block],
        out_specs=pl.BlockSpec((rows * 16, 128), lambda i: (i, 0)),
        compiler_params=pltpu.CompilerParams(vmem_limit_bytes=32 * 2**20),
        cost_estimate=pl.CostEstimate(flops=2**22, bytes_accessed=12 * 2**20, transcendentals=0),
    )(where, mine, theirs)


def dot_t(a, b):
    return lax.dot_general(
        a, b, (((0,), (0,)), ((), ())), precision=HIGHEST, preferred_element_type=jnp.float32
    )


def dot_n(a, b):
    return lax.dot_general(
        a, b, (((1,), (0,)), ((), ())), precision=HIGHEST, preferred_element_type=jnp.float32
    )


def factor_kernel(scale, g_ref, u_ref, inv_ref, work, block, inv):
    n, nb, np_ = 512, 128, 8
    rid = lax.broadcasted_iota(jnp.int32, (n, n), 0)
    cid = lax.broadcasted_iota(jnp.int32, (n, n), 1)
    total = g_ref[...] * scale
    work[...] = jnp.where(rid == cid, total, reg_alpha * total)
    u_ref[...] = jnp.zeros((n, n), jnp.float32)
    inv_ref[...] = jnp.zeros((n, n), jnp.float32)
    sub = lax.broadcasted_iota(jnp.int32, (np_, nb), 0)
    lane = lax.broadcasted_iota(jnp.int32, (np_, nb), 1)
    eye = (
        lax.broadcasted_iota(jnp.int32, (nb, nb), 0) == lax.broadcasted_iota(jnp.int32, (nb, nb), 1)
    ).astype(jnp.float32)
    for k in range(n // nb):
        lo, hi = k * nb, (k + 1) * nb
        block[...] = work[lo:hi, lo:hi]
        inv[...] = eye

        def panel(p, _):
            base = pl.multiple_of(p * np_, np_)
            v = block[pl.ds(base, np_), :]
            xv = inv[pl.ds(base, np_), :]
            rolled = pltpu.roll(v, lax.rem(nb - base, nb), 1)
            pc = [jnp.broadcast_to(rolled[:, i:i + 1], (np_, nb)) for i in range(np_)]
            for i in range(np_):
                s = lax.rsqrt(pc[i][i:i + 1, :])
                u = v[i:i + 1, :] * s
                xu = xv[i:i + 1, :] * s
                below = jnp.where(sub > i, pc[i] * s, 0.0)
                here = sub == i
                for j in range(i + 1, np_):
                    pc[j] = pc[j] - below * (pc[j][i:i + 1, :] * s)
                v = jnp.where(here, u, v - below * u)
                xv = jnp.where(here, xu, xv - below * xu)
            v = jnp.where(lane >= base + sub, v, 0.0)
            block[pl.ds(base, np_), :] = v
            inv[pl.ds(base, np_), :] = xv
            later = jnp.where(lane >= base + np_, v, 0.0)
            block[...] -= dot_t(later, v)
            inv[...] -= dot_t(later, xv)
            return 0

        lax.fori_loop(0, nb // np_, panel, 0)
        x = inv[...]
        u_ref[lo:hi, lo:hi] = block[...]
        inv_ref[lo:hi, lo:hi] = x
        if k:
            inner = dot_t(u_ref[0:lo, lo:hi], inv_ref[0:lo, 0:lo])
            inv_ref[lo:hi, 0:lo] = -dot_n(x, inner)
        if hi < n:
            right = dot_n(x, work[lo:hi, hi:n])
            u_ref[lo:hi, hi:n] = right
            work[hi:n, hi:n] -= dot_t(right, right)


def factor(g, scale):
    full = pl.BlockSpec(memory_space=pltpu.VMEM)
    shape = jax.ShapeDtypeStruct((512, 512), jnp.float32)
    return pl.pallas_call(
        functools.partial(factor_kernel, scale),
        out_shape=(shape, shape),
        in_specs=[full],
        out_specs=(full, full),
        scratch_shapes=[
            pltpu.VMEM((512, 512), jnp.float32),
            pltpu.VMEM((128, 128), jnp.float32),
            pltpu.VMEM((128, 128), jnp.float32),
        ],
        compiler_params=pltpu.CompilerParams(vmem_limit_bytes=32 * 2**20),
        cost_estimate=pl.CostEstimate(flops=2**30, bytes_accessed=4 * 2**20, transcendentals=512),
    )(g)


def lead_gram(cols, z, core, row):
    other = move(cols, lambda x, y, z, c: (x, y, 1 - z, c) if (x // 2, y) == (0, 0) and z < 2 else None)
    both = jnp.where(z == 0, jnp.concatenate([cols, other], 1), jnp.concatenate([other, cols], 1))
    part = lax.dot_general(
        both, both, (((0,), (0,)), ((), ())), preferred_element_type=jnp.float32
    )
    part = part.reshape(2, 256, 512)
    mine = lax.dynamic_index_in_dim(part, core, 0, keepdims=False)
    away = lax.dynamic_index_in_dim(part, 1 - core, 0, keepdims=False)
    lead = lambda x, y, z: (x // 2, y) == (0, 0) and z < 2
    mine = mine + move(away, lambda x, y, z, c: (x, y, z, 1 - c) if lead(x, y, z) else None)
    mine = mine + move(mine, lambda x, y, z, c: (x ^ 1, y, z, c) if lead(x, y, z) else None)
    mine = jnp.where(row == 0, mine, 0.0)
    mine = mine + move(mine, lambda x, y, z, c: (x + 2, y, z, c) if lead(x, y, z) else None)
    edge = lambda y, z: y == 0 and z < 2
    sent = [
        move(mine, lambda x, y, z, c, to=to: (x, to, z, c) if edge(y, z) else None) for to in (1, 3, 2)
    ]
    mine = mine + (sent[0] + sent[1] + sent[2])
    theirs = move(mine, lambda x, y, z, c: (x, y, z, 1 - c) if z < 2 else None)
    return jnp.where(
        core == 0, jnp.concatenate([mine, theirs], 0), jnp.concatenate([theirs, mine], 0)
    )


def per_device(acts_one, acts_two):
    cal, row, z = (lax.axis_index(a) for a in AXES)
    core = cal % 2
    total_tokens = 8 * acts_one.shape[0]
    scale = 1.0 / total_tokens
    device = (cal * 8 + row) * 8 + z
    meta = lax.dynamic_index_in_dim(jnp.asarray(TABLE), device, 0, keepdims=False)

    lead = lead_gram(jnp.concatenate([acts_one, acts_two], 0), z, core, row)
    upper, inverse = factor(lead, scale)

    piece = jnp.concatenate([acts_one.T, acts_two.T], 1)[None]
    r0 = move(piece, row_home)
    r1 = move(r0, z_step(0))
    r2 = move(jnp.concatenate([r0, r1], 0), z_step(1))
    r3 = move(r2, z_step(2))
    r4 = move(r3, z_step(3))
    row_bufs = (r0, r1, r2, r3, r4)

    def ring(value, step):
        one = move(value, step(0))
        return value, one, move(value, step(1)), move(one, step(1))

    first = jnp.concatenate(ring(acts_one[None], x_step), 0)
    second = jnp.concatenate(ring(acts_two[None], y_step), 0)
    first_bufs = ring(first, y_step)
    second_bufs = ring(second, x_step)

    theirs = gram_part(False, meta, row_bufs, first_bufs, second_bufs)
    mine = gram_part(True, meta, row_bufs, first_bufs, second_bufs)
    theirs = move(theirs, core_swap)

    row_start = row * 2048 + cal * 512
    where = jnp.stack([row_start, z * 256]).astype(jnp.int32)
    gram_reg = finish(where, mine, theirs, scale)

    block = (mine[0] + theirs[0]) * scale
    row_ids = row_start + jnp.arange(512, dtype=jnp.int32)[:, None]
    col_ids = z * 256 + jnp.arange(256, dtype=jnp.int32)[None, :]
    block = jnp.where(row_ids == col_ids, block, reg_alpha * block)
    weights = jnp.where(z == 0, inverse[:, :256], inverse[:, 256:])
    solved = lax.dot_general(
        weights, block, (((1,), (1,)), ((), ())), precision=HIGHEST,
        preferred_element_type=jnp.float32,
    )
    head = jnp.where(z == 0, upper, 0.0)
    solved = jnp.where((row == 0) & (cal == 0), head, solved).reshape(8, 64, 512)
    share = jnp.where(z == 0, solved[0], 0.0)
    for to in range(1, 8):
        extra = to + 3 if to < 5 else None

        def target(x, y, z, c, to=to, extra=extra):
            if z == 0:
                return x, y, to, c
            return (x, y, extra, c) if z == 1 and extra is not None else None

        value = solved[to] if extra is None else jnp.where(z == 0, solved[to], solved[extra])
        share = share + move(value, target)
    return gram_reg.reshape(1, 512, 8, 1, 256), share.T.reshape(1, 512, 64)


def solution(mesh):
    return jax.shard_map(
        per_device,
        mesh=mesh,
        in_specs=(P("cal", ("row", "col")), P("cal", ("row", "col"))),
        out_specs=(P("row", "cal", None, "col", None), P("row", "cal", "col")),
        check_vma=False,
    )
```

time: 698 us -> 337 us (0.48)
  waiting for transfers between devices: 492 us -> 90.8 us
  starting transfers between devices: 0.2 us -> 154 us
  other arithmetic: 126 us -> 7.78 us
  Pallas kernels: 0 us -> 68.5 us
  matrix products: 30 us -> 6.58 us
  local copies, waits for them, and re-layouts: 27 us -> 5.97 us
  between operations: 17 us -> 1.2 us
    all_gather x3 -> x0, waiting for transfers between devices: 240 us -> none  [the longest x1 103 us: per_device(): columns = lax.all_gather(local, 'row', axis=1, tiled=True)]
    ppermute x0 -> x33, starting transfers between devices: none -> 154 us  [move(): return lax.ppermute(value, AXES, sorted(pairs))]
    reduce_scatter x1 -> x0, waiting for transfers between devices: 148 us -> none  [per_device(): block = lax.psum_scatter(term, 'cal', scatter_dimension=0, tiled=True)]
    another operation x17 -> x1, other arithmetic: 118 us -> 0.08 us  [per_device(): where = jnp.stack([row_start, z * 256]).astype(jnp.int32)]
    psum x1 -> x0, waiting for transfers between devices: 104 us -> none  [from_root(): return lax.psum(block, axis)]
    ppermute x0 -> x33, waiting for transfers between devices: none -> 90.8 us  [move(): return lax.ppermute(value, AXES, sorted(pairs))]
    pallas_call x0 -> x4, Pallas kernels: none -> 68.5 us  [the longest x1 38.8 us: factor(): pl.pallas_call(functools.partial(factor_kernel, scale), out_shape=(shape,...]
    dot_general x1 -> x2, matrix products: 20.4 us -> 6.58 us  [the longest x1 3.98 us: lead_gram(): lax.dot_general(both, both, (((0,), (0,)), ((), ())), preferred_element_t...]
  transfers between devices with their start and end apart: 5 -> 33, of which waited for: 5 -> 13; matrix products, arithmetic and copies ran while one was open for 2% -> 4% of each run, Pallas kernels for 0% -> 20%
where the time goes in v1:
time: 337 us; the launch traced here: 334 us
  starting transfers between devices  154 us (46%)
  waiting for transfers between devices  90.8 us (27%)
  Pallas kernels  68.5 us (20%)
  other arithmetic  7.78 us (2%)
  matrix products  6.58 us (2%)
  local copies, waits for them, and re-layouts  5.97 us (2%)
    ppermute x33, starting transfers between devices, move(): return lax.ppermute(value, AXES, sorted(pairs))  154 us
    ppermute x33, waiting for transfers between devices, move(): return lax.ppermute(value, AXES, sorted(pairs))  90.8 us
    pallas_call x1, Pallas kernels, factor(): pl.pallas_call(functools.partial(factor_kernel, scale), out_shape=(shape,...  38.8 us
    pallas_call x2, Pallas kernels, gram_part(): pl.pallas_call(functools.partial(gram_kernel, own), out_shape=jax.ShapeDt...  23.8 us
  transfers between devices with their start and end apart: 33, of which 13 were waited for; matrix products, arithmetic and copies ran while one was open for 4% of the time, Pallas kernels for 20%

profile of v1, /device:TPU:1, one launch (start us, length us, event | category | flops | bytes accessed | tf_op | source)
XLA Modules:
  0.0 334.4 jit_solution(7853839778651282430)
XLA Ops:
  0.6 1.2 copy.6
  1.8 1.2 copy.5
  3.9 44.9 %collective-permute-start.1 = (bf16[1,256,1536]{2,1,0:T(8,128)(2,1)S(1)}, bf16[1,256,1536]{2,1,0:T(8,128)(2,1)S(1)}, u32[]{:S(2)}, u32[]{:S(2)}) collective-permute-start(bf16[1,256,1536]{2,1,0:T(8,128)(2,1)S(1)} %collective-permute-done.refs_0_), channel_id=1, source_target_pairs={{0,1},{1,0},{2,3},{3,2},{4,5},{5,4},{6,7},{7,6},{8,9},{9,8},{10,11... | collective-permute-start | bytes 2359304 | tf_op jit(solution)/shard_map/ppermute | solution.py:36
  48.9 9.4 %collective-permute-done.1.refs_1_ = bf16[1,256,1536]{2,1,0:T(8,128)(2,1)S(1)} collective-permute-done((bf16[1,256,1536]{2,1,0:T(8,128)(2,1)S(1)}, bf16[1,256,1536]{2,1,0:T(8,128)(2,1)S(1)}, u32[]{:S(2)}, u32[]{:S(2)}) %collective-permute-start.1) | collective-permute-done | bytes 786464 | tf_op jit(solution)/shard_map/ppermute | solution.py:36
  59.1 2.5 collective-permute-start.5
  61.6 2.7 collective-permute-start.11
  64.4 2.9 collective-permute-done.5
  67.3 1.3 collective-permute-start.12
  68.6 1.2 collective-permute-done.11
  69.8 5.3 %collective-permute-done.6 = bf16[1,768,256]{2,1,0:T(8,128)(2,1)S(1)} collective-permute-done((bf16[1,768,256]{2,1,0:T(8,128)(2,1)S(1)}, bf16[1,768,256]{2,1,0:T(8,128)(2,1)S(1)}, u32[]{:S(2)}, u32[]{:S(2)}) %collective-permute-start.6) | collective-permute-done | bytes 393248 | tf_op jit(solution)/shard_map/ppermute | solution.py:36
  75.2 4.2 %collective-permute-done.7 = bf16[1,768,256]{2,1,0:T(8,128)(2,1)S(1)} collective-permute-done((bf16[1,768,256]{2,1,0:T(8,128)(2,1)S(1)}, bf16[1,768,256]{2,1,0:T(8,128)(2,1)S(1)}, u32[]{:S(2)}, u32[]{:S(2)}) %collective-permute-start.7) | collective-permute-done | bytes 393248 | tf_op jit(solution)/shard_map/ppermute | solution.py:36
  80.2 2.8 collective-permute-start.14
  83.9 1.1 copy-done.7
  85.1 5.3 %collective-permute-start.18 = (bf16[1536,256]{1,0:T(8,128)(2,1)S(1)}, bf16[1536,256]{1,0:T(8,128)(2,1)S(1)}, u32[]{:S(2)}, u32[]{:S(2)}) collective-permute-start(bf16[1536,256]{1,0:T(8,128)(2,1)S(1)} %constant_dynamic-update-slice_fusion), channel_id=1, source_target_pairs={{0,1},{1,0},{64,65},{65,64},{128,129},{129,128},{192,193},{193,192}} | collective-permute-start | bytes 2359304 | tf_op jit(solution)/shard_map/ppermute | solution.py:36
  90.5 9.7 %collective-permute-done.18 = bf16[1536,256]{1,0:T(8,128)(2,1)S(1)} collective-permute-done((bf16[1536,256]{1,0:T(8,128)(2,1)S(1)}, bf16[1536,256]{1,0:T(8,128)(2,1)S(1)}, u32[]{:S(2)}, u32[]{:S(2)}) %collective-permute-start.18) | collective-permute-done | bytes 786464 | tf_op jit(solution)/shard_map/ppermute | solution.py:36
  100.2 6.4 %collective-permute-start.15 = (bf16[4,768,256]{2,1,0:T(8,128)(2,1)S(1)}, bf16[4,768,256]{2,1,0:T(8,128)(2,1)}, u32[]{:S(2)}, u32[]{:S(2)}) collective-permute-start(bf16[4,768,256]{2,1,0:T(8,128)(2,1)S(1)} %pad_maximum_fusion.2.refs_9_), channel_id=1, source_target_pairs={{0,160},{1,161},{2,162},{3,163},{4,164},{5,165},{6,166},{7,167},{8... | collective-permute-start | bytes 4718600 | tf_op jit(solution)/shard_map/ppermute | solution.py:36
  106.7 2.9 collective-permute-start.10
  110.5 4.0 %fusion = f32[512,512]{1,0:T(8,128)S(1)} fusion(bf16[1536,256]{1,0:T(8,128)(2,1)} %copy-done.14, bf16[1536,256]{1,0:T(8,128)(2,1)} %copy-done.13, pred[]{:T(512)S(6)} %eq.16), kind=kOutput, calls=%fused_computation.4 | convolution fusion | flops 812384256 | bytes 2621441 | tf_op jit(solution)/shard_map/dot_general | solution.py:280
  115.4 6.1 %collective-permute-done.9.refs_7_ = bf16[4,768,256]{2,1,0:T(8,128)(2,1)} collective-permute-done((bf16[4,768,256]{2,1,0:T(8,128)(2,1)S(1)}, bf16[4,768,256]{2,1,0:T(8,128)(2,1)}, u32[]{:S(2)}, u32[]{:S(2)}) %collective-permute-start.9) | collective-permute-done | bytes 1572896 | tf_op jit(solution)/shard_map/ppermute | solution.py:36
  121.5 34.0 %collective-permute-start.19 = (f32[256,512]{1,0:T(8,128)}, f32[256,512]{1,0:T(8,128)}, u32[]{:S(2)}, u32[]{:S(2)}) collective-permute-start(f32[256,512]{1,0:T(8,128)} %dynamic-slice_bitcast_fusion), channel_id=1, source_target_pairs={{0,64},{1,65},{64,0},{65,1},{128,192},{129,193},{192,128},{193,129}} | collective-permute-start | bytes 1572872 | tf_op jit(solution)/shard_map/ppermute | solution.py:36
  155.6 11.9 %shard_map.51 = f32[8,512,256]{2,1,0:T(8,128)} custom-call(s32[32]{0:T(128)S(1)} %fusion.27.meta, bf16[1,256,1536]{2,1,0:T(8,128)(2,1)S(1)} %copy-done.2, bf16[1,256,1536]{2,1,0:T(8,128)(2,1)S(1)} %copy-done.5, bf16[2,256,1536]{2,1,0:T(8,128)(2,1)S(1)} %copy-done.8, bf16[2,256,1536]{2,1,0:T(8,128)(2,1)} %collective-permute-done.3.refs_3_, ...), custom_call_target="tpu_custom_call" | custom-call | flops 6442450944 | bytes 25165824 | tf_op jit(solution)/shard_map/pallas_call | solution.py:145
  167.5 27.6 %collective-permute-start.17 = (f32[8,512,256]{2,1,0:T(8,128)}, f32[8,512,256]{2,1,0:T(8,128)}, u32[]{:S(2)}, u32[]{:S(2)}) collective-permute-start(f32[8,512,256]{2,1,0:T(8,128)} %shard_map.51), channel_id=1, source_target_pairs={{0,64},{1,65},{2,66},{3,67},{4,68},{5,69},{6,70},{7,71},{8,72},{9,... | collective-permute-start | bytes 12582920 | tf_op jit(solution)/shard_map/ppermute | solution.py:36
  195.2 2.1 bitcast_add_fusion
  197.3 2.3 collective-permute-start.20
  199.7 13.4 %collective-permute-done.20 = f32[256,512]{1,0:T(8,128)} collective-permute-done((f32[256,512]{1,0:T(8,128)}, f32[256,512]{1,0:T(8,128)}, u32[]{:S(2)}, u32[]{:S(2)}) %collective-permute-start.20) | collective-permute-done | bytes 524320 | tf_op jit(solution)/shard_map/ppermute | solution.py:36
  213.0 1.3 add_select_fusion
  214.3 1.3 collective-permute-start.21
  215.7 10.7 %collective-permute-done.21 = f32[256,512]{1,0:T(8,128)S(1)} collective-permute-done((f32[256,512]{1,0:T(8,128)S(1)}, f32[256,512]{1,0:T(8,128)S(1)}, u32[]{:S(2)}, u32[]{:S(2)}) %collective-permute-start.21) | collective-permute-done | bytes 524320 | tf_op jit(solution)/shard_map/ppermute | solution.py:36
  226.4 1.3 collective-permute-start.24
  227.8 1.3 collective-permute-start.22
  229.1 1.3 collective-permute-start.23
  230.4 7.4 %collective-permute-done.24 = f32[256,512]{1,0:T(8,128)S(1)} collective-permute-done((f32[256,512]{1,0:T(8,128)S(1)}, f32[256,512]{1,0:T(8,128)S(1)}, u32[]{:S(2)}, u32[]{:S(2)}) %collective-permute-start.24) | collective-permute-done | bytes 524320 | tf_op jit(solution)/shard_map/ppermute | solution.py:36
  237.8 11.2 %collective-permute-done.22 = f32[256,512]{1,0:T(8,128)S(1)} collective-permute-done((f32[256,512]{1,0:T(8,128)S(1)}, f32[256,512]{1,0:T(8,128)S(1)}, u32[]{:S(2)}, u32[]{:S(2)}) %collective-permute-start.22) | collective-permute-done | bytes 524320 | tf_op jit(solution)/shard_map/ppermute | solution.py:36
  250.1 3.9 %collective-permute-start.25 = (f32[256,512]{1,0:T(8,128)}, f32[256,512]{1,0:T(8,128)}, u32[]{:S(2)}, u32[]{:S(2)}) collective-permute-start(f32[256,512]{1,0:T(8,128)} %add_add_fusion), channel_id=1, source_target_pairs={{0,64},{1,65},{8,72},{9,73},{16,80},{17,81},{24,88},{25,89},{32,96... | collective-permute-start | bytes 1572872 | tf_op jit(solution)/shard_map/ppermute | solution.py:36
  254.1 1.8 collective-permute-done.25
  255.9 1.7 maximum_select_fusion.2.g_ref
  257.7 38.8 %shard_map.53 = (f32[512,512]{1,0:T(8,128)S(1)}, f32[512,512]{1,0:T(8,128)S(1)}) custom-call(f32[512,512]{1,0:T(8,128)S(1)} %maximum_select_fusion.2.g_ref), custom_call_target="tpu_custom_call" | custom-call | flops 1073741824 | bytes 4194304 | tf_op jit(solution)/shard_map/pallas_call | solution.py:262
  296.5 11.9 %shard_map.50.a_ref = f32[8,512,256]{2,1,0:T(8,128)} custom-call(s32[32]{0:T(128)S(1)} %fusion.27.meta, bf16[1,256,1536]{2,1,0:T(8,128)(2,1)S(1)} %copy-done.3, bf16[1,256,1536]{2,1,0:T(8,128)(2,1)S(1)} %copy-done.6, bf16[2,256,1536]{2,1,0:T(8,128)(2,1)S(1)} %copy-done.9, bf16[2,256,1536]{2,1,0:T(8,128)(2,1)} %collective-permute-done.3.refs_3_, ...), custom_call_target="tpu_custom_call" | custom-call | flops 6442450944 | bytes 25165824 | tf_op jit(solution)/shard_map/pallas_call | solution.py:145
  308.4 2.6 convolution_select_fusion
  311.1 1.3 collective-permute-start.32
  312.4 1.3 collective-permute-start.31
  313.7 1.3 collective-permute-start.30
  315.0 1.3 collective-permute-start.29
  316.3 1.3 collective-permute-start.28
  317.6 1.3 collective-permute-start.27
  318.9 7.4 %collective-permute-done.31 = f32[64,512]{1,0:T(8,128)S(1)} collective-permute-done((f32[64,512]{1,0:T(8,128)S(1)}, f32[64,512]{1,0:T(8,128)S(1)}, u32[]{:S(2)}, u32[]{:S(2)}) %collective-permute-start.31) | collective-permute-done | bytes 131104 | tf_op jit(solution)/shard_map/ppermute | solution.py:36
  326.4 1.3 collective-permute-start.26
  327.7 5.9 %shard_map.52 = f32[8192,128]{1,0:T(8,128)} custom-call(s32[2]{0:T(128)S(1)} %pad_add_fusion.where_ref, f32[8,512,256]{2,1,0:T(8,128)S(1)} %copy-done, f32[8,512,256]{2,1,0:T(8,128)} %collective-permute-done.17.b_ref), custom_call_target="tpu_custom_call" | custom-call | flops 4194304 | bytes 12582912 | tf_op jit(solution)/shard_map/pallas_call | solution.py:181
  (74 shorter events, 7.6 us)
Async XLA Ops:
  3.0 56.1 %copy-start.10 = (bf16[768,256]{1,0:T(8,128)(2,1)S(1)}, bf16[768,256]{1,0:T(8,128)(2,1)}, u32[]{:S(2)}) copy-start(bf16[768,256]{1,0:T(8,128)(2,1)} %param.3) | copy-start | bytes 1179652
  3.0 58.6 %copy-start.11 = (bf16[768,256]{1,0:T(8,128)(2,1)S(1)}, bf16[768,256]{1,0:T(8,128)(2,1)}, u32[]{:S(2)}) copy-start(bf16[768,256]{1,0:T(8,128)(2,1)} %param.4) | copy-start | bytes 1179652
  3.1 0.9 collective-permute-start
  3.9 54.5 %copy-start.1 = (bf16[1,256,1536]{2,1,0:T(8,128)(2,1)}, bf16[1,256,1536]{2,1,0:T(8,128)(2,1)S(1)}, u32[]{:S(2)}) copy-start(bf16[1,256,1536]{2,1,0:T(8,128)(2,1)S(1)} %collective-permute-done.refs_0_) | copy-start | bytes 2359300
  3.9 54.3 %collective-permute-start.1 = (bf16[1,256,1536]{2,1,0:T(8,128)(2,1)S(1)}, bf16[1,256,1536]{2,1,0:T(8,128)(2,1)S(1)}, u32[]{:S(2)}, u32[]{:S(2)}) collective-permute-start(bf16[1,256,1536]{2,1,0:T(8,128)(2,1)S(1)} %collective-permute-done.refs_0_), channel_id=1, source_target_pairs={{0,1},{1,0},{2,3},{3,2},{4,5},{5,4},{6,7},{7,6},{8,9},{9,8},{10,11... | collective-permute-start | bytes 2359304 | tf_op jit(solution)/shard_map/ppermute | solution.py:36
  58.2 0.9 copy-start.4
  59.1 23.9 %collective-permute-start.2 = (bf16[2,256,1536]{2,1,0:T(8,128)(2,1)S(1)}, bf16[2,256,1536]{2,1,0:T(8,128)(2,1)S(1)}, u32[]{:S(2)}, u32[]{:S(2)}) collective-permute-start(bf16[2,256,1536]{2,1,0:T(8,128)(2,1)S(1)} %pad_maximum_fusion), channel_id=1, source_target_pairs={{0,7},{1,2},{2,1},{3,4},{4,3},{5,6},{6,5},{7,0},{8,15},{9,10},{10,... | collective-permute-start | bytes 4718600 | tf_op jit(solution)/shard_map/ppermute | solution.py:36
  59.1 8.1 %collective-permute-start.5 = (bf16[1,768,256]{2,1,0:T(8,128)(2,1)S(1)}, bf16[1,768,256]{2,1,0:T(8,128)(2,1)S(1)}, u32[]{:S(2)}, u32[]{:S(2)}) collective-permute-start(bf16[1,768,256]{2,1,0:T(8,128)(2,1)S(1)} %bitcast.29), channel_id=1, source_target_pairs={{0,128},{1,129},{2,130},{3,131},{4,132},{5,133},{6,134},{7,135},{8... | collective-permute-start | bytes 1179656 | tf_op jit(solution)/shard_map/ppermute | solution.py:36
  61.6 8.2 %collective-permute-start.11 = (bf16[1,768,256]{2,1,0:T(8,128)(2,1)S(1)}, bf16[1,768,256]{2,1,0:T(8,128)(2,1)S(1)}, u32[]{:S(2)}, u32[]{:S(2)}) collective-permute-start(bf16[1,768,256]{2,1,0:T(8,128)(2,1)S(1)} %bitcast.32), channel_id=1, source_target_pairs={{0,8},{1,9},{2,10},{3,11},{4,12},{5,13},{6,14},{7,15},{8,0},{9,1},... | collective-permute-start | bytes 1179656 | tf_op jit(solution)/shard_map/ppermute | solution.py:36
  64.4 10.8 %collective-permute-start.6 = (bf16[1,768,256]{2,1,0:T(8,128)(2,1)S(1)}, bf16[1,768,256]{2,1,0:T(8,128)(2,1)S(1)}, u32[]{:S(2)}, u32[]{:S(2)}) collective-permute-start(bf16[1,768,256]{2,1,0:T(8,128)(2,1)S(1)} %bitcast.30), channel_id=1, source_target_pairs={{0,160},{1,161},{2,162},{3,163},{4,164},{5,165},{6,166},{7,167},{8... | collective-permute-start | bytes 1179656 | tf_op jit(solution)/shard_map/ppermute | solution.py:36
  67.3 12.1 %collective-permute-start.7 = (bf16[1,768,256]{2,1,0:T(8,128)(2,1)S(1)}, bf16[1,768,256]{2,1,0:T(8,128)(2,1)S(1)}, u32[]{:S(2)}, u32[]{:S(2)}) collective-permute-start(bf16[1,768,256]{2,1,0:T(8,128)(2,1)S(1)} %collective-permute-done.5), channel_id=1, source_target_pairs={{0,160},{1,161},{2,162},{3,163},{4,164},{5,165},{6,166},{7,167},{8... | collective-permute-start | bytes 1179656 | tf_op jit(solution)/shard_map/ppermute | solution.py:36
  67.3 12.7 %collective-permute-start.12 = (bf16[1,768,256]{2,1,0:T(8,128)(2,1)S(1)}, bf16[1,768,256]{2,1,0:T(8,128)(2,1)S(1)}, u32[]{:S(2)}, u32[]{:S(2)}) collective-permute-start(bf16[1,768,256]{2,1,0:T(8,128)(2,1)S(1)} %bitcast.33), channel_id=1, source_target_pairs={{0,24},{1,25},{2,26},{3,27},{4,28},{5,29},{6,30},{7,31},{8,16},{9,... | collective-permute-start | bytes 1179656 | tf_op jit(solution)/shard_map/ppermute | solution.py:36
  69.8 10.2 %collective-permute-start.13 = (bf16[1,768,256]{2,1,0:T(8,128)(2,1)S(1)}, bf16[1,768,256]{2,1,0:T(8,128)(2,1)S(1)}, u32[]{:S(2)}, u32[]{:S(2)}) collective-permute-start(bf16[1,768,256]{2,1,0:T(8,128)(2,1)S(1)} %collective-permute-done.11), channel_id=1, source_target_pairs={{0,24},{1,25},{2,26},{3,27},{4,28},{5,29},{6,30},{7,31},{8,16},{9,... | collective-permute-start | bytes 1179656 | tf_op jit(solution)/shard_map/ppermute | solution.py:36
  79.6 27.1 %collective-permute-start.8 = (bf16[4,768,256]{2,1,0:T(8,128)(2,1)S(1)}, bf16[4,768,256]{2,1,0:T(8,128)(2,1)}, u32[]{:S(2)}, u32[]{:S(2)}) collective-permute-start(bf16[4,768,256]{2,1,0:T(8,128)(2,1)S(1)} %pad_maximum_fusion.1.refs_5_), channel_id=1, source_target_pairs={{0,8},{1,9},{2,10},{3,11},{4,12},{5,13},{6,14},{7,15},{8,0},{9,1},... | collective-permute-start | bytes 4718600 | tf_op jit(solution)/shard_map/ppermute | solution.py:36
  80.2 29.4 %collective-permute-start.14 = (bf16[4,768,256]{2,1,0:T(8,128)(2,1)S(1)}, bf16[4,768,256]{2,1,0:T(8,128)(2,1)}, u32[]{:S(2)}, u32[]{:S(2)}) collective-permute-start(bf16[4,768,256]{2,1,0:T(8,128)(2,1)S(1)} %pad_maximum_fusion.2.refs_9_), channel_id=1, source_target_pairs={{0,128},{1,129},{2,130},{3,131},{4,132},{5,133},{6,134},{7,135},{8... | collective-permute-start | bytes 4718600 | tf_op jit(solution)/shard_map/ppermute | solution.py:36
  83.0 26.6 %collective-permute-start.3 = (bf16[2,256,1536]{2,1,0:T(8,128)(2,1)S(1)}, bf16[2,256,1536]{2,1,0:T(8,128)(2,1)}, u32[]{:S(2)}, u32[]{:S(2)}) collective-permute-start(bf16[2,256,1536]{2,1,0:T(8,128)(2,1)S(1)} %collective-permute-done.2.refs_2_), channel_id=1, source_target_pairs={{0,1},{1,0},{2,3},{3,2},{4,5},{5,4},{6,7},{7,6},{8,9},{9,8},{10,11... | collective-permute-start | bytes 4718600 | tf_op jit(solution)/shard_map/ppermute | solution.py:36
  83.9 1.1 copy-start.7
  85.1 24.5 %copy-start.13 = (bf16[1536,256]{1,0:T(8,128)(2,1)}, bf16[1536,256]{1,0:T(8,128)(2,1)S(1)}, u32[]{:S(2)}) copy-start(bf16[1536,256]{1,0:T(8,128)(2,1)S(1)} %constant_dynamic-update-slice_fusion) | copy-start | bytes 2359300
  85.1 15.1 %collective-permute-start.18 = (bf16[1536,256]{1,0:T(8,128)(2,1)S(1)}, bf16[1536,256]{1,0:T(8,128)(2,1)S(1)}, u32[]{:S(2)}, u32[]{:S(2)}) collective-permute-start(bf16[1536,256]{1,0:T(8,128)(2,1)S(1)} %constant_dynamic-update-slice_fusion), channel_id=1, source_target_pairs={{0,1},{1,0},{64,65},{65,64},{128,129},{129,128},{192,193},{193,192}} | collective-permute-start | bytes 2359304 | tf_op jit(solution)/shard_map/ppermute | solution.py:36
  90.4 31.1 %collective-permute-start.9 = (bf16[4,768,256]{2,1,0:T(8,128)(2,1)S(1)}, bf16[4,768,256]{2,1,0:T(8,128)(2,1)}, u32[]{:S(2)}, u32[]{:S(2)}) collective-permute-start(bf16[4,768,256]{2,1,0:T(8,128)(2,1)S(1)} %pad_maximum_fusion.1.refs_5_), channel_id=1, source_target_pairs={{0,24},{1,25},{2,26},{3,27},{4,28},{5,29},{6,30},{7,31},{8,16},{9,... | collective-permute-start | bytes 4718600 | tf_op jit(solution)/shard_map/ppermute | solution.py:36
  100.2 9.5 %copy-start.14 = (bf16[1536,256]{1,0:T(8,128)(2,1)}, bf16[1536,256]{1,0:T(8,128)(2,1)S(1)}, u32[]{:S(2)}) copy-start(bf16[1536,256]{1,0:T(8,128)(2,1)S(1)} %collective-permute-done.18) | copy-start | bytes 2359300
  100.2 55.3 %collective-permute-start.15 = (bf16[4,768,256]{2,1,0:T(8,128)(2,1)S(1)}, bf16[4,768,256]{2,1,0:T(8,128)(2,1)}, u32[]{:S(2)}, u32[]{:S(2)}) collective-permute-start(bf16[4,768,256]{2,1,0:T(8,128)(2,1)S(1)} %pad_maximum_fusion.2.refs_9_), channel_id=1, source_target_pairs={{0,160},{1,161},{2,162},{3,163},{4,164},{5,165},{6,166},{7,167},{8... | collective-permute-start | bytes 4718600 | tf_op jit(solution)/shard_map/ppermute | solution.py:36
  106.7 48.9 %collective-permute-start.10 = (bf16[4,768,256]{2,1,0:T(8,128)(2,1)}, bf16[4,768,256]{2,1,0:T(8,128)(2,1)}, u32[]{:S(2)}, u32[]{:S(2)}) collective-permute-start(bf16[4,768,256]{2,1,0:T(8,128)(2,1)} %collective-permute-done.8.refs_6_), channel_id=1, source_target_pairs={{0,24},{1,25},{2,26},{3,27},{4,28},{5,29},{6,30},{7,31},{8,16},{9,... | collective-permute-start | bytes 4718600 | tf_op jit(solution)/shard_map/ppermute | solution.py:36
  109.6 46.0 %collective-permute-start.16 = (bf16[4,768,256]{2,1,0:T(8,128)(2,1)}, bf16[4,768,256]{2,1,0:T(8,128)(2,1)}, u32[]{:S(2)}, u32[]{:S(2)}) collective-permute-start(bf16[4,768,256]{2,1,0:T(8,128)(2,1)} %collective-permute-done.14.refs_10_), channel_id=1, source_target_pairs={{0,160},{1,161},{2,162},{3,163},{4,164},{5,165},{6,166},{7,167},{8... | collective-permute-start | bytes 4718600 | tf_op jit(solution)/shard_map/ppermute | solution.py:36
  109.6 46.0 %collective-permute-start.4 = (bf16[2,256,1536]{2,1,0:T(8,128)(2,1)}, bf16[2,256,1536]{2,1,0:T(8,128)(2,1)}, u32[]{:S(2)}, u32[]{:S(2)}) collective-permute-start(bf16[2,256,1536]{2,1,0:T(8,128)(2,1)} %collective-permute-done.3.refs_3_), channel_id=1, source_target_pairs={{0,7},{1,2},{2,1},{3,4},{4,3},{5,6},{6,5},{7,0},{8,15},{9,10},{10,... | collective-permute-start | bytes 4718600 | tf_op jit(solution)/shard_map/ppermute | solution.py:36
  110.5 45.1 %copy-start.2 = (bf16[1,256,1536]{2,1,0:T(8,128)(2,1)S(1)}, bf16[1,256,1536]{2,1,0:T(8,128)(2,1)}, u32[]{:S(2)}) copy-start(bf16[1,256,1536]{2,1,0:T(8,128)(2,1)} %copy-done.1) | copy-start | bytes 2359300
  110.5 45.1 %copy-start.5 = (bf16[1,256,1536]{2,1,0:T(8,128)(2,1)S(1)}, bf16[1,256,1536]{2,1,0:T(8,128)(2,1)}, u32[]{:S(2)}) copy-start(bf16[1,256,1536]{2,1,0:T(8,128)(2,1)} %copy-done.4) | copy-start | bytes 2359300
  110.5 45.1 %copy-start.8 = (bf16[2,256,1536]{2,1,0:T(8,128)(2,1)S(1)}, bf16[2,256,1536]{2,1,0:T(8,128)(2,1)}, u32[]{:S(2)}) copy-start(bf16[2,256,1536]{2,1,0:T(8,128)(2,1)} %copy-done.7) | copy-start | bytes 4718596
  114.4 41.1 %copy-start.12 = (f32[512,512]{1,0:T(8,128)}, f32[512,512]{1,0:T(8,128)S(1)}, u32[]{:S(2)}) copy-start(f32[512,512]{1,0:T(8,128)S(1)} %fusion) | copy-start | bytes 3145732
  121.5 73.7 %collective-permute-start.19 = (f32[256,512]{1,0:T(8,128)}, f32[256,512]{1,0:T(8,128)}, u32[]{:S(2)}, u32[]{:S(2)}) collective-permute-start(f32[256,512]{1,0:T(8,128)} %dynamic-slice_bitcast_fusion), channel_id=1, source_target_pairs={{0,64},{1,65},{64,0},{65,1},{128,192},{129,193},{192,128},{193,129}} | collective-permute-start | bytes 1572872 | tf_op jit(solution)/shard_map/ppermute | solution.py:36
  167.5 140.8 %collective-permute-start.17 = (f32[8,512,256]{2,1,0:T(8,128)}, f32[8,512,256]{2,1,0:T(8,128)}, u32[]{:S(2)}, u32[]{:S(2)}) collective-permute-start(f32[8,512,256]{2,1,0:T(8,128)} %shard_map.51), channel_id=1, source_target_pairs={{0,64},{1,65},{2,66},{3,67},{4,68},{5,69},{6,70},{7,71},{8,72},{9,... | collective-permute-start | bytes 12582920 | tf_op jit(solution)/shard_map/ppermute | solution.py:36
  197.3 15.7 %collective-permute-start.20 = (f32[256,512]{1,0:T(8,128)}, f32[256,512]{1,0:T(8,128)}, u32[]{:S(2)}, u32[]{:S(2)}) collective-permute-start(f32[256,512]{1,0:T(8,128)} %bitcast_add_fusion), channel_id=1, source_target_pairs={{0,128},{1,129},{64,192},{65,193},{128,0},{129,1},{192,64},{193,65}} | collective-permute-start | bytes 1572872 | tf_op jit(solution)/shard_map/ppermute | solution.py:36
  214.3 12.0 %collective-permute-start.21 = (f32[256,512]{1,0:T(8,128)S(1)}, f32[256,512]{1,0:T(8,128)S(1)}, u32[]{:S(2)}, u32[]{:S(2)}) collective-permute-start(f32[256,512]{1,0:T(8,128)S(1)} %add_select_fusion), channel_id=1, source_target_pairs={{0,32},{1,33},{64,96},{65,97},{128,160},{129,161},{192,224},{193,2... | collective-permute-start | bytes 1572872 | tf_op jit(solution)/shard_map/ppermute | solution.py:36
  226.4 11.4 %collective-permute-start.24 = (f32[256,512]{1,0:T(8,128)S(1)}, f32[256,512]{1,0:T(8,128)S(1)}, u32[]{:S(2)}, u32[]{:S(2)}) collective-permute-start(f32[256,512]{1,0:T(8,128)S(1)} %add.99), channel_id=1, source_target_pairs={{0,16},{1,17},{32,48},{33,49},{64,80},{65,81},{96,112},{97,113},{1... | collective-permute-start | bytes 1572872 | tf_op jit(solution)/shard_map/ppermute | solution.py:36
  227.8 21.3 %collective-permute-start.22 = (f32[256,512]{1,0:T(8,128)S(1)}, f32[256,512]{1,0:T(8,128)S(1)}, u32[]{:S(2)}, u32[]{:S(2)}) collective-permute-start(f32[256,512]{1,0:T(8,128)S(1)} %add.99), channel_id=1, source_target_pairs={{0,8},{1,9},{32,40},{33,41},{64,72},{65,73},{96,104},{97,105},{128... | collective-permute-start | bytes 1572872 | tf_op jit(solution)/shard_map/ppermute | solution.py:36
  229.1 20.0 %collective-permute-start.23 = (f32[256,512]{1,0:T(8,128)S(1)}, f32[256,512]{1,0:T(8,128)S(1)}, u32[]{:S(2)}, u32[]{:S(2)}) collective-permute-start(f32[256,512]{1,0:T(8,128)S(1)} %add.99), channel_id=1, source_target_pairs={{0,24},{1,25},{32,56},{33,57},{64,88},{65,89},{96,120},{97,121},{1... | collective-permute-start | bytes 1572872 | tf_op jit(solution)/shard_map/ppermute | solution.py:36
  250.1 5.8 %collective-permute-start.25 = (f32[256,512]{1,0:T(8,128)}, f32[256,512]{1,0:T(8,128)}, u32[]{:S(2)}, u32[]{:S(2)}) collective-permute-start(f32[256,512]{1,0:T(8,128)} %add_add_fusion), channel_id=1, source_target_pairs={{0,64},{1,65},{8,72},{9,73},{16,80},{17,81},{24,88},{25,89},{32,96... | collective-permute-start | bytes 1572872 | tf_op jit(solution)/shard_map/ppermute | solution.py:36
  257.6 38.8 %copy-start.3 = (bf16[1,256,1536]{2,1,0:T(8,128)(2,1)S(1)}, bf16[1,256,1536]{2,1,0:T(8,128)(2,1)}, u32[]{:S(2)}) copy-start(bf16[1,256,1536]{2,1,0:T(8,128)(2,1)} %copy-done.1) | copy-start | bytes 2359300
  257.6 38.8 %copy-start.6 = (bf16[1,256,1536]{2,1,0:T(8,128)(2,1)S(1)}, bf16[1,256,1536]{2,1,0:T(8,128)(2,1)}, u32[]{:S(2)}) copy-start(bf16[1,256,1536]{2,1,0:T(8,128)(2,1)} %copy-done.4) | copy-start | bytes 2359300
  257.7 38.8 %copy-start.9 = (bf16[2,256,1536]{2,1,0:T(8,128)(2,1)S(1)}, bf16[2,256,1536]{2,1,0:T(8,128)(2,1)}, u32[]{:S(2)}) copy-start(bf16[2,256,1536]{2,1,0:T(8,128)(2,1)} %copy-done.7) | copy-start | bytes 4718596
  308.4 19.4 %copy-start = (f32[8,512,256]{2,1,0:T(8,128)S(1)}, f32[8,512,256]{2,1,0:T(8,128)}, u32[]{:S(2)}) copy-start(f32[8,512,256]{2,1,0:T(8,128)} %shard_map.50.a_ref) | copy-start | bytes 12582916
  311.1 6.5 %collective-permute-start.32 = (f32[64,512]{1,0:T(8,128)S(1)}, f32[64,512]{1,0:T(8,128)S(1)}, u32[]{:S(2)}, u32[]{:S(2)}) collective-permute-start(f32[64,512]{1,0:T(8,128)S(1)} %get-tuple-element.9), channel_id=1, source_target_pairs={{0,7},{8,15},{16,23},{24,31},{32,39},{40,47},{48,55},{56,63},{64,7... | collective-permute-start | bytes 393224 | tf_op jit(solution)/shard_map/ppermute | solution.py:36
  312.4 14.0 %collective-permute-start.31 = (f32[64,512]{1,0:T(8,128)S(1)}, f32[64,512]{1,0:T(8,128)S(1)}, u32[]{:S(2)}, u32[]{:S(2)}) collective-permute-start(f32[64,512]{1,0:T(8,128)S(1)} %get-tuple-element.10), channel_id=1, source_target_pairs={{0,6},{8,14},{16,22},{24,30},{32,38},{40,46},{48,54},{56,62},{64,7... | collective-permute-start | bytes 393224 | tf_op jit(solution)/shard_map/ppermute | solution.py:36
  313.7 19.9 %collective-permute-start.30 = (f32[64,512]{1,0:T(8,128)S(1)}, f32[64,512]{1,0:T(8,128)S(1)}, u32[]{:S(2)}, u32[]{:S(2)}) collective-permute-start(f32[64,512]{1,0:T(8,128)S(1)} %get-tuple-element.12), channel_id=1, source_target_pairs={{0,5},{8,13},{16,21},{24,29},{32,37},{40,45},{48,53},{56,61},{64,6... | collective-permute-start | bytes 393224 | tf_op jit(solution)/shard_map/ppermute | solution.py:36
  315.0 18.6 %collective-permute-start.29 = (f32[64,512]{1,0:T(8,128)S(1)}, f32[64,512]{1,0:T(8,128)S(1)}, u32[]{:S(2)}, u32[]{:S(2)}) collective-permute-start(f32[64,512]{1,0:T(8,128)S(1)} %get-tuple-element.14), channel_id=1, source_target_pairs={{0,4},{1,7},{8,12},{9,15},{16,20},{17,23},{24,28},{25,31},{32,36},... | collective-permute-start | bytes 393224 | tf_op jit(solution)/shard_map/ppermute | solution.py:36
  316.3 17.3 %collective-permute-start.28 = (f32[64,512]{1,0:T(8,128)S(1)}, f32[64,512]{1,0:T(8,128)S(1)}, u32[]{:S(2)}, u32[]{:S(2)}) collective-permute-start(f32[64,512]{1,0:T(8,128)S(1)} %get-tuple-element.11), channel_id=1, source_target_pairs={{0,3},{1,6},{8,11},{9,14},{16,19},{17,22},{24,27},{25,30},{32,35},... | collective-permute-start | bytes 393224 | tf_op jit(solution)/shard_map/ppermute | solution.py:36
  317.6 16.0 %collective-permute-start.27 = (f32[64,512]{1,0:T(8,128)S(1)}, f32[64,512]{1,0:T(8,128)S(1)}, u32[]{:S(2)}, u32[]{:S(2)}) collective-permute-start(f32[64,512]{1,0:T(8,128)S(1)} %get-tuple-element.13), channel_id=1, source_target_pairs={{0,2},{1,5},{8,10},{9,13},{16,18},{17,21},{24,26},{25,29},{32,34},... | collective-permute-start | bytes 393224 | tf_op jit(solution)/shard_map/ppermute | solution.py:36
  326.4 7.3 %collective-permute-start.26 = (f32[64,512]{1,0:T(8,128)S(1)}, f32[64,512]{1,0:T(8,128)S(1)}, u32[]{:S(2)}, u32[]{:S(2)}) collective-permute-start(f32[64,512]{1,0:T(8,128)S(1)} %get-tuple-element.8), channel_id=1, source_target_pairs={{0,1},{1,4},{8,9},{9,12},{16,17},{17,20},{24,25},{25,28},{32,33},{... | collective-permute-start | bytes 393224 | tf_op jit(solution)/shard_map/ppermute | solution.py:36

commit v2 on v1

v2 whole, which is shorter than its diff:
```python
import functools

import jax
import jax.numpy as jnp
import numpy as np
from jax import lax
from jax.experimental import pallas as pl
from jax.experimental.pallas import tpu as pltpu
from jax.sharding import PartitionSpec as P

PANEL = 512
reg_alpha = 0.9
AXES = ("cal", "row", "col")
NX, NY, NZ = 4, 4, 8
HIGHEST = lax.Precision.HIGHEST


def flat(x, y, z, core):
    return (((x % 2) * 2 + core) * 8 + (x // 2) * 4 + y) * 8 + z


def devices():
    for x in range(NX):
        for y in range(NY):
            for z in range(NZ):
                for core in range(2):
                    yield x, y, z, core


def move(value, target):
    pairs = []
    for device in devices():
        to = target(*device)
        if to is not None:
            pairs.append((flat(*device), flat(*to)))
    return lax.ppermute(value, AXES, sorted(pairs))


def near(i, size, phase):
    return i ^ 1 if phase == 0 else (i + 1 if i % 2 else i - 1) % size


def x_step(s):
    return lambda x, y, z, c: (near(x, NX, (s + c) % 2), y, z, c)


def y_step(s):
    return lambda x, y, z, c: (x, near(y, NY, (s + c) % 2), z, c)


def z_step(s):
    return lambda x, y, z, c: (x, y, near(z, NZ, (s + c) % 2), c)


def core_swap(x, y, z, c):
    return x, y, z, 1 - c


def row_home(x, y, z, c):
    return (x, y, z, c) if z // 4 == x % 2 else (x ^ 1, y, 7 - z, c)


def tables():
    table = np.zeros((256, 32), np.int32)
    for x, y, z, c in devices():
        def ring4(i):
            p1 = lambda v: near(v, 4, c % 2)
            p2 = lambda v: near(v, 4, (1 + c) % 2)
            return [i, p1(i), p2(i), p1(p2(i))]

        step = lambda v, s: near(v, NZ, (s + c) % 2)
        first = lambda v: [v, step(v, 0)]
        third = lambda v: first(step(step(v, 2), 1))
        slots = first(z) + first(step(z, 1)) + third(z) + third(step(z, 3))
        assert sorted(slots) == list(range(8))
        low = x % 2
        blocks = [(p if p // 4 == low else 7 - p) - 4 * low for p in slots]
        halves = [low if p // 4 == low else 1 - low for p in slots]
        table[flat(x, y, z, c)] = ring4(x) + ring4(y) + blocks + halves + [c, low] + [0] * 6
    return table


TABLE = tables()


def start_rows(meta, wanted, row_refs, rows, sem):
    tokens = row_refs[0].shape[2]
    copies = []
    for ref in row_refs:
        for i in range(ref.shape[0]):
            slot = len(copies)
            block, side = meta[8 + slot], meta[16 + slot]
            dst = rows.at[
                pl.ds(pl.multiple_of((block % 2) * 256, 256), 256),
                pl.ds(pl.multiple_of(side * tokens, tokens), tokens),
            ]
            copy = pltpu.make_async_copy(ref.at[i], dst, sem.at[slot])
            copies.append((block // 2 == wanted, copy))
    for want, copy in copies:
        pl.when(want)(copy.start)

    def wait():
        for want, copy in copies:
            pl.when(want)(copy.wait)

    return wait


def gram_kernel(own, scale, *refs):
    meta, refs = refs[0], refs[1:]
    row_refs, first_refs, second_refs, refs = refs[:5], refs[5:9], refs[9:13], refs[13:]
    if own:
        other_ref, out_ref, rows, cols, other, row_sem, col_sem, sem = refs
    else:
        out_ref, rows, cols, other, row_sem, col_sem, sem = refs
    tokens = row_refs[0].shape[2]
    half = tokens // 2
    core = meta[24]
    wait_rows = start_rows(meta, core if own else 1 - core, row_refs, rows, row_sem)

    def column(j, pair):
        x = jnp.where(core == 0, meta[2 * pair], meta[pair])
        return (x // 2) * 4 + meta[4 + j]

    col_copies = []
    for j in range(4):
        group = []
        for i in range(4):
            pair = jnp.where(core == 0, i // 2, i % 2)
            side = meta[i] % 2
            for which, ref in ((0, first_refs[j].at[i]), (1, second_refs[i].at[j])):
                dst = cols.at[
                    2 * j + pair,
                    pl.ds(pl.multiple_of(side * tokens + which * half, half), half),
                ]
                copy = pltpu.make_async_copy(ref, dst, col_sem.at[j, i, which])
                copy.start()
                group.append(copy)
        if own:
            for pair in range(2):
                k = 2 * j + pair
                copy = pltpu.make_async_copy(other_ref.at[column(j, pair)], other.at[k], sem.at[k])
                copy.start()
                group.append(copy)
        col_copies.append(group)
    wait_rows()
    out_copies = []
    row_ids = meta[25] + lax.broadcasted_iota(jnp.int32, (512, 128), 0)
    lane = meta[26] + lax.broadcasted_iota(jnp.int32, (512, 128), 1)
    for j in range(4):
        for copy in col_copies[j]:
            copy.wait()
        for pair in range(2):
            a = column(j, pair)
            k = 2 * j + pair
            total = jnp.dot(rows[...], cols[k], preferred_element_type=jnp.float32)
            if own:
                for h in range(2):
                    part = total[:, h * 128:(h + 1) * 128] + other[k, :, h * 128:(h + 1) * 128]
                    part = part * scale
                    same = row_ids == lane + (a * 2048 + h * 128)
                    out_ref[pl.ds(2 * a + h, 512, stride=16), :] = jnp.where(
                        same, part, reg_alpha * part
                    )
            else:
                other[k] = total
                copy = pltpu.make_async_copy(other.at[k], out_ref.at[a], sem.at[k])
                copy.start()
                out_copies.append(copy)
    for copy in out_copies:
        copy.wait()


def gram_part(scale, meta, row_bufs, first_bufs, second_bufs, other=None):
    own = other is not None
    tokens = row_bufs[0].shape[2]
    any_spec = pl.BlockSpec(memory_space=pl.ANY)
    shape = (512 * 16, 128) if own else (8, 512, 256)
    return pl.pallas_call(
        functools.partial(gram_kernel, own, scale),
        out_shape=jax.ShapeDtypeStruct(shape, jnp.float32),
        in_specs=[pl.BlockSpec(memory_space=pltpu.SMEM)] + [any_spec] * (13 + own),
        out_specs=pl.BlockSpec(memory_space=pltpu.VMEM) if own else any_spec,
        scratch_shapes=[
            pltpu.VMEM((512, 2 * tokens), jnp.bfloat16),
            pltpu.VMEM((8, 2 * tokens, 256), jnp.bfloat16),
            pltpu.VMEM((8, 512, 256), jnp.float32),
            pltpu.SemaphoreType.DMA((8,)),
            pltpu.SemaphoreType.DMA((4, 4, 2)),
            pltpu.SemaphoreType.DMA((8,)),
        ],
        compiler_params=pltpu.CompilerParams(vmem_limit_bytes=40 * 2**20),
        cost_estimate=pl.CostEstimate(
            flops=2 * 512 * 2048 * 2 * tokens, bytes_accessed=24 * 2**20, transcendentals=0
        ),
    )(meta, *row_bufs, *first_bufs, *second_bufs, *([other] if own else []))


def lead_kernel(*refs):
    meta, refs = refs[0], refs[1:]
    row_refs, first_refs, second_refs = refs[:5], refs[5:9], refs[9:13]
    out_ref, rows, cols, row_sem, col_sem = refs[13:]
    tokens = row_refs[0].shape[2]
    half = tokens // 2
    wait_rows = start_rows(meta, meta[24], row_refs, rows, row_sem)
    copies = []
    for j in range(4):
        for i in range(4):
            want = (meta[i] // 2 == 0) & (meta[4 + j] == 0)
            side = meta[i] % 2
            for which, ref in ((0, first_refs[j].at[i]), (1, second_refs[i].at[j])):
                dst = cols.at[pl.ds(pl.multiple_of(side * tokens + which * half, half), half)]
                copies.append((want, pltpu.make_async_copy(ref, dst, col_sem.at[j, i, which])))
    for want, copy in copies:
        pl.when(want)(copy.start)
    wait_rows()
    for want, copy in copies:
        pl.when(want)(copy.wait)
    out_ref[...] = jnp.dot(rows[...], cols[...], preferred_element_type=jnp.float32)


def lead_part(meta, row_bufs, first_bufs, second_bufs):
    tokens = row_bufs[0].shape[2]
    any_spec = pl.BlockSpec(memory_space=pl.ANY)
    return pl.pallas_call(
        lead_kernel,
        out_shape=jax.ShapeDtypeStruct((512, 256), jnp.float32),
        in_specs=[pl.BlockSpec(memory_space=pltpu.SMEM)] + [any_spec] * 13,
        out_specs=pl.BlockSpec(memory_space=pltpu.VMEM),
        scratch_shapes=[
            pltpu.VMEM((512, 2 * tokens), jnp.bfloat16),
            pltpu.VMEM((2 * tokens, 256), jnp.bfloat16),
            pltpu.SemaphoreType.DMA((8,)),
            pltpu.SemaphoreType.DMA((4, 4, 2)),
        ],
        compiler_params=pltpu.CompilerParams(vmem_limit_bytes=40 * 2**20),
        cost_estimate=pl.CostEstimate(
            flops=2 * 512 * 256 * 2 * tokens, bytes_accessed=5 * 2**20, transcendentals=0
        ),
    )(meta, *row_bufs, *first_bufs, *second_bufs)


def dot_t(a, b):
    return lax.dot_general(
        a, b, (((0,), (0,)), ((), ())), precision=HIGHEST, preferred_element_type=jnp.float32
    )


def dot_n(a, b):
    return lax.dot_general(
        a, b, (((1,), (0,)), ((), ())), precision=HIGHEST, preferred_element_type=jnp.float32
    )


def factor_kernel(k, work_ref, u_in, inv_in, work, u_ref, inv_ref, block, inv):
    n, nb, np_ = 512, 128, 8
    sub = lax.broadcasted_iota(jnp.int32, (np_, nb), 0)
    lane = lax.broadcasted_iota(jnp.int32, (np_, nb), 1)
    eye = (
        lax.broadcasted_iota(jnp.int32, (nb, nb), 0) == lax.broadcasted_iota(jnp.int32, (nb, nb), 1)
    ).astype(jnp.float32)
    lo, hi = k * nb, (k + 1) * nb
    work[...] = work_ref[...]
    u_ref[...] = u_in[...]
    inv_ref[...] = inv_in[...]
    block[...] = work[lo:hi, lo:hi]
    inv[...] = eye

    def panel(p, _):
        base = pl.multiple_of(p * np_, np_)
        v = block[pl.ds(base, np_), :]
        xv = inv[pl.ds(base, np_), :]
        rolled = pltpu.roll(v, lax.rem(nb - base, nb), 1)
        pc = [jnp.broadcast_to(rolled[:, i:i + 1], (np_, nb)) for i in range(np_)]
        for i in range(np_):
            s = lax.rsqrt(pc[i][i:i + 1, :])
            u = v[i:i + 1, :] * s
            xu = xv[i:i + 1, :] * s
            below = jnp.where(sub > i, pc[i] * s, 0.0)
            here = sub == i
            for j in range(i + 1, np_):
                pc[j] = pc[j] - below * (pc[j][i:i + 1, :] * s)
            v = jnp.where(here, u, v - below * u)
            xv = jnp.where(here, xu, xv - below * xu)
        v = jnp.where(lane >= base + sub, v, 0.0)
        block[pl.ds(base, np_), :] = v
        inv[pl.ds(base, np_), :] = xv
        later = jnp.where(lane >= base + np_, v, 0.0)
        block[...] -= dot_t(later, v)
        inv[...] -= dot_t(later, xv)
        return 0

    lax.fori_loop(0, nb // np_, panel, 0)
    x = inv[...]
    u_ref[lo:hi, lo:hi] = block[...]
    inv_ref[lo:hi, lo:hi] = x
    if k:
        inner = dot_t(u_ref[0:lo, lo:hi], inv_ref[0:lo, 0:lo])
        inv_ref[lo:hi, 0:lo] = -dot_n(x, inner)
    if hi < n:
        right = dot_n(x, work[lo:hi, hi:n])
        u_ref[lo:hi, hi:n] = right
        work[hi:n, hi:n] -= dot_t(right, right)


def factor_part(k, work, upper, inverse):
    full = pl.BlockSpec(memory_space=pltpu.VMEM)
    shape = jax.ShapeDtypeStruct((512, 512), jnp.float32)
    return pl.pallas_call(
        functools.partial(factor_kernel, k),
        out_shape=(shape,) * 3,
        in_specs=[full] * 3,
        out_specs=(full,) * 3,
        scratch_shapes=[
            pltpu.VMEM((128, 128), jnp.float32),
            pltpu.VMEM((128, 128), jnp.float32),
        ],
        compiler_params=pltpu.CompilerParams(vmem_limit_bytes=32 * 2**20),
        cost_estimate=pl.CostEstimate(flops=2**33, bytes_accessed=6 * 2**20, transcendentals=512),
    )(work, upper, inverse)


def per_device(acts_one, acts_two):
    cal, row, z = (lax.axis_index(a) for a in AXES)
    core = cal % 2
    total_tokens = 8 * acts_one.shape[0]
    scale = 1.0 / total_tokens
    device = (cal * 8 + row) * 8 + z
    meta = lax.dynamic_index_in_dim(jnp.asarray(TABLE), device, 0, keepdims=False)
    after = lax.optimization_barrier
    root = lambda x, y, z: (x // 2, y) == (0, 0) and z < 2

    cols = jnp.concatenate([acts_one, acts_two], 0)
    one_t, two_t = acts_one.T, acts_two.T
    a0, b0 = acts_one[None], acts_two[None]
    one_t = move(one_t, row_home)
    a1 = move(a0, x_step(0))
    b1 = move(b0, y_step(0))
    other = move(cols, lambda x, y, z, c: (x, y, 1 - z, c) if root(x, y, z) else None)
    one_t, a1, b1, other, two_t = after((one_t, a1, b1, other, two_t))

    middle = two_t.shape[1] // 2
    q3 = move(two_t[:, :middle], row_home)
    left, right = jnp.where(z == 0, cols, other), jnp.where(z == 0, other, cols)
    part = [
        lax.dot_general(p, q, (((0,), (0,)), ((), ())), preferred_element_type=jnp.float32)
        for p, q in ((left, left), (left, right), (right, right))
    ]
    part = jnp.concatenate(part, 0).reshape(2, 384, 256)
    lead = lax.dynamic_index_in_dim(part, core, 0, keepdims=False)
    away = lax.dynamic_index_in_dim(part, 1 - core, 0, keepdims=False)
    lead = lead + move(away, lambda x, y, z, c: (x, y, z, 1 - c) if root(x, y, z) else None)
    q3, lead, one_t, two_t, a1, b1 = after((q3, lead, one_t, two_t, a1, b1))

    q4 = move(two_t[:, middle:], row_home)
    a01 = jnp.concatenate([a0, a1], 0)
    b01 = jnp.concatenate([b0, b1], 0)
    a23 = move(a01, x_step(1))
    b23 = move(b01, y_step(1))
    lead = lead + move(lead, lambda x, y, z, c: (x ^ 1, y, z, c) if root(x, y, z) else None)
    lead = jnp.where(row == 0, lead, 0.0)
    q3, q4, lead, one_t, a01, a23, b01, b23 = after((q3, q4, lead, one_t, a01, a23, b01, b23))

    r0 = jnp.concatenate([one_t, q3, q4], 1)[None]
    r1 = move(r0, z_step(0))
    first = jnp.concatenate([a01, a23], 0)
    second = jnp.concatenate([b01, b23], 0)
    lead = lead + move(lead, lambda x, y, z, c: (x + 2, y, z, c) if root(x, y, z) else None)
    lead = lead + move(lead, lambda x, y, z, c: (x, 1, z, c) if y == 0 and z < 2 else None)
    r0, r1, first, second, lead = after((r0, r1, first, second, lead))

    r2 = move(jnp.concatenate([r0, r1], 0), z_step(1))
    first1 = move(first, y_step(0))
    second1 = move(second, x_step(0))
    lead = lead + move(lead, lambda x, y, z, c: (x, 3 - y, z, c) if y < 2 and z < 2 else None)
    theirs = move(lead, lambda x, y, z, c: (x, y, z, 1 - c) if z < 2 else None)
    r0, r1, r2, first, first1, second, second1, lead, theirs = after(
        (r0, r1, r2, first, first1, second, second1, lead, theirs)
    )

    r3 = move(r2, z_step(2))
    first2 = move(first, y_step(1))
    second2 = move(second, x_step(1))
    low = jnp.where(core == 0, lead, theirs)
    high = jnp.where(core == 0, theirs, lead)
    corner = jnp.concatenate([low[256:], high[:128]], 0)
    gram = jnp.concatenate(
        [
            jnp.concatenate([low[:256], corner], 1),
            jnp.concatenate([corner.T, high[128:]], 1),
        ],
        0,
    ) * scale
    ids = jnp.arange(512, dtype=jnp.int32)
    work = jnp.where(ids[:, None] == ids[None, :], gram, reg_alpha * gram)
    zeros = jnp.zeros((512, 512), jnp.float32)
    state = factor_part(0, work, zeros, zeros)
    state = factor_part(1, *state)
    r0, r1, r2, r3, first, first1, first2, second, second1, second2, state = after(
        (r0, r1, r2, r3, first, first1, first2, second, second1, second2, state)
    )

    r4 = move(r3, z_step(3))
    first3 = move(first1, y_step(1))
    second3 = move(second1, x_step(1))
    state = factor_part(2, *state)
    _, upper, inverse = factor_part(3, *state)
    r0, r1, r2, r3, r4, first, first1, first2, first3, second, second1, second2, second3, upper, inverse = after(
        (r0, r1, r2, r3, r4, first, first1, first2, first3, second, second1, second2, second3, upper, inverse)
    )

    pieces = (
        (r0, r1, r2, r3, r4),
        (first, first1, first2, first3),
        (second, second1, second2, second3),
    )
    row_start = row * 2048 + cal * 512
    meta = meta.at[25].set(row_start).at[26].set(z * 256)
    theirs = gram_part(scale, meta, *pieces)
    theirs_lead = move(theirs[0], core_swap)
    theirs = move(theirs, core_swap)

    block = (lead_part(meta, *pieces) + theirs_lead) * scale
    row_ids = row_start + jnp.arange(512, dtype=jnp.int32)[:, None]
    col_ids = z * 256 + jnp.arange(256, dtype=jnp.int32)[None, :]
    block = jnp.where(row_ids == col_ids, block, reg_alpha * block)
    weights = jnp.where(z == 0, inverse[:, :256], inverse[:, 256:])
    solved = lax.dot_general(
        weights, block, (((1,), (1,)), ((), ())), precision=HIGHEST,
        preferred_element_type=jnp.float32,
    )
    head = jnp.where(z == 0, upper, 0.0)
    solved = jnp.where((row == 0) & (cal == 0), head, solved).reshape(8, 64, 512)
    share = jnp.where(z == 0, solved[0], 0.0)
    for to in range(1, 8):
        extra = to + 3 if to < 5 else None

        def target(x, y, z, c, to=to, extra=extra):
            if z == 0:
                return x, y, to, c
            return (x, y, extra, c) if z == 1 and extra is not None else None

        value = solved[to] if extra is None else jnp.where(z == 0, solved[to], solved[extra])
        share = share + move(value, target)

    gram_reg = gram_part(scale, meta, *pieces, other=theirs)
    return gram_reg.reshape(1, 512, 8, 1, 256), share.T.reshape(1, 512, 64)


def solution(mesh):
    return jax.shard_map(
        per_device,
        mesh=mesh,
        in_specs=(P("cal", ("row", "col")), P("cal", ("row", "col"))),
        out_specs=(P("row", "cal", None, "col", None), P("row", "cal", "col")),
        check_vma=False,
    )
```

time: 337 us -> 252 us (0.75)
  starting transfers between devices: 154 us -> 71.6 us
  waiting for transfers between devices: 90.8 us -> 69.6 us
  local copies, waits for them, and re-layouts: 5.97 us -> 17.7 us
  Pallas kernels: 68.5 us -> 72.5 us
    ppermute x33, starting transfers between devices: 154 us -> 71.6 us  [move(): return lax.ppermute(value, AXES, sorted(pairs))]
    ppermute x33, waiting for transfers between devices: 90.8 us -> 69.6 us  [move(): return lax.ppermute(value, AXES, sorted(pairs))]
    unnamed x33 -> x73, local copies, waits for them, and re-layouts: 4.29 us -> 11.4 us
    pallas_call x4 -> x7, Pallas kernels: 68.5 us -> 72.5 us  [the longest x4 39.6 us: factor_part(): pl.pallas_call(functools.partial(factor_kernel, k), out_shape=(shape,) *...]
  transfers between devices with their start and end apart: 33 -> 33, of which waited for: 13 -> 11; matrix products, arithmetic and copies ran while one was open for 4% -> 3% of each run, Pallas kernels for 20% -> 17%
where the time goes in v2:
time: 252 us; the launch traced here: 248 us
  Pallas kernels  72.5 us (29%)
  starting transfers between devices  71.6 us (28%)
  waiting for transfers between devices  69.6 us (28%)
  local copies, waits for them, and re-layouts  17.7 us (7%)
  other arithmetic  9.35 us (4%)
  matrix products  5.42 us (2%)
    ppermute x33, starting transfers between devices, move(): return lax.ppermute(value, AXES, sorted(pairs))  71.6 us
    ppermute x33, waiting for transfers between devices, move(): return lax.ppermute(value, AXES, sorted(pairs))  69.6 us
    pallas_call x4, Pallas kernels, factor_part(): pl.pallas_call(functools.partial(factor_kernel, k), out_shape=(shape,) *...  39.6 us
    pallas_call x2, Pallas kernels, gram_part(): pl.pallas_call(functools.partial(gram_kernel, own, scale), out_shape=jax....  29.2 us
    unnamed x73, local copies, waits for them, and re-layouts  11.4 us
  transfers between devices with their start and end apart: 33, of which 11 were waited for; matrix products, arithmetic and copies ran while one was open for 3% of the time, Pallas kernels for 17%

profile of v2, /device:TPU:1, one launch (start us, length us, event | category | flops | bytes accessed | tf_op | source)
XLA Modules:
  0.0 248.0 jit_solution(1623937771249156035)
XLA Ops:
  2.8 4.4 %collective-permute-start.3 = (bf16[1536,256]{1,0:T(8,128)(2,1)S(1)}, bf16[1536,256]{1,0:T(8,128)(2,1)}, u32[]{:S(2)}, u32[]{:S(2)}) collective-permute-start(bf16[1536,256]{1,0:T(8,128)(2,1)S(1)} %constant_dynamic-update-slice_fusion), channel_id=1, source_target_pairs={{0,1},{1,0},{64,65},{65,64},{128,129},{129,128},{192,193},{193,192}} | collective-permute-start | bytes 2359304 | tf_op jit(solution)/shard_map/ppermute | solution.py:36
  8.9 9.5 %collective-permute-start.1 = (bf16[1,768,256]{2,1,0:T(8,128)(2,1)S(1)}, bf16[1,768,256]{2,1,0:T(8,128)(2,1)S(1)}, u32[]{:S(2)}, u32[]{:S(2)}) collective-permute-start(bf16[1,768,256]{2,1,0:T(8,128)(2,1)S(1)} %bitcast.25), channel_id=1, source_target_pairs={{0,128},{1,129},{2,130},{3,131},{4,132},{5,133},{6,134},{7,135},{8... | collective-permute-start | bytes 1179656 | tf_op jit(solution)/shard_map/ppermute | solution.py:36
  18.7 4.9 %collective-permute-done.1 = bf16[1,768,256]{2,1,0:T(8,128)(2,1)S(1)} collective-permute-done((bf16[1,768,256]{2,1,0:T(8,128)(2,1)S(1)}, bf16[1,768,256]{2,1,0:T(8,128)(2,1)S(1)}, u32[]{:S(2)}, u32[]{:S(2)}) %collective-permute-start.1) | collective-permute-done | bytes 393248 | tf_op jit(solution)/shard_map/ppermute | solution.py:36
  23.6 8.1 %collective-permute-done.3 = bf16[1536,256]{1,0:T(8,128)(2,1)} collective-permute-done((bf16[1536,256]{1,0:T(8,128)(2,1)S(1)}, bf16[1536,256]{1,0:T(8,128)(2,1)}, u32[]{:S(2)}, u32[]{:S(2)}) %collective-permute-start.3) | collective-permute-done | bytes 786464 | tf_op jit(solution)/shard_map/ppermute | solution.py:36
  31.8 1.7 fusion.11
  33.5 2.0 fusion.13
  36.1 3.5 %collective-permute-start.5 = (f32[384,256]{1,0:T(8,128)S(1)}, f32[384,256]{1,0:T(8,128)S(1)}, u32[]{:S(2)}, u32[]{:S(2)}) collective-permute-start(f32[384,256]{1,0:T(8,128)S(1)} %dynamic-slice_bitcast_fusion), channel_id=1, source_target_pairs={{0,64},{1,65},{64,0},{65,1},{128,192},{129,193},{192,128},{193,129}} | collective-permute-start | bytes 1179656 | tf_op jit(solution)/shard_map/ppermute | solution.py:36
  39.7 1.5 collective-permute-start.4
  42.5 11.2 %collective-permute-start.8 = (bf16[2,768,256]{2,1,0:T(8,128)(2,1)S(1)}, bf16[2,768,256]{2,1,0:T(8,128)(2,1)}, u32[]{:S(2)}, u32[]{:S(2)}) collective-permute-start(bf16[2,768,256]{2,1,0:T(8,128)(2,1)S(1)} %pad_maximum_fusion.4), channel_id=1, source_target_pairs={{0,160},{1,161},{2,162},{3,163},{4,164},{5,165},{6,166},{7,167},{8... | collective-permute-start | bytes 2359304 | tf_op jit(solution)/shard_map/ppermute | solution.py:36
  53.7 1.9 collective-permute-start.7
  56.3 18.9 %collective-permute-done.7 = f32[384,256]{1,0:T(8,128)S(1)} collective-permute-done((f32[384,256]{1,0:T(8,128)S(1)}, f32[384,256]{1,0:T(8,128)S(1)}, u32[]{:S(2)}, u32[]{:S(2)}) %collective-permute-start.7) | collective-permute-done | bytes 393248 | tf_op jit(solution)/shard_map/ppermute | solution.py:36
  75.4 1.4 collective-permute-start.11
  77.9 6.1 %collective-permute-done.11 = f32[384,256]{1,0:T(8,128)S(1)} collective-permute-done((f32[384,256]{1,0:T(8,128)S(1)}, f32[384,256]{1,0:T(8,128)S(1)}, u32[]{:S(2)}, u32[]{:S(2)}) %collective-permute-start.11) | collective-permute-done | bytes 393248 | tf_op jit(solution)/shard_map/ppermute | solution.py:36
  84.1 1.3 collective-permute-start.12
  85.4 1.6 pad_maximum_fusion
  87.1 6.1 %collective-permute-done.12 = f32[384,256]{1,0:T(8,128)S(1)} collective-permute-done((f32[384,256]{1,0:T(8,128)S(1)}, f32[384,256]{1,0:T(8,128)S(1)}, u32[]{:S(2)}, u32[]{:S(2)}) %collective-permute-start.12) | collective-permute-done | bytes 393248 | tf_op jit(solution)/shard_map/ppermute | solution.py:36
  93.2 1.4 pad_maximum_fusion.2
  95.6 5.0 %collective-permute-start.15 = (bf16[4,768,256]{2,1,0:T(8,128)(2,1)S(1)}, bf16[4,768,256]{2,1,0:T(8,128)(2,1)}, u32[]{:S(2)}, u32[]{:S(2)}) collective-permute-start(bf16[4,768,256]{2,1,0:T(8,128)(2,1)S(1)} %get-tuple-element.164.refs_10_), channel_id=1, source_target_pairs={{0,128},{1,129},{2,130},{3,131},{4,132},{5,133},{6,134},{7,135},{8... | collective-permute-start | bytes 4718600 | tf_op jit(solution)/shard_map/ppermute | solution.py:36
  100.6 4.6 %collective-permute-start.16 = (f32[384,256]{1,0:T(8,128)S(1)}, f32[384,256]{1,0:T(8,128)S(1)}, u32[]{:S(2)}, u32[]{:S(2)}) collective-permute-start(f32[384,256]{1,0:T(8,128)S(1)} %add.102), channel_id=1, source_target_pairs={{0,24},{1,25},{8,16},{9,17},{32,56},{33,57},{40,48},{41,49},{64,88... | collective-permute-start | bytes 1179656 | tf_op jit(solution)/shard_map/ppermute | solution.py:36
  105.2 16.2 %collective-permute-done.16 = f32[384,256]{1,0:T(8,128)S(1)} collective-permute-done((f32[384,256]{1,0:T(8,128)S(1)}, f32[384,256]{1,0:T(8,128)S(1)}, u32[]{:S(2)}, u32[]{:S(2)}) %collective-permute-start.16) | collective-permute-done | bytes 393248 | tf_op jit(solution)/shard_map/ppermute | solution.py:36
  121.5 1.9 collective-permute-start.17
  128.5 1.8 copy.7
  131.3 3.7 %collective-permute-start.20 = (bf16[4,768,256]{2,1,0:T(8,128)(2,1)S(1)}, bf16[4,768,256]{2,1,0:T(8,128)(2,1)S(1)}, u32[]{:S(2)}, u32[]{:S(2)}) collective-permute-start(bf16[4,768,256]{2,1,0:T(8,128)(2,1)S(1)} %get-tuple-element.164.refs_10_), channel_id=1, source_target_pairs={{0,160},{1,161},{2,162},{3,163},{4,164},{5,165},{6,166},{7,167},{8... | collective-permute-start | bytes 4718600 | tf_op jit(solution)/shard_map/ppermute | solution.py:36
  135.0 1.3 multiply_select_fusion.work_ref
  136.4 9.9 %shard_map.50 = (f32[512,512]{1,0:T(8,128)S(1)}, f32[512,512]{1,0:T(8,128)S(1)}, f32[512,512]{1,0:T(8,128)S(1)}) custom-call(f32[512,512]{1,0:T(8,128)S(1)} %multiply_select_fusion.work_ref, f32[512,512]{1,0:T(8,128)S(1)} %broadcast_in_dim.30.u_in.inv_in, f32[512,512]{1,0:T(8,128)S(1)} %broadcast_in_dim.30.u_in.inv_in), custom_call_target="tpu_custom_call" | custom-call | flops 8589934592 | bytes 6291456 | tf_op jit(solution)/shard_map/pallas_call | solution.py:309
  146.3 9.8 %shard_map.51 = (f32[512,512]{1,0:T(8,128)S(1)}, f32[512,512]{1,0:T(8,128)S(1)}, f32[512,512]{1,0:T(8,128)S(1)}) custom-call(f32[512,512]{1,0:T(8,128)S(1)} %get-tuple-element.131.work_ref, f32[512,512]{1,0:T(8,128)S(1)} %get-tuple-element.132.u_in, f32[512,512]{1,0:T(8,128)S(1)} %get-tuple-element.133.inv_in), custom_call_target="tpu_custom_call" | custom-call | flops 8589934592 | bytes 6291456 | tf_op jit(solution)/shard_map/pallas_call | solution.py:309
  157.2 9.9 %shard_map.52 = (f32[512,512]{1,0:T(8,128)S(1)}, f32[512,512]{1,0:T(8,128)S(1)}, f32[512,512]{1,0:T(8,128)S(1)}) custom-call(f32[512,512]{1,0:T(8,128)S(1)} %get-tuple-element.147.work_ref, f32[512,512]{1,0:T(8,128)S(1)} %get-tuple-element.148.u_in, f32[512,512]{1,0:T(8,128)S(1)} %get-tuple-element.149.inv_in), custom_call_target="tpu_custom_call" | custom-call | flops 8589934592 | bytes 6291456 | tf_op jit(solution)/shard_map/pallas_call | solution.py:309
  167.2 10.0 %shard_map.53 = (f32[512,512]{1,0:T(8,128)}, f32[512,512]{1,0:T(8,128)S(1)}, f32[512,512]{1,0:T(8,128)S(1)}) custom-call(f32[512,512]{1,0:T(8,128)S(1)} %get-tuple-element.150.work_ref, f32[512,512]{1,0:T(8,128)S(1)} %get-tuple-element.151.u_in, f32[512,512]{1,0:T(8,128)S(1)} %get-tuple-element.152.inv_in), custom_call_target="tpu_custom_call" | custom-call | flops 8589934592 | bytes 6291456 | tf_op jit(solution)/shard_map/pallas_call | solution.py:309
  179.2 1.2 copy-done.23
  180.3 13.2 %shard_map.54 = f32[8,512,256]{2,1,0:T(8,128)} custom-call(s32[32]{0:T(128)S(1)} %constant_dynamic-update-slice_fusion.2.refs_0_, bf16[1,256,1536]{2,1,0:T(8,128)(2,1)S(1)} %copy-done.3, bf16[1,256,1536]{2,1,0:T(8,128)(2,1)S(1)} %copy-done.6, bf16[2,256,1536]{2,1,0:T(8,128)(2,1)} %collective-permute-done.13.refs_3_, ...), custom_call_target="tpu_custom_call" | custom-call | flops 6442450944 | bytes 25165824 | tf_op jit(solution)/shard_map/pallas_call | solution.py:179
  193.6 4.0 %collective-permute-start.24 = (f32[8,512,256]{2,1,0:T(8,128)}, f32[8,512,256]{2,1,0:T(8,128)}, u32[]{:S(2)}, u32[]{:S(2)}) collective-permute-start(f32[8,512,256]{2,1,0:T(8,128)} %shard_map.54), channel_id=1, source_target_pairs={{0,64},{1,65},{2,66},{3,67},{4,68},{5,69},{6,70},{7,71},{8,72},{9,... | collective-permute-start | bytes 12582920 | tf_op jit(solution)/shard_map/ppermute | solution.py:36
  200.0 1.4 copy-done.9
  201.4 1.4 copy-done.11
  202.8 1.4 copy-done.14
  204.2 1.4 copy-done.16
  205.6 3.7 %shard_map.56 = f32[512,256]{1,0:T(8,128)S(1)} custom-call(s32[32]{0:T(128)S(1)} %constant_dynamic-update-slice_fusion.2.refs_0_, bf16[1,256,1536]{2,1,0:T(8,128)(2,1)S(1)} %copy-done.4, bf16[1,256,1536]{2,1,0:T(8,128)(2,1)S(1)} %copy-done.7, bf16[2,256,1536]{2,1,0:T(8,128)(2,1)} %collective-permute-done.13.refs_3_, bf16[2,256,1536]{2,1,0:T(8,128)(2,1)S(1)} %copy-done.9, ...), custom_call_target="tpu_custom_call" | custom-call | flops 805306368 | bytes 5242880 | tf_op jit(solution)/shard_map/pallas_call | solution.py:225
  209.4 1.2 select_select_fusion
  210.8 3.7 %collective-permute-start.26 = (f32[64,512]{1,0:T(8,128)S(1)}, f32[64,512]{1,0:T(8,128)S(1)}, u32[]{:S(2)}, u32[]{:S(2)}) collective-permute-start(f32[64,512]{1,0:T(8,128)S(1)} %get-tuple-element.172), channel_id=1, source_target_pairs={{0,1},{1,4},{8,9},{9,12},{16,17},{17,20},{24,25},{25,28},{32,33},{... | collective-permute-start | bytes 393224 | tf_op jit(solution)/shard_map/ppermute | solution.py:36
  214.4 1.9 collective-permute-start.32
  216.3 1.3 collective-permute-start.31
  217.6 1.3 collective-permute-start.28
  219.0 1.3 collective-permute-start.30
  220.3 4.3 %collective-permute-done.32 = f32[64,512]{1,0:T(8,128)S(1)} collective-permute-done((f32[64,512]{1,0:T(8,128)S(1)}, f32[64,512]{1,0:T(8,128)S(1)}, u32[]{:S(2)}, u32[]{:S(2)}) %collective-permute-start.32) | collective-permute-done | bytes 131104 | tf_op jit(solution)/shard_map/ppermute | solution.py:36
  224.5 1.3 collective-permute-start.27
  225.8 1.7 collective-permute-done.31
  227.5 1.3 collective-permute-start.29
  228.8 1.5 collective-permute-done.30
  231.7 16.0 %shard_map.55 = f32[8192,128]{1,0:T(8,128)} custom-call(s32[32]{0:T(128)S(1)} %constant_dynamic-update-slice_fusion.2.refs_0_, bf16[1,256,1536]{2,1,0:T(8,128)(2,1)S(1)} %copy-done.4, bf16[1,256,1536]{2,1,0:T(8,128)(2,1)S(1)} %copy-done.7, bf16[2,256,1536]{2,1,0:T(8,128)(2,1)} %collective-permute-done.13.refs_3_, bf16[2,256,1536]{2,1,0:T(8,128)(2,1)S(1)} %copy-done.9, ...), custom_call_target="tpu_custom_call" | custom-call | flops 6442450944 | bytes 25165824 | tf_op jit(solution)/shard_map/pallas_call | solution.py:179
  (134 shorter events, 22.1 us)
Async XLA Ops:
  2.8 29.0 %copy-start.33 = (bf16[1536,256]{1,0:T(8,128)(2,1)}, bf16[1536,256]{1,0:T(8,128)(2,1)S(1)}, u32[]{:S(2)}) copy-start(bf16[1536,256]{1,0:T(8,128)(2,1)S(1)} %constant_dynamic-update-slice_fusion) | copy-start | bytes 2359300
  2.8 29.0 %collective-permute-start.3 = (bf16[1536,256]{1,0:T(8,128)(2,1)S(1)}, bf16[1536,256]{1,0:T(8,128)(2,1)}, u32[]{:S(2)}, u32[]{:S(2)}) collective-permute-start(bf16[1536,256]{1,0:T(8,128)(2,1)S(1)} %constant_dynamic-update-slice_fusion), channel_id=1, source_target_pairs={{0,1},{1,0},{64,65},{65,64},{128,129},{129,128},{192,193},{193,192}} | collective-permute-start | bytes 2359304 | tf_op jit(solution)/shard_map/ppermute | solution.py:36
  7.4 11.3 %collective-permute-start = (bf16[256,768]{1,0:T(8,128)(2,1)S(1)}, bf16[256,768]{1,0:T(8,128)(2,1)S(1)}, u32[]{:S(2)}, u32[]{:S(2)}) collective-permute-start(bf16[256,768]{1,0:T(8,128)(2,1)S(1)} %bitcast.33), channel_id=1, source_target_pairs={{0,0},{1,1},{2,2},{3,3},{4,131},{5,130},{6,129},{7,128},{8,8},{9,9... | collective-permute-start | bytes 1179656 | tf_op jit(solution)/shard_map/ppermute | solution.py:36
  8.1 10.6 %collective-permute-start.2 = (bf16[1,768,256]{2,1,0:T(8,128)(2,1)S(1)}, bf16[1,768,256]{2,1,0:T(8,128)(2,1)S(1)}, u32[]{:S(2)}, u32[]{:S(2)}) collective-permute-start(bf16[1,768,256]{2,1,0:T(8,128)(2,1)S(1)} %bitcast.27), channel_id=1, source_target_pairs={{0,8},{1,9},{2,10},{3,11},{4,12},{5,13},{6,14},{7,15},{8,0},{9,1},... | collective-permute-start | bytes 1179656 | tf_op jit(solution)/shard_map/ppermute | solution.py:36
  8.9 14.7 %collective-permute-start.1 = (bf16[1,768,256]{2,1,0:T(8,128)(2,1)S(1)}, bf16[1,768,256]{2,1,0:T(8,128)(2,1)S(1)}, u32[]{:S(2)}, u32[]{:S(2)}) collective-permute-start(bf16[1,768,256]{2,1,0:T(8,128)(2,1)S(1)} %bitcast.25), channel_id=1, source_target_pairs={{0,128},{1,129},{2,130},{3,131},{4,132},{5,133},{6,134},{7,135},{8... | collective-permute-start | bytes 1179656 | tf_op jit(solution)/shard_map/ppermute | solution.py:36
  18.7 14.8 %copy-start.30 = (bf16[1,768,256]{2,1,0:T(8,128)(2,1)}, bf16[1,768,256]{2,1,0:T(8,128)(2,1)S(1)}, u32[]{:S(2)}) copy-start(bf16[1,768,256]{2,1,0:T(8,128)(2,1)S(1)} %collective-permute-done.2) | copy-start | bytes 1179652
  36.1 5.0 %collective-permute-start.5 = (f32[384,256]{1,0:T(8,128)S(1)}, f32[384,256]{1,0:T(8,128)S(1)}, u32[]{:S(2)}, u32[]{:S(2)}) collective-permute-start(f32[384,256]{1,0:T(8,128)S(1)} %dynamic-slice_bitcast_fusion), channel_id=1, source_target_pairs={{0,64},{1,65},{64,0},{65,1},{128,192},{129,193},{192,128},{193,129}} | collective-permute-start | bytes 1179656 | tf_op jit(solution)/shard_map/ppermute | solution.py:36
  39.7 1.5 collective-permute-start.4
  42.3 33.0 %copy-start.26 = (bf16[2,768,256]{2,1,0:T(8,128)(2,1)}, bf16[2,768,256]{2,1,0:T(8,128)(2,1)S(1)}, u32[]{:S(2)}) copy-start(bf16[2,768,256]{2,1,0:T(8,128)(2,1)S(1)} %pad_maximum_fusion.4) | copy-start | bytes 2359300
  42.4 35.4 %copy-start.28 = (bf16[2,768,256]{2,1,0:T(8,128)(2,1)}, bf16[2,768,256]{2,1,0:T(8,128)(2,1)S(1)}, u32[]{:S(2)}) copy-start(bf16[2,768,256]{2,1,0:T(8,128)(2,1)S(1)} %pad_maximum_fusion.5) | copy-start | bytes 2359300
  42.4 33.0 %collective-permute-start.9 = (bf16[2,768,256]{2,1,0:T(8,128)(2,1)S(1)}, bf16[2,768,256]{2,1,0:T(8,128)(2,1)}, u32[]{:S(2)}, u32[]{:S(2)}) collective-permute-start(bf16[2,768,256]{2,1,0:T(8,128)(2,1)S(1)} %pad_maximum_fusion.5), channel_id=1, source_target_pairs={{0,24},{1,25},{2,26},{3,27},{4,28},{5,29},{6,30},{7,31},{8,16},{9,... | collective-permute-start | bytes 2359304 | tf_op jit(solution)/shard_map/ppermute | solution.py:36
  42.5 32.9 %collective-permute-start.8 = (bf16[2,768,256]{2,1,0:T(8,128)(2,1)S(1)}, bf16[2,768,256]{2,1,0:T(8,128)(2,1)}, u32[]{:S(2)}, u32[]{:S(2)}) collective-permute-start(bf16[2,768,256]{2,1,0:T(8,128)(2,1)S(1)} %pad_maximum_fusion.4), channel_id=1, source_target_pairs={{0,160},{1,161},{2,162},{3,163},{4,164},{5,165},{6,166},{7,167},{8... | collective-permute-start | bytes 2359304 | tf_op jit(solution)/shard_map/ppermute | solution.py:36
  53.7 21.6 %collective-permute-start.7 = (f32[384,256]{1,0:T(8,128)S(1)}, f32[384,256]{1,0:T(8,128)S(1)}, u32[]{:S(2)}, u32[]{:S(2)}) collective-permute-start(f32[384,256]{1,0:T(8,128)S(1)} %bitcast_add_fusion), channel_id=1, source_target_pairs={{0,128},{1,129},{64,192},{65,193},{128,0},{129,1},{192,64},{193,65}} | collective-permute-start | bytes 1179656 | tf_op jit(solution)/shard_map/ppermute | solution.py:36
  55.6 19.7 %collective-permute-start.6 = (bf16[256,384]{1,0:T(8,128)(2,1)S(1)}, bf16[256,384]{1,0:T(8,128)(2,1)S(1)}, u32[]{:S(2)}, u32[]{:S(2)}) collective-permute-start(bf16[256,384]{1,0:T(8,128)(2,1)S(1)} %slice.83), channel_id=1, source_target_pairs={{0,0},{1,1},{2,2},{3,3},{4,131},{5,130},{6,129},{7,128},{8,8},{9,9... | collective-permute-start | bytes 589832 | tf_op jit(solution)/shard_map/ppermute | solution.py:36
  75.4 8.7 %collective-permute-start.11 = (f32[384,256]{1,0:T(8,128)S(1)}, f32[384,256]{1,0:T(8,128)S(1)}, u32[]{:S(2)}, u32[]{:S(2)}) collective-permute-start(f32[384,256]{1,0:T(8,128)S(1)} %add_select_fusion), channel_id=1, source_target_pairs={{0,32},{1,33},{64,96},{65,97},{128,160},{129,161},{192,224},{193,2... | collective-permute-start | bytes 1179656 | tf_op jit(solution)/shard_map/ppermute | solution.py:36
  77.8 15.4 %copy-start.2 = (bf16[1,256,1536]{2,1,0:T(8,128)(2,1)}, bf16[1,256,1536]{2,1,0:T(8,128)(2,1)S(1)}, u32[]{:S(2)}) copy-start(bf16[1,256,1536]{2,1,0:T(8,128)(2,1)S(1)} %maximum_bitcast_fusion.refs_1_) | copy-start | bytes 2359300
  77.8 15.4 %collective-permute-start.10 = (bf16[1,256,1536]{2,1,0:T(8,128)(2,1)S(1)}, bf16[1,256,1536]{2,1,0:T(8,128)(2,1)S(1)}, u32[]{:S(2)}, u32[]{:S(2)}) collective-permute-start(bf16[1,256,1536]{2,1,0:T(8,128)(2,1)S(1)} %maximum_bitcast_fusion.refs_1_), channel_id=1, source_target_pairs={{0,1},{1,0},{2,3},{3,2},{4,5},{5,4},{6,7},{7,6},{8,9},{9,8},{10,11... | collective-permute-start | bytes 2359304 | tf_op jit(solution)/shard_map/ppermute | solution.py:36
  84.1 9.1 %collective-permute-start.12 = (f32[384,256]{1,0:T(8,128)S(1)}, f32[384,256]{1,0:T(8,128)S(1)}, u32[]{:S(2)}, u32[]{:S(2)}) collective-permute-start(f32[384,256]{1,0:T(8,128)S(1)} %add.101), channel_id=1, source_target_pairs={{0,8},{1,9},{32,40},{33,41},{64,72},{65,73},{96,104},{97,105},{128... | collective-permute-start | bytes 1179656 | tf_op jit(solution)/shard_map/ppermute | solution.py:36
  87.1 92.1 %copy-start = (bf16[4,768,256]{2,1,0:T(8,128)(2,1)}, bf16[4,768,256]{2,1,0:T(8,128)(2,1)S(1)}, u32[]{:S(2)}) copy-start(bf16[4,768,256]{2,1,0:T(8,128)(2,1)S(1)} %get-tuple-element.164.refs_10_) | copy-start | bytes 4718596
  94.6 30.6 %collective-permute-start.13 = (bf16[2,256,1536]{2,1,0:T(8,128)(2,1)}, bf16[2,256,1536]{2,1,0:T(8,128)(2,1)}, u32[]{:S(2)}, u32[]{:S(2)}) collective-permute-start(bf16[2,256,1536]{2,1,0:T(8,128)(2,1)} %pad_maximum_fusion.2), channel_id=1, source_target_pairs={{0,7},{1,2},{2,1},{3,4},{4,3},{5,6},{6,5},{7,0},{8,15},{9,10},{10,... | collective-permute-start | bytes 4718600 | tf_op jit(solution)/shard_map/ppermute | solution.py:36
  95.6 29.6 %collective-permute-start.14 = (bf16[4,768,256]{2,1,0:T(8,128)(2,1)S(1)}, bf16[4,768,256]{2,1,0:T(8,128)(2,1)}, u32[]{:S(2)}, u32[]{:S(2)}) collective-permute-start(bf16[4,768,256]{2,1,0:T(8,128)(2,1)S(1)} %get-tuple-element.160.refs_6_), channel_id=1, source_target_pairs={{0,8},{1,9},{2,10},{3,11},{4,12},{5,13},{6,14},{7,15},{8,0},{9,1},... | collective-permute-start | bytes 4718600 | tf_op jit(solution)/shard_map/ppermute | solution.py:36
  95.6 29.6 %collective-permute-start.15 = (bf16[4,768,256]{2,1,0:T(8,128)(2,1)S(1)}, bf16[4,768,256]{2,1,0:T(8,128)(2,1)}, u32[]{:S(2)}, u32[]{:S(2)}) collective-permute-start(bf16[4,768,256]{2,1,0:T(8,128)(2,1)S(1)} %get-tuple-element.164.refs_10_), channel_id=1, source_target_pairs={{0,128},{1,129},{2,130},{3,131},{4,132},{5,133},{6,134},{7,135},{8... | collective-permute-start | bytes 4718600 | tf_op jit(solution)/shard_map/ppermute | solution.py:36
  100.6 20.8 %collective-permute-start.16 = (f32[384,256]{1,0:T(8,128)S(1)}, f32[384,256]{1,0:T(8,128)S(1)}, u32[]{:S(2)}, u32[]{:S(2)}) collective-permute-start(f32[384,256]{1,0:T(8,128)S(1)} %add.102), channel_id=1, source_target_pairs={{0,24},{1,25},{8,16},{9,17},{32,56},{33,57},{40,48},{41,49},{64,88... | collective-permute-start | bytes 1179656 | tf_op jit(solution)/shard_map/ppermute | solution.py:36
  121.5 3.7 %collective-permute-start.17 = (f32[384,256]{1,0:T(8,128)S(1)}, f32[384,256]{1,0:T(8,128)}, u32[]{:S(2)}, u32[]{:S(2)}) collective-permute-start(f32[384,256]{1,0:T(8,128)S(1)} %add.103), channel_id=1, source_target_pairs={{0,64},{1,65},{8,72},{9,73},{16,80},{17,81},{24,88},{25,89},{32,96... | collective-permute-start | bytes 1179656 | tf_op jit(solution)/shard_map/ppermute | solution.py:36
  130.3 25.8 %collective-permute-start.18 = (bf16[2,256,1536]{2,1,0:T(8,128)(2,1)}, bf16[2,256,1536]{2,1,0:T(8,128)(2,1)S(1)}, u32[]{:S(2)}, u32[]{:S(2)}) collective-permute-start(bf16[2,256,1536]{2,1,0:T(8,128)(2,1)} %collective-permute-done.13.refs_3_), channel_id=1, source_target_pairs={{0,1},{1,0},{2,3},{3,2},{4,5},{5,4},{6,7},{7,6},{8,9},{9,8},{10,11... | collective-permute-start | bytes 4718600 | tf_op jit(solution)/shard_map/ppermute | solution.py:36
  130.3 25.8 %collective-permute-start.19 = (bf16[4,768,256]{2,1,0:T(8,128)(2,1)S(1)}, bf16[4,768,256]{2,1,0:T(8,128)(2,1)S(1)}, u32[]{:S(2)}, u32[]{:S(2)}) collective-permute-start(bf16[4,768,256]{2,1,0:T(8,128)(2,1)S(1)} %get-tuple-element.160.refs_6_), channel_id=1, source_target_pairs={{0,24},{1,25},{2,26},{3,27},{4,28},{5,29},{6,30},{7,31},{8,16},{9,... | collective-permute-start | bytes 4718600 | tf_op jit(solution)/shard_map/ppermute | solution.py:36
  131.3 24.8 %collective-permute-start.20 = (bf16[4,768,256]{2,1,0:T(8,128)(2,1)S(1)}, bf16[4,768,256]{2,1,0:T(8,128)(2,1)S(1)}, u32[]{:S(2)}, u32[]{:S(2)}) collective-permute-start(bf16[4,768,256]{2,1,0:T(8,128)(2,1)S(1)} %get-tuple-element.164.refs_10_), channel_id=1, source_target_pairs={{0,160},{1,161},{2,162},{3,163},{4,164},{5,165},{6,166},{7,167},{8... | collective-permute-start | bytes 4718600 | tf_op jit(solution)/shard_map/ppermute | solution.py:36
  156.1 23.1 %copy-start.8 = (bf16[2,256,1536]{2,1,0:T(8,128)(2,1)}, bf16[2,256,1536]{2,1,0:T(8,128)(2,1)S(1)}, u32[]{:S(2)}) copy-start(bf16[2,256,1536]{2,1,0:T(8,128)(2,1)S(1)} %collective-permute-done.18.refs_4_) | copy-start | bytes 4718596
  156.1 23.0 %copy-start.10 = (bf16[4,768,256]{2,1,0:T(8,128)(2,1)}, bf16[4,768,256]{2,1,0:T(8,128)(2,1)S(1)}, u32[]{:S(2)}) copy-start(bf16[4,768,256]{2,1,0:T(8,128)(2,1)S(1)} %collective-permute-done.19.refs_8_) | copy-start | bytes 4718596
  156.2 23.0 %collective-permute-start.21 = (bf16[2,256,1536]{2,1,0:T(8,128)(2,1)S(1)}, bf16[2,256,1536]{2,1,0:T(8,128)(2,1)S(1)}, u32[]{:S(2)}, u32[]{:S(2)}) collective-permute-start(bf16[2,256,1536]{2,1,0:T(8,128)(2,1)S(1)} %collective-permute-done.18.refs_4_), channel_id=1, source_target_pairs={{0,7},{1,2},{2,1},{3,4},{4,3},{5,6},{6,5},{7,0},{8,15},{9,10},{10,... | collective-permute-start | bytes 4718600 | tf_op jit(solution)/shard_map/ppermute | solution.py:36
  156.3 22.9 %collective-permute-start.22 = (bf16[4,768,256]{2,1,0:T(8,128)(2,1)}, bf16[4,768,256]{2,1,0:T(8,128)(2,1)S(1)}, u32[]{:S(2)}, u32[]{:S(2)}) collective-permute-start(bf16[4,768,256]{2,1,0:T(8,128)(2,1)} %collective-permute-done.14.refs_7_), channel_id=1, source_target_pairs={{0,24},{1,25},{2,26},{3,27},{4,28},{5,29},{6,30},{7,31},{8,16},{9,... | collective-permute-start | bytes 4718600 | tf_op jit(solution)/shard_map/ppermute | solution.py:36
  157.2 21.9 %collective-permute-start.23 = (bf16[4,768,256]{2,1,0:T(8,128)(2,1)}, bf16[4,768,256]{2,1,0:T(8,128)(2,1)S(1)}, u32[]{:S(2)}, u32[]{:S(2)}) collective-permute-start(bf16[4,768,256]{2,1,0:T(8,128)(2,1)} %collective-permute-done.15.refs_11_), channel_id=1, source_target_pairs={{0,160},{1,161},{2,162},{3,163},{4,164},{5,165},{6,166},{7,167},{8... | collective-permute-start | bytes 4718600 | tf_op jit(solution)/shard_map/ppermute | solution.py:36
  167.1 13.2 %copy-start.3 = (bf16[1,256,1536]{2,1,0:T(8,128)(2,1)S(1)}, bf16[1,256,1536]{2,1,0:T(8,128)(2,1)}, u32[]{:S(2)}) copy-start(bf16[1,256,1536]{2,1,0:T(8,128)(2,1)} %copy-done.2) | copy-start | bytes 2359300
  167.1 13.2 %copy-start.6 = (bf16[1,256,1536]{2,1,0:T(8,128)(2,1)S(1)}, bf16[1,256,1536]{2,1,0:T(8,128)(2,1)}, u32[]{:S(2)}) copy-start(bf16[1,256,1536]{2,1,0:T(8,128)(2,1)} %copy-done.5) | copy-start | bytes 2359300
  179.1 14.4 %copy-start.13 = (bf16[2,256,1536]{2,1,0:T(8,128)(2,1)}, bf16[2,256,1536]{2,1,0:T(8,128)(2,1)S(1)}, u32[]{:S(2)}) copy-start(bf16[2,256,1536]{2,1,0:T(8,128)(2,1)S(1)} %collective-permute-done.21.refs_5_) | copy-start | bytes 4718596
  179.1 14.4 %copy-start.15 = (bf16[4,768,256]{2,1,0:T(8,128)(2,1)}, bf16[4,768,256]{2,1,0:T(8,128)(2,1)S(1)}, u32[]{:S(2)}) copy-start(bf16[4,768,256]{2,1,0:T(8,128)(2,1)S(1)} %collective-permute-done.22.refs_9_) | copy-start | bytes 4718596
  193.6 38.1 %collective-permute-start.24 = (f32[8,512,256]{2,1,0:T(8,128)}, f32[8,512,256]{2,1,0:T(8,128)}, u32[]{:S(2)}, u32[]{:S(2)}) collective-permute-start(f32[8,512,256]{2,1,0:T(8,128)} %shard_map.54), channel_id=1, source_target_pairs={{0,64},{1,65},{2,66},{3,67},{4,68},{5,69},{6,70},{7,71},{8,72},{9,... | collective-permute-start | bytes 12582920 | tf_op jit(solution)/shard_map/ppermute | solution.py:36
  198.7 10.6 %collective-permute-start.25 = (f32[512,256]{1,0:T(8,128)S(1)}, f32[512,256]{1,0:T(8,128)S(1)}, u32[]{:S(2)}, u32[]{:S(2)}) collective-permute-start(f32[512,256]{1,0:T(8,128)S(1)} %slice_bitcast_fusion), channel_id=1, source_target_pairs={{0,64},{1,65},{2,66},{3,67},{4,68},{5,69},{6,70},{7,71},{8,72},{9,... | collective-permute-start | bytes 1572872 | tf_op jit(solution)/shard_map/ppermute | solution.py:36
  209.4 22.3 %copy-start.12 = (bf16[4,768,256]{2,1,0:T(8,128)(2,1)S(1)}, bf16[4,768,256]{2,1,0:T(8,128)(2,1)}, u32[]{:S(2)}) copy-start(bf16[4,768,256]{2,1,0:T(8,128)(2,1)} %copy-done.10) | copy-start | bytes 4718596
  209.4 22.3 %copy-start.17 = (bf16[4,768,256]{2,1,0:T(8,128)(2,1)S(1)}, bf16[4,768,256]{2,1,0:T(8,128)(2,1)}, u32[]{:S(2)}) copy-start(bf16[4,768,256]{2,1,0:T(8,128)(2,1)} %copy-done.15) | copy-start | bytes 4718596
  210.6 21.1 %copy-start.1 = (bf16[4,768,256]{2,1,0:T(8,128)(2,1)S(1)}, bf16[4,768,256]{2,1,0:T(8,128)(2,1)}, u32[]{:S(2)}) copy-start(bf16[4,768,256]{2,1,0:T(8,128)(2,1)} %copy-done) | copy-start | bytes 4718596
  210.8 8.2 %collective-permute-start.26 = (f32[64,512]{1,0:T(8,128)S(1)}, f32[64,512]{1,0:T(8,128)S(1)}, u32[]{:S(2)}, u32[]{:S(2)}) collective-permute-start(f32[64,512]{1,0:T(8,128)S(1)} %get-tuple-element.172), channel_id=1, source_target_pairs={{0,1},{1,4},{8,9},{9,12},{16,17},{17,20},{24,25},{25,28},{32,33},{... | collective-permute-start | bytes 393224 | tf_op jit(solution)/shard_map/ppermute | solution.py:36
  214.4 10.1 %collective-permute-start.32 = (f32[64,512]{1,0:T(8,128)S(1)}, f32[64,512]{1,0:T(8,128)S(1)}, u32[]{:S(2)}, u32[]{:S(2)}) collective-permute-start(f32[64,512]{1,0:T(8,128)S(1)} %get-tuple-element.173), channel_id=1, source_target_pairs={{0,7},{8,15},{16,23},{24,31},{32,39},{40,47},{48,55},{56,63},{64,7... | collective-permute-start | bytes 393224 | tf_op jit(solution)/shard_map/ppermute | solution.py:36
  216.3 11.2 %collective-permute-start.31 = (f32[64,512]{1,0:T(8,128)S(1)}, f32[64,512]{1,0:T(8,128)S(1)}, u32[]{:S(2)}, u32[]{:S(2)}) collective-permute-start(f32[64,512]{1,0:T(8,128)S(1)} %get-tuple-element.174), channel_id=1, source_target_pairs={{0,6},{8,14},{16,22},{24,30},{32,38},{40,46},{48,54},{56,62},{64,7... | collective-permute-start | bytes 393224 | tf_op jit(solution)/shard_map/ppermute | solution.py:36
  217.6 11.1 %collective-permute-start.28 = (f32[64,512]{1,0:T(8,128)S(1)}, f32[64,512]{1,0:T(8,128)S(1)}, u32[]{:S(2)}, u32[]{:S(2)}) collective-permute-start(f32[64,512]{1,0:T(8,128)S(1)} %get-tuple-element.175), channel_id=1, source_target_pairs={{0,3},{1,6},{8,11},{9,14},{16,19},{17,22},{24,27},{25,30},{32,35},... | collective-permute-start | bytes 393224 | tf_op jit(solution)/shard_map/ppermute | solution.py:36
  219.0 11.3 %collective-permute-start.30 = (f32[64,512]{1,0:T(8,128)S(1)}, f32[64,512]{1,0:T(8,128)S(1)}, u32[]{:S(2)}, u32[]{:S(2)}) collective-permute-start(f32[64,512]{1,0:T(8,128)S(1)} %get-tuple-element.176), channel_id=1, source_target_pairs={{0,5},{8,13},{16,21},{24,29},{32,37},{40,45},{48,53},{56,61},{64,6... | collective-permute-start | bytes 393224 | tf_op jit(solution)/shard_map/ppermute | solution.py:36
  224.5 5.8 %collective-permute-start.27 = (f32[64,512]{1,0:T(8,128)S(1)}, f32[64,512]{1,0:T(8,128)S(1)}, u32[]{:S(2)}, u32[]{:S(2)}) collective-permute-start(f32[64,512]{1,0:T(8,128)S(1)} %get-tuple-element.177), channel_id=1, source_target_pairs={{0,2},{1,5},{8,10},{9,13},{16,18},{17,21},{24,26},{25,29},{32,34},... | collective-permute-start | bytes 393224 | tf_op jit(solution)/shard_map/ppermute | solution.py:36
  227.5 3.5 %collective-permute-start.29 = (f32[64,512]{1,0:T(8,128)S(1)}, f32[64,512]{1,0:T(8,128)S(1)}, u32[]{:S(2)}, u32[]{:S(2)}) collective-permute-start(f32[64,512]{1,0:T(8,128)S(1)} %get-tuple-element.178), channel_id=1, source_target_pairs={{0,4},{1,7},{8,12},{9,15},{16,20},{17,23},{24,28},{25,31},{32,36},... | collective-permute-start | bytes 393224 | tf_op jit(solution)/shard_map/ppermute | solution.py:36
  (20 other events, 81.1 us)

commit v3 on v2

--- a/solution.py
+++ b/solution.py
@@ -108,7 +108,7 @@
 
 def gram_kernel(own, scale, *refs):
     meta, refs = refs[0], refs[1:]
-    row_refs, first_refs, second_refs, refs = refs[:5], refs[5:9], refs[9:13], refs[13:]
+    row_refs, first_refs, second_refs, refs = refs[:4], refs[4:8], refs[8:12], refs[12:]
     if own:
         other_ref, out_ref, rows, cols, other, row_sem, col_sem, sem = refs
     else:
@@ -179,7 +179,7 @@
     return pl.pallas_call(
         functools.partial(gram_kernel, own, scale),
         out_shape=jax.ShapeDtypeStruct(shape, jnp.float32),
-        in_specs=[pl.BlockSpec(memory_space=pltpu.SMEM)] + [any_spec] * (13 + own),
+        in_specs=[pl.BlockSpec(memory_space=pltpu.SMEM)] + [any_spec] * (12 + own),
         out_specs=pl.BlockSpec(memory_space=pltpu.VMEM) if own else any_spec,
         scratch_shapes=[
             pltpu.VMEM((512, 2 * tokens), jnp.bfloat16),
@@ -189,7 +189,7 @@
             pltpu.SemaphoreType.DMA((4, 4, 2)),
             pltpu.SemaphoreType.DMA((8,)),
         ],
-        compiler_params=pltpu.CompilerParams(vmem_limit_bytes=40 * 2**20),
+        compiler_params=pltpu.CompilerParams(vmem_limit_bytes=62 * 2**20),
         cost_estimate=pl.CostEstimate(
             flops=2 * 512 * 2048 * 2 * tokens, bytes_accessed=24 * 2**20, transcendentals=0
         ),
@@ -198,12 +198,21 @@
 
 def lead_kernel(*refs):
     meta, refs = refs[0], refs[1:]
-    row_refs, first_refs, second_refs = refs[:5], refs[5:9], refs[9:13]
-    out_ref, rows, cols, row_sem, col_sem = refs[13:]
+    row_refs, first_refs, second_refs = refs[:4], refs[4:8], refs[8:12]
+    own_ref, away_ref, rows, cols, row_sem, col_sem = refs[12:]
     tokens = row_refs[0].shape[2]
     half = tokens // 2
-    wait_rows = start_rows(meta, meta[24], row_refs, rows, row_sem)
     copies = []
+    for ref in row_refs:
+        for i in range(ref.shape[0]):
+            slot = len(copies)
+            block, side = meta[8 + slot], meta[16 + slot]
+            at = jnp.where(block // 2 == meta[24], 0, 512) + (block % 2) * 256
+            dst = rows.at[
+                pl.ds(pl.multiple_of(at, 256), 256),
+                pl.ds(pl.multiple_of(side * tokens, tokens), tokens),
+            ]
+            copies.append((True, pltpu.make_async_copy(ref.at[i], dst, row_sem.at[slot])))
     for j in range(4):
         for i in range(4):
             want = (meta[i] // 2 == 0) & (meta[4 + j] == 0)
@@ -213,29 +222,30 @@
                 copies.append((want, pltpu.make_async_copy(ref, dst, col_sem.at[j, i, which])))
     for want, copy in copies:
         pl.when(want)(copy.start)
-    wait_rows()
     for want, copy in copies:
         pl.when(want)(copy.wait)
-    out_ref[...] = jnp.dot(rows[...], cols[...], preferred_element_type=jnp.float32)
+    own_ref[...] = jnp.dot(rows[:512], cols[...], preferred_element_type=jnp.float32)
+    away_ref[...] = jnp.dot(rows[512:], cols[...], preferred_element_type=jnp.float32)
 
 
 def lead_part(meta, row_bufs, first_bufs, second_bufs):
     tokens = row_bufs[0].shape[2]
     any_spec = pl.BlockSpec(memory_space=pl.ANY)
+    vmem = pl.BlockSpec(memory_space=pltpu.VMEM)
     return pl.pallas_call(
         lead_kernel,
-        out_shape=jax.ShapeDtypeStruct((512, 256), jnp.float32),
-        in_specs=[pl.BlockSpec(memory_space=pltpu.SMEM)] + [any_spec] * 13,
-        out_specs=pl.BlockSpec(memory_space=pltpu.VMEM),
+        out_shape=(jax.ShapeDtypeStruct((512, 256), jnp.float32),) * 2,
+        in_specs=[pl.BlockSpec(memory_space=pltpu.SMEM)] + [any_spec] * 12,
+        out_specs=(vmem, vmem),
         scratch_shapes=[
-            pltpu.VMEM((512, 2 * tokens), jnp.bfloat16),
+            pltpu.VMEM((1024, 2 * tokens), jnp.bfloat16),
             pltpu.VMEM((2 * tokens, 256), jnp.bfloat16),
             pltpu.SemaphoreType.DMA((8,)),
             pltpu.SemaphoreType.DMA((4, 4, 2)),
         ],
-        compiler_params=pltpu.CompilerParams(vmem_limit_bytes=40 * 2**20),
+        compiler_params=pltpu.CompilerParams(vmem_limit_bytes=62 * 2**20),
         cost_estimate=pl.CostEstimate(
-            flops=2 * 512 * 256 * 2 * tokens, bytes_accessed=5 * 2**20, transcendentals=0
+            flops=4 * 512 * 256 * 2 * tokens, bytes_accessed=9 * 2**20, transcendentals=0
         ),
     )(meta, *row_bufs, *first_bufs, *second_bufs)
 
@@ -316,7 +326,7 @@
             pltpu.VMEM((128, 128), jnp.float32),
         ],
         compiler_params=pltpu.CompilerParams(vmem_limit_bytes=32 * 2**20),
-        cost_estimate=pl.CostEstimate(flops=2**33, bytes_accessed=6 * 2**20, transcendentals=512),
+        cost_estimate=pl.CostEstimate(flops=2**20, bytes_accessed=2**20, transcendentals=512),
     )(work, upper, inverse)
 
 
@@ -331,16 +341,18 @@
     root = lambda x, y, z: (x // 2, y) == (0, 0) and z < 2
 
     cols = jnp.concatenate([acts_one, acts_two], 0)
-    one_t, two_t = acts_one.T, acts_two.T
+    piece = jnp.concatenate([acts_one.T, acts_two.T], 1)[None]
     a0, b0 = acts_one[None], acts_two[None]
-    one_t = move(one_t, row_home)
     a1 = move(a0, x_step(0))
     b1 = move(b0, y_step(0))
     other = move(cols, lambda x, y, z, c: (x, y, 1 - z, c) if root(x, y, z) else None)
-    one_t, a1, b1, other, two_t = after((one_t, a1, b1, other, two_t))
-
-    middle = two_t.shape[1] // 2
-    q3 = move(two_t[:, :middle], row_home)
+    a1, b1, other, piece = after((a1, b1, other, piece))
+
+    r0 = move(piece, row_home)
+    a01 = jnp.concatenate([a0, a1], 0)
+    b01 = jnp.concatenate([b0, b1], 0)
+    a23 = move(a01, x_step(1))
+    b23 = move(b01, y_step(1))
     left, right = jnp.where(z == 0, cols, other), jnp.where(z == 0, other, cols)
     part = [
         lax.dot_general(p, q, (((0,), (0,)), ((), ())), preferred_element_type=jnp.float32)
@@ -350,37 +362,26 @@
     lead = lax.dynamic_index_in_dim(part, core, 0, keepdims=False)
     away = lax.dynamic_index_in_dim(part, 1 - core, 0, keepdims=False)
     lead = lead + move(away, lambda x, y, z, c: (x, y, z, 1 - c) if root(x, y, z) else None)
-    q3, lead, one_t, two_t, a1, b1 = after((q3, lead, one_t, two_t, a1, b1))
-
-    q4 = move(two_t[:, middle:], row_home)
-    a01 = jnp.concatenate([a0, a1], 0)
-    b01 = jnp.concatenate([b0, b1], 0)
-    a23 = move(a01, x_step(1))
-    b23 = move(b01, y_step(1))
     lead = lead + move(lead, lambda x, y, z, c: (x ^ 1, y, z, c) if root(x, y, z) else None)
-    lead = jnp.where(row == 0, lead, 0.0)
-    q3, q4, lead, one_t, a01, a23, b01, b23 = after((q3, q4, lead, one_t, a01, a23, b01, b23))
-
-    r0 = jnp.concatenate([one_t, q3, q4], 1)[None]
+    r0, lead, a01, a23, b01, b23 = after((r0, lead, a01, a23, b01, b23))
+
     r1 = move(r0, z_step(0))
     first = jnp.concatenate([a01, a23], 0)
     second = jnp.concatenate([b01, b23], 0)
+    lead = jnp.where(row == 0, lead, 0.0)
     lead = lead + move(lead, lambda x, y, z, c: (x + 2, y, z, c) if root(x, y, z) else None)
-    lead = lead + move(lead, lambda x, y, z, c: (x, 1, z, c) if y == 0 and z < 2 else None)
+    sent = [
+        move(lead, lambda x, y, z, c, to=to: (x, to, z, c) if y == 0 and z < 2 else None)
+        for to in (1, 3, 2)
+    ]
+    lead = lead + (sent[0] + sent[1] + sent[2])
     r0, r1, first, second, lead = after((r0, r1, first, second, lead))
 
-    r2 = move(jnp.concatenate([r0, r1], 0), z_step(1))
+    r01 = jnp.concatenate([r0, r1], 0)
+    r2 = move(r01, z_step(1))
     first1 = move(first, y_step(0))
     second1 = move(second, x_step(0))
-    lead = lead + move(lead, lambda x, y, z, c: (x, 3 - y, z, c) if y < 2 and z < 2 else None)
     theirs = move(lead, lambda x, y, z, c: (x, y, z, 1 - c) if z < 2 else None)
-    r0, r1, r2, first, first1, second, second1, lead, theirs = after(
-        (r0, r1, r2, first, first1, second, second1, lead, theirs)
-    )
-
-    r3 = move(r2, z_step(2))
-    first2 = move(first, y_step(1))
-    second2 = move(second, x_step(1))
     low = jnp.where(core == 0, lead, theirs)
     high = jnp.where(core == 0, theirs, lead)
     corner = jnp.concatenate([low[256:], high[:128]], 0)
@@ -395,52 +396,66 @@
     work = jnp.where(ids[:, None] == ids[None, :], gram, reg_alpha * gram)
     zeros = jnp.zeros((512, 512), jnp.float32)
     state = factor_part(0, work, zeros, zeros)
+    r01, r2, first, first1, second, second1, state = after(
+        (r01, r2, first, first1, second, second1, state)
+    )
+
+    r3 = move(r2, z_step(2))
+    first2 = move(first, y_step(1))
+    second2 = move(second, x_step(1))
     state = factor_part(1, *state)
-    r0, r1, r2, r3, first, first1, first2, second, second1, second2, state = after(
-        (r0, r1, r2, r3, first, first1, first2, second, second1, second2, state)
+    state = factor_part(2, *state)
+    r01, r2, r3, first, first1, first2, second, second1, second2, state = after(
+        (r01, r2, r3, first, first1, first2, second, second1, second2, state)
     )
 
     r4 = move(r3, z_step(3))
     first3 = move(first1, y_step(1))
     second3 = move(second1, x_step(1))
-    state = factor_part(2, *state)
     _, upper, inverse = factor_part(3, *state)
-    r0, r1, r2, r3, r4, first, first1, first2, first3, second, second1, second2, second3, upper, inverse = after(
-        (r0, r1, r2, r3, r4, first, first1, first2, first3, second, second1, second2, second3, upper, inverse)
+    r01, r2, r3, r4, first, first1, first2, first3, second, second1, second2, second3, upper, inverse = after(
+        (r01, r2, r3, r4, first, first1, first2, first3, second, second1, second2, second3, upper, inverse)
     )
 
     pieces = (
-        (r0, r1, r2, r3, r4),
+        (r01, r2, r3, r4),
         (first, first1, first2, first3),
         (second, second1, second2, second3),
     )
     row_start = row * 2048 + cal * 512
     meta = meta.at[25].set(row_start).at[26].set(z * 256)
-    theirs = gram_part(scale, meta, *pieces)
-    theirs_lead = move(theirs[0], core_swap)
-    theirs = move(theirs, core_swap)
-
-    block = (lead_part(meta, *pieces) + theirs_lead) * scale
+
+    block, away = lead_part(meta, *pieces)
+    block = block + move(away, lambda x, y, z, c: (x, y, z, 1 - c) if z < 2 else None)
+    block = block * scale
     row_ids = row_start + jnp.arange(512, dtype=jnp.int32)[:, None]
     col_ids = z * 256 + jnp.arange(256, dtype=jnp.int32)[None, :]
     block = jnp.where(row_ids == col_ids, block, reg_alpha * block)
-    weights = jnp.where(z == 0, inverse[:, :256], inverse[:, 256:])
-    solved = lax.dot_general(
-        weights, block, (((1,), (1,)), ((), ())), precision=HIGHEST,
-        preferred_element_type=jnp.float32,
-    )
-    head = jnp.where(z == 0, upper, 0.0)
-    solved = jnp.where((row == 0) & (cal == 0), head, solved).reshape(8, 64, 512)
-    share = jnp.where(z == 0, solved[0], 0.0)
-    for to in range(1, 8):
-        extra = to + 3 if to < 5 else None
-
-        def target(x, y, z, c, to=to, extra=extra):
-            if z == 0:
-                return x, y, to, c
-            return (x, y, extra, c) if z == 1 and extra is not None else None
-
-        value = solved[to] if extra is None else jnp.where(z == 0, solved[to], solved[extra])
+    block, pieces = after((block, pieces))
+    left = move(block, lambda x, y, z, c: (x, y, 1, c) if z == 0 else None)
+
+    theirs = gram_part(scale, meta, *pieces)
+    theirs = move(theirs, core_swap)
+
+    def times(weights, rows):
+        return lax.dot_general(
+            weights, rows, (((1,), (1,)), ((), ())), precision=HIGHEST,
+            preferred_element_type=jnp.float32,
+        )
+
+    low = z == 0
+    solved = times(jnp.where(low, inverse[:256, :256], inverse[256:, 256:]), block)
+    solved = solved + times(jnp.where(low, 0.0, inverse[256:, :256]), left)
+    head = jnp.where(low, upper[:256], upper[256:])
+    solved = jnp.where((row == 0) & (cal == 0), head, solved).reshape(4, 64, 512)
+    share = jnp.where(low, solved[0], 0.0)
+    for i in range(4):
+        def target(x, y, z, c, i=i):
+            if z == 0 and i < 3:
+                return x, y, i + 1, c
+            return (x, y, i + 4, c) if z == 1 else None
+
+        value = jnp.where(low, solved[i + 1], solved[i]) if i < 3 else solved[i]
         share = share + move(value, target)
 
     gram_reg = gram_part(scale, meta, *pieces, other=theirs)

time: 252 us -> 254 us (level); the launches traced: 248 us -> 253 us
  starting transfers between devices: 71.6 us -> 86.6 us
  local copies, waits for them, and re-layouts: 17.7 us -> 7.57 us
  Pallas kernels: 72.5 us -> 79.8 us
  waiting for transfers between devices: 69.6 us -> 63.3 us
    ppermute x33 -> x30, starting transfers between devices: 71.6 us -> 86.6 us  [move(): return lax.ppermute(value, AXES, sorted(pairs))]
    unnamed x73 -> x20, local copies, waits for them, and re-layouts: 11.4 us -> 4.67 us
    ppermute x33 -> x30, waiting for transfers between devices: 69.6 us -> 63.3 us  [move(): return lax.ppermute(value, AXES, sorted(pairs))]
    pallas_call x2, Pallas kernels: 29.2 us -> 33.1 us  [gram_part(): pl.pallas_call(functools.partial(gram_kernel, own, scale), out_shape=jax....]
    pallas_call x1, Pallas kernels: 3.71 us -> 7.06 us  [lead_part(): pl.pallas_call(lead_kernel, out_shape=(jax.ShapeDtypeStruct((512, 256), j...]
  transfers between devices with their start and end apart: 33 -> 30, of which waited for: 11 -> 17; matrix products, arithmetic and copies ran while one was open for 3% -> 4% of each run, Pallas kernels for 17% -> 16%
where the time goes in v3:
time: 254 us; the launch traced here: 253 us
  starting transfers between devices  86.6 us (34%)
  Pallas kernels  79.8 us (31%)
  waiting for transfers between devices  63.3 us (25%)
  other arithmetic  7.9 us (3%)
  local copies, waits for them, and re-layouts  7.57 us (3%)
  matrix products  6.44 us (3%)
    ppermute x30, starting transfers between devices, move(): return lax.ppermute(value, AXES, sorted(pairs))  86.6 us
    ppermute x30, waiting for transfers between devices, move(): return lax.ppermute(value, AXES, sorted(pairs))  63.3 us
    pallas_call x4, Pallas kernels, factor_part(): pl.pallas_call(functools.partial(factor_kernel, k), out_shape=(shape,) *...  39.6 us
    pallas_call x2, Pallas kernels, gram_part(): pl.pallas_call(functools.partial(gram_kernel, own, scale), out_shape=jax....  33.1 us
    pallas_call x1, Pallas kernels, lead_part(): pl.pallas_call(lead_kernel, out_shape=(jax.ShapeDtypeStruct((512, 256), j...  7.06 us
  transfers between devices with their start and end apart: 30, of which 17 were waited for; matrix products, arithmetic and copies ran while one was open for 4% of the time, Pallas kernels for 16%

profile of v3, /device:TPU:1, one launch (start us, length us, event | category | flops | bytes accessed | tf_op | source)
XLA Modules:
  0.0 252.9 jit_solution(14067051093673589498)
XLA Ops:
  2.8 4.4 %collective-permute-start.2 = (bf16[1536,256]{1,0:T(8,128)(2,1)S(1)}, bf16[1536,256]{1,0:T(8,128)(2,1)}, u32[]{:S(2)}, u32[]{:S(2)}) collective-permute-start(bf16[1536,256]{1,0:T(8,128)(2,1)S(1)} %constant_dynamic-update-slice_fusion), channel_id=1, source_target_pairs={{0,1},{1,0},{64,65},{65,64},{128,129},{129,128},{192,193},{193,192}} | collective-permute-start | bytes 2359304 | tf_op jit(solution)/shard_map/ppermute | solution.py:36
  7.9 2.5 collective-permute-start
  11.7 3.4 %collective-permute-done.1 = bf16[1,768,256]{2,1,0:T(8,128)(2,1)S(1)} collective-permute-done((bf16[1,768,256]{2,1,0:T(8,128)(2,1)S(1)}, bf16[1,768,256]{2,1,0:T(8,128)(2,1)S(1)}, u32[]{:S(2)}, u32[]{:S(2)}) %collective-permute-start.1) | collective-permute-done | bytes 393248 | tf_op jit(solution)/shard_map/ppermute | solution.py:36
  15.7 7.6 %collective-permute-done.2 = bf16[1536,256]{1,0:T(8,128)(2,1)} collective-permute-done((bf16[1536,256]{1,0:T(8,128)(2,1)S(1)}, bf16[1536,256]{1,0:T(8,128)(2,1)}, u32[]{:S(2)}, u32[]{:S(2)}) %collective-permute-start.2) | collective-permute-done | bytes 786464 | tf_op jit(solution)/shard_map/ppermute | solution.py:36
  23.3 1.7 fusion
  25.0 1.9 fusion.2
  28.3 4.3 %collective-permute-start.4 = (f32[384,256]{1,0:T(8,128)}, f32[384,256]{1,0:T(8,128)}, u32[]{:S(2)}, u32[]{:S(2)}) collective-permute-start(f32[384,256]{1,0:T(8,128)} %dynamic-slice_bitcast_fusion), channel_id=1, source_target_pairs={{0,64},{1,65},{64,0},{65,1},{128,192},{129,193},{192,128},{193,129}} | collective-permute-start | bytes 1179656 | tf_op jit(solution)/shard_map/ppermute | solution.py:36
  32.9 1.3 collective-permute-start.6
  34.2 7.4 %collective-permute-start.3 = (bf16[1,256,1536]{2,1,0:T(8,128)(2,1)}, bf16[1,256,1536]{2,1,0:T(8,128)(2,1)}, u32[]{:S(2)}, u32[]{:S(2)}) collective-permute-start(bf16[1,256,1536]{2,1,0:T(8,128)(2,1)} %maximum_bitcast_fusion), channel_id=1, source_target_pairs={{0,0},{1,1},{2,2},{3,3},{4,131},{5,130},{6,129},{7,128},{8,8},{9,9... | collective-permute-start | bytes 2359304 | tf_op jit(solution)/shard_map/ppermute | solution.py:36
  42.7 1.9 collective-permute-start.5
  44.6 10.1 %collective-permute-done.5 = f32[384,256]{1,0:T(8,128)S(1)} collective-permute-done((f32[384,256]{1,0:T(8,128)S(1)}, f32[384,256]{1,0:T(8,128)S(1)}, u32[]{:S(2)}, u32[]{:S(2)}) %collective-permute-start.5) | collective-permute-done | bytes 393248 | tf_op jit(solution)/shard_map/ppermute | solution.py:36
  54.8 1.3 collective-permute-start.9
  56.1 18.6 %collective-permute-start.8 = (bf16[1,256,1536]{2,1,0:T(8,128)(2,1)}, bf16[1,256,1536]{2,1,0:T(8,128)(2,1)S(1)}, u32[]{:S(2)}, u32[]{:S(2)}) collective-permute-start(bf16[1,256,1536]{2,1,0:T(8,128)(2,1)} %collective-permute-done.3), channel_id=1, source_target_pairs={{0,1},{1,0},{2,3},{3,2},{4,5},{5,4},{6,7},{7,6},{8,9},{9,8},{10,11... | collective-permute-start | bytes 2359304 | tf_op jit(solution)/shard_map/ppermute | solution.py:36
  74.7 4.8 %collective-permute-done.9 = f32[384,256]{1,0:T(8,128)S(1)} collective-permute-done((f32[384,256]{1,0:T(8,128)S(1)}, f32[384,256]{1,0:T(8,128)S(1)}, u32[]{:S(2)}, u32[]{:S(2)}) %collective-permute-start.9) | collective-permute-done | bytes 393248 | tf_op jit(solution)/shard_map/ppermute | solution.py:36
  79.6 1.3 collective-permute-start.12
  80.9 1.3 collective-permute-start.11
  82.2 1.3 collective-permute-start.10
  83.5 3.3 %pad_maximum_fusion = (bf16[4,768,256]{2,1,0:T(8,128)(2,1)}, bf16[4,768,256]{2,1,0:T(8,128)(2,1)}) fusion(bf16[2,768,256]{2,1,0:T(8,128)(2,1)} %collective-permute-done.6, bf16[2,768,256]{2,1,0:T(8,128)(2,1)S(1)} %pad_maximum_fusion.3, bf16[2,768,256]{2,1,0:T(8,128)(2,1)} %collective-permute-done.7, bf16[2,768,256]{2,1,0:T(8,128)(2,1)S(1)} %pad_maximum_fusion.4), kind=kLoop, calls=%fused_computation | loop fusion | flops 1572864 | bytes 6291456 | tf_op jit(solution)/shard_map/concatenate | solution.py:369
  86.8 2.2 collective-permute-done.12
  89.0 1.3 collective-permute-done.11
  90.4 7.1 %collective-permute-done.10 = f32[384,256]{1,0:T(8,128)S(1)} collective-permute-done((f32[384,256]{1,0:T(8,128)S(1)}, f32[384,256]{1,0:T(8,128)S(1)}, u32[]{:S(2)}, u32[]{:S(2)}) %collective-permute-start.10) | collective-permute-done | bytes 393248 | tf_op jit(solution)/shard_map/ppermute | solution.py:36
  99.0 7.3 %collective-permute-start.15 = (bf16[4,768,256]{2,1,0:T(8,128)(2,1)}, bf16[4,768,256]{2,1,0:T(8,128)(2,1)}, u32[]{:S(2)}, u32[]{:S(2)}) collective-permute-start(bf16[4,768,256]{2,1,0:T(8,128)(2,1)} %get-tuple-element.171.refs_9_), channel_id=1, source_target_pairs={{0,128},{1,129},{2,130},{3,131},{4,132},{5,133},{6,134},{7,135},{8... | collective-permute-start | bytes 4718600 | tf_op jit(solution)/shard_map/ppermute | solution.py:36
  106.3 3.3 %collective-permute-start.16 = (f32[384,256]{1,0:T(8,128)S(1)}, f32[384,256]{1,0:T(8,128)S(1)}, u32[]{:S(2)}, u32[]{:S(2)}) collective-permute-start(f32[384,256]{1,0:T(8,128)S(1)} %add_add_fusion), channel_id=1, source_target_pairs={{0,64},{1,65},{8,72},{9,73},{16,80},{17,81},{24,88},{25,89},{32,96... | collective-permute-start | bytes 1179656 | tf_op jit(solution)/shard_map/ppermute | solution.py:36
  109.7 1.3 collective-permute-done.16
  111.6 9.9 %shard_map.50 = (f32[512,512]{1,0:T(8,128)S(1)}, f32[512,512]{1,0:T(8,128)S(1)}, f32[512,512]{1,0:T(8,128)S(1)}) custom-call(f32[512,512]{1,0:T(8,128)S(1)} %multiply_select_fusion.work_ref, f32[512,512]{1,0:T(8,128)S(1)} %broadcast_in_dim.32.u_in.inv_in, f32[512,512]{1,0:T(8,128)S(1)} %broadcast_in_dim.32.u_in.inv_in), custom_call_target="tpu_custom_call" | custom-call | flops 1048576 | bytes 1048576 | tf_op jit(solution)/shard_map/pallas_call | solution.py:319
  121.5 3.0 %collective-permute-done.15.refs_10_ = bf16[4,768,256]{2,1,0:T(8,128)(2,1)} collective-permute-done((bf16[4,768,256]{2,1,0:T(8,128)(2,1)}, bf16[4,768,256]{2,1,0:T(8,128)(2,1)}, u32[]{:S(2)}, u32[]{:S(2)}) %collective-permute-start.15) | collective-permute-done | bytes 1572896 | tf_op jit(solution)/shard_map/ppermute | solution.py:36
  124.4 2.2 collective-permute-start.18
  126.6 9.8 %shard_map.51 = (f32[512,512]{1,0:T(8,128)S(1)}, f32[512,512]{1,0:T(8,128)S(1)}, f32[512,512]{1,0:T(8,128)S(1)}) custom-call(f32[512,512]{1,0:T(8,128)S(1)} %get-tuple-element.126.work_ref, f32[512,512]{1,0:T(8,128)S(1)} %get-tuple-element.127.u_in, f32[512,512]{1,0:T(8,128)S(1)} %get-tuple-element.128.inv_in), custom_call_target="tpu_custom_call" | custom-call | flops 1048576 | bytes 1048576 | tf_op jit(solution)/shard_map/pallas_call | solution.py:319
  136.5 9.9 %shard_map.52 = (f32[512,512]{1,0:T(8,128)S(1)}, f32[512,512]{1,0:T(8,128)S(1)}, f32[512,512]{1,0:T(8,128)S(1)}) custom-call(f32[512,512]{1,0:T(8,128)S(1)} %get-tuple-element.129.work_ref, f32[512,512]{1,0:T(8,128)S(1)} %get-tuple-element.130.u_in, f32[512,512]{1,0:T(8,128)S(1)} %get-tuple-element.131.inv_in), custom_call_target="tpu_custom_call" | custom-call | flops 1048576 | bytes 1048576 | tf_op jit(solution)/shard_map/pallas_call | solution.py:319
  146.5 1.3 collective-permute-start.20
  147.8 1.4 collective-permute-start.22
  150.0 10.0 %shard_map.53 = (f32[512,512]{1,0:T(8,128)}, f32[512,512]{1,0:T(8,128)S(1)}, f32[512,512]{1,0:T(8,128)S(1)}) custom-call(f32[512,512]{1,0:T(8,128)S(1)} %get-tuple-element.144.work_ref, f32[512,512]{1,0:T(8,128)S(1)} %get-tuple-element.145.u_in, f32[512,512]{1,0:T(8,128)S(1)} %get-tuple-element.146.inv_in), custom_call_target="tpu_custom_call" | custom-call | flops 1048576 | bytes 1048576 | tf_op jit(solution)/shard_map/pallas_call | solution.py:319
  162.0 4.4 %collective-permute-done.20.refs_4_ = bf16[2,256,1536]{2,1,0:T(8,128)(2,1)} collective-permute-done((bf16[2,256,1536]{2,1,0:T(8,128)(2,1)}, bf16[2,256,1536]{2,1,0:T(8,128)(2,1)}, u32[]{:S(2)}, u32[]{:S(2)}) %collective-permute-start.20) | collective-permute-done | bytes 1572896 | tf_op jit(solution)/shard_map/ppermute | solution.py:36
  166.4 1.3 collective-permute-done.21.refs_8_
  167.7 7.1 %shard_map.54 = (f32[512,256]{1,0:T(8,128)}, f32[512,256]{1,0:T(8,128)}) custom-call(s32[32]{0:T(128)} %copy-done.7, bf16[2,256,1536]{2,1,0:T(8,128)(2,1)} %copy-done.4, bf16[2,256,1536]{2,1,0:T(8,128)(2,1)} %collective-permute-done.13.refs_2_, bf16[2,256,1536]{2,1,0:T(8,128)(2,1)} %collective-permute-done.17.refs_3_, ...), custom_call_target="tpu_custom_call" | custom-call | flops 1610612736 | bytes 9437184 | tf_op jit(solution)/shard_map/pallas_call | solution.py:235
  174.8 14.0 %collective-permute-start.23 = (f32[512,256]{1,0:T(8,128)}, f32[512,256]{1,0:T(8,128)S(1)}, u32[]{:S(2)}, u32[]{:S(2)}) collective-permute-start(f32[512,256]{1,0:T(8,128)} %get-tuple-element.162), channel_id=1, source_target_pairs={{0,64},{1,65},{8,72},{9,73},{16,80},{17,81},{24,88},{25,89},{32,96... | collective-permute-start | bytes 1572872 | tf_op jit(solution)/shard_map/ppermute | solution.py:36
  188.8 1.7 collective-permute-done.23
  190.5 1.2 multiply_select_fusion.1
  191.7 14.6 %shard_map.55 = f32[8,512,256]{2,1,0:T(8,128)} custom-call(s32[32]{0:T(128)} %copy-done.7, bf16[2,256,1536]{2,1,0:T(8,128)(2,1)} %copy-done.4, bf16[2,256,1536]{2,1,0:T(8,128)(2,1)} %collective-permute-done.13.refs_2_, bf16[2,256,1536]{2,1,0:T(8,128)(2,1)} %collective-permute-done.17.refs_3_, bf16[2,256,1536]{2,1,0:T(8,128)(2,1)} %collective-permute-done.20.refs_4_, ...), custom_call_target="tpu_custom_call" | custom-call | flops 6442450944 | bytes 25165824 | tf_op jit(solution)/shard_map/pallas_call | solution.py:179
  207.1 2.1 collective-permute-start.25
  209.9 9.9 %collective-permute-done.25 = f32[512,256]{1,0:T(8,128)} collective-permute-done((f32[512,256]{1,0:T(8,128)S(1)}, f32[512,256]{1,0:T(8,128)}, u32[]{:S(2)}, u32[]{:S(2)}) %collective-permute-start.25) | collective-permute-done | bytes 524320 | tf_op jit(solution)/shard_map/ppermute | solution.py:36
  219.8 1.7 select_select_fusion
  221.5 4.2 %collective-permute-start.26 = (f32[64,512]{1,0:T(8,128)S(1)}, f32[64,512]{1,0:T(8,128)S(1)}, u32[]{:S(2)}, u32[]{:S(2)}) collective-permute-start(f32[64,512]{1,0:T(8,128)S(1)} %get-tuple-element.182), channel_id=1, source_target_pairs={{0,1},{1,4},{8,9},{9,12},{16,17},{17,20},{24,25},{25,28},{32,33},{... | collective-permute-start | bytes 393224 | tf_op jit(solution)/shard_map/ppermute | solution.py:36
  225.8 1.3 collective-permute-start.28
  227.7 1.3 collective-permute-start.27
  229.1 1.6 collective-permute-done.28
  230.6 2.8 %collective-permute-done.27 = f32[64,512]{1,0:T(8,128)S(1)} collective-permute-done((f32[64,512]{1,0:T(8,128)S(1)}, f32[64,512]{1,0:T(8,128)S(1)}, u32[]{:S(2)}, u32[]{:S(2)}) %collective-permute-start.27) | collective-permute-done | bytes 131104 | tf_op jit(solution)/shard_map/ppermute | solution.py:36
  234.2 18.6 %shard_map.56 = f32[8192,128]{1,0:T(8,128)} custom-call(s32[32]{0:T(128)} %copy-done.7, bf16[2,256,1536]{2,1,0:T(8,128)(2,1)} %copy-done.4, bf16[2,256,1536]{2,1,0:T(8,128)(2,1)} %collective-permute-done.13.refs_2_, bf16[2,256,1536]{2,1,0:T(8,128)(2,1)} %collective-permute-done.17.refs_3_, bf16[2,256,1536]{2,1,0:T(8,128)(2,1)} %collective-permute-done.20.refs_4_, ...), custom_call_target="tpu_custom_call" | custom-call | flops 6442450944 | bytes 25165824 | tf_op jit(solution)/shard_map/pallas_call | solution.py:179
  (74 shorter events, 15.5 us)
Async XLA Ops:
  0.6 7.3 %copy-start.6 = (bf16[768,256]{1,0:T(8,128)(2,1)S(1)}, bf16[768,256]{1,0:T(8,128)(2,1)}, u32[]{:S(2)}) copy-start(bf16[768,256]{1,0:T(8,128)(2,1)} %param.7) | copy-start | bytes 1179652
  0.6 6.5 %copy-start.5 = (bf16[768,256]{1,0:T(8,128)(2,1)S(1)}, bf16[768,256]{1,0:T(8,128)(2,1)}, u32[]{:S(2)}) copy-start(bf16[768,256]{1,0:T(8,128)(2,1)} %param.8) | copy-start | bytes 1179652
  2.8 20.6 %collective-permute-start.2 = (bf16[1536,256]{1,0:T(8,128)(2,1)S(1)}, bf16[1536,256]{1,0:T(8,128)(2,1)}, u32[]{:S(2)}, u32[]{:S(2)}) collective-permute-start(bf16[1536,256]{1,0:T(8,128)(2,1)S(1)} %constant_dynamic-update-slice_fusion), channel_id=1, source_target_pairs={{0,1},{1,0},{64,65},{65,64},{128,129},{129,128},{192,193},{193,192}} | collective-permute-start | bytes 2359304 | tf_op jit(solution)/shard_map/ppermute | solution.py:36
  7.2 7.9 %collective-permute-start.1 = (bf16[1,768,256]{2,1,0:T(8,128)(2,1)S(1)}, bf16[1,768,256]{2,1,0:T(8,128)(2,1)S(1)}, u32[]{:S(2)}, u32[]{:S(2)}) collective-permute-start(bf16[1,768,256]{2,1,0:T(8,128)(2,1)S(1)} %bitcast.25), channel_id=1, source_target_pairs={{0,8},{1,9},{2,10},{3,11},{4,12},{5,13},{6,14},{7,15},{8,0},{9,1},... | collective-permute-start | bytes 1179656 | tf_op jit(solution)/shard_map/ppermute | solution.py:36
  7.9 7.8 %collective-permute-start = (bf16[1,768,256]{2,1,0:T(8,128)(2,1)S(1)}, bf16[1,768,256]{2,1,0:T(8,128)(2,1)S(1)}, u32[]{:S(2)}, u32[]{:S(2)}) collective-permute-start(bf16[1,768,256]{2,1,0:T(8,128)(2,1)S(1)} %bitcast.27), channel_id=1, source_target_pairs={{0,128},{1,129},{2,130},{3,131},{4,132},{5,133},{6,134},{7,135},{8... | collective-permute-start | bytes 1179656 | tf_op jit(solution)/shard_map/ppermute | solution.py:36
  28.3 13.3 %collective-permute-start.4 = (f32[384,256]{1,0:T(8,128)}, f32[384,256]{1,0:T(8,128)}, u32[]{:S(2)}, u32[]{:S(2)}) collective-permute-start(f32[384,256]{1,0:T(8,128)} %dynamic-slice_bitcast_fusion), channel_id=1, source_target_pairs={{0,64},{1,65},{64,0},{65,1},{128,192},{129,193},{192,128},{193,129}} | collective-permute-start | bytes 1179656 | tf_op jit(solution)/shard_map/ppermute | solution.py:36
  32.7 22.0 %collective-permute-start.7 = (bf16[2,768,256]{2,1,0:T(8,128)(2,1)S(1)}, bf16[2,768,256]{2,1,0:T(8,128)(2,1)}, u32[]{:S(2)}, u32[]{:S(2)}) collective-permute-start(bf16[2,768,256]{2,1,0:T(8,128)(2,1)S(1)} %pad_maximum_fusion.4), channel_id=1, source_target_pairs={{0,24},{1,25},{2,26},{3,27},{4,28},{5,29},{6,30},{7,31},{8,16},{9,... | collective-permute-start | bytes 2359304 | tf_op jit(solution)/shard_map/ppermute | solution.py:36
  32.9 21.9 %collective-permute-start.6 = (bf16[2,768,256]{2,1,0:T(8,128)(2,1)S(1)}, bf16[2,768,256]{2,1,0:T(8,128)(2,1)}, u32[]{:S(2)}, u32[]{:S(2)}) collective-permute-start(bf16[2,768,256]{2,1,0:T(8,128)(2,1)S(1)} %pad_maximum_fusion.3), channel_id=1, source_target_pairs={{0,160},{1,161},{2,162},{3,163},{4,164},{5,165},{6,166},{7,167},{8... | collective-permute-start | bytes 2359304 | tf_op jit(solution)/shard_map/ppermute | solution.py:36
  34.2 20.6 %collective-permute-start.3 = (bf16[1,256,1536]{2,1,0:T(8,128)(2,1)}, bf16[1,256,1536]{2,1,0:T(8,128)(2,1)}, u32[]{:S(2)}, u32[]{:S(2)}) collective-permute-start(bf16[1,256,1536]{2,1,0:T(8,128)(2,1)} %maximum_bitcast_fusion), channel_id=1, source_target_pairs={{0,0},{1,1},{2,2},{3,3},{4,131},{5,130},{6,129},{7,128},{8,8},{9,9... | collective-permute-start | bytes 2359304 | tf_op jit(solution)/shard_map/ppermute | solution.py:36
  42.7 12.0 %collective-permute-start.5 = (f32[384,256]{1,0:T(8,128)S(1)}, f32[384,256]{1,0:T(8,128)S(1)}, u32[]{:S(2)}, u32[]{:S(2)}) collective-permute-start(f32[384,256]{1,0:T(8,128)S(1)} %bitcast_add_fusion), channel_id=1, source_target_pairs={{0,128},{1,129},{64,192},{65,193},{128,0},{129,1},{192,64},{193,65}} | collective-permute-start | bytes 1179656 | tf_op jit(solution)/shard_map/ppermute | solution.py:36
  54.8 24.7 %collective-permute-start.9 = (f32[384,256]{1,0:T(8,128)S(1)}, f32[384,256]{1,0:T(8,128)S(1)}, u32[]{:S(2)}, u32[]{:S(2)}) collective-permute-start(f32[384,256]{1,0:T(8,128)S(1)} %broadcast_select_fusion.6), channel_id=1, source_target_pairs={{0,32},{1,33},{64,96},{65,97},{128,160},{129,161},{192,224},{193,2... | collective-permute-start | bytes 1179656 | tf_op jit(solution)/shard_map/ppermute | solution.py:36
  56.1 41.4 %collective-permute-start.8 = (bf16[1,256,1536]{2,1,0:T(8,128)(2,1)}, bf16[1,256,1536]{2,1,0:T(8,128)(2,1)S(1)}, u32[]{:S(2)}, u32[]{:S(2)}) collective-permute-start(bf16[1,256,1536]{2,1,0:T(8,128)(2,1)} %collective-permute-done.3), channel_id=1, source_target_pairs={{0,1},{1,0},{2,3},{3,2},{4,5},{5,4},{6,7},{7,6},{8,9},{9,8},{10,11... | collective-permute-start | bytes 2359304 | tf_op jit(solution)/shard_map/ppermute | solution.py:36
  79.6 9.5 %collective-permute-start.12 = (f32[384,256]{1,0:T(8,128)S(1)}, f32[384,256]{1,0:T(8,128)S(1)}, u32[]{:S(2)}, u32[]{:S(2)}) collective-permute-start(f32[384,256]{1,0:T(8,128)S(1)} %fusion.18), channel_id=1, source_target_pairs={{0,16},{1,17},{32,48},{33,49},{64,80},{65,81},{96,112},{97,113},{1... | collective-permute-start | bytes 1179656 | tf_op jit(solution)/shard_map/ppermute | solution.py:36
  80.9 9.5 %collective-permute-start.11 = (f32[384,256]{1,0:T(8,128)S(1)}, f32[384,256]{1,0:T(8,128)S(1)}, u32[]{:S(2)}, u32[]{:S(2)}) collective-permute-start(f32[384,256]{1,0:T(8,128)S(1)} %fusion.18), channel_id=1, source_target_pairs={{0,24},{1,25},{32,56},{33,57},{64,88},{65,89},{96,120},{97,121},{1... | collective-permute-start | bytes 1179656 | tf_op jit(solution)/shard_map/ppermute | solution.py:36
  82.2 15.3 %collective-permute-start.10 = (f32[384,256]{1,0:T(8,128)S(1)}, f32[384,256]{1,0:T(8,128)S(1)}, u32[]{:S(2)}, u32[]{:S(2)}) collective-permute-start(f32[384,256]{1,0:T(8,128)S(1)} %fusion.18), channel_id=1, source_target_pairs={{0,8},{1,9},{32,40},{33,41},{64,72},{65,73},{96,104},{97,105},{128... | collective-permute-start | bytes 1179656 | tf_op jit(solution)/shard_map/ppermute | solution.py:36
  98.8 12.3 %copy-start.4 = (bf16[2,256,1536]{2,1,0:T(8,128)(2,1)}, bf16[2,256,1536]{2,1,0:T(8,128)(2,1)S(1)}, u32[]{:S(2)}) copy-start(bf16[2,256,1536]{2,1,0:T(8,128)(2,1)S(1)} %constant_dynamic-update-slice_fusion.2.refs_1_) | copy-start | bytes 4718596
  98.8 22.6 %collective-permute-start.13 = (bf16[2,256,1536]{2,1,0:T(8,128)(2,1)S(1)}, bf16[2,256,1536]{2,1,0:T(8,128)(2,1)}, u32[]{:S(2)}, u32[]{:S(2)}) collective-permute-start(bf16[2,256,1536]{2,1,0:T(8,128)(2,1)S(1)} %constant_dynamic-update-slice_fusion.2.refs_1_), channel_id=1, source_target_pairs={{0,7},{1,2},{2,1},{3,4},{4,3},{5,6},{6,5},{7,0},{8,15},{9,10},{10,... | collective-permute-start | bytes 4718600 | tf_op jit(solution)/shard_map/ppermute | solution.py:36
  98.9 22.5 %collective-permute-start.14 = (bf16[4,768,256]{2,1,0:T(8,128)(2,1)}, bf16[4,768,256]{2,1,0:T(8,128)(2,1)}, u32[]{:S(2)}, u32[]{:S(2)}) collective-permute-start(bf16[4,768,256]{2,1,0:T(8,128)(2,1)} %get-tuple-element.167.refs_5_), channel_id=1, source_target_pairs={{0,8},{1,9},{2,10},{3,11},{4,12},{5,13},{6,14},{7,15},{8,0},{9,1},... | collective-permute-start | bytes 4718600 | tf_op jit(solution)/shard_map/ppermute | solution.py:36
  99.0 25.4 %collective-permute-start.15 = (bf16[4,768,256]{2,1,0:T(8,128)(2,1)}, bf16[4,768,256]{2,1,0:T(8,128)(2,1)}, u32[]{:S(2)}, u32[]{:S(2)}) collective-permute-start(bf16[4,768,256]{2,1,0:T(8,128)(2,1)} %get-tuple-element.171.refs_9_), channel_id=1, source_target_pairs={{0,128},{1,129},{2,130},{3,131},{4,132},{5,133},{6,134},{7,135},{8... | collective-permute-start | bytes 4718600 | tf_op jit(solution)/shard_map/ppermute | solution.py:36
  106.3 4.7 %collective-permute-start.16 = (f32[384,256]{1,0:T(8,128)S(1)}, f32[384,256]{1,0:T(8,128)S(1)}, u32[]{:S(2)}, u32[]{:S(2)}) collective-permute-start(f32[384,256]{1,0:T(8,128)S(1)} %add_add_fusion), channel_id=1, source_target_pairs={{0,64},{1,65},{8,72},{9,73},{16,80},{17,81},{24,88},{25,89},{32,96... | collective-permute-start | bytes 1179656 | tf_op jit(solution)/shard_map/ppermute | solution.py:36
  124.4 21.9 %collective-permute-start.17 = (bf16[2,256,1536]{2,1,0:T(8,128)(2,1)}, bf16[2,256,1536]{2,1,0:T(8,128)(2,1)}, u32[]{:S(2)}, u32[]{:S(2)}) collective-permute-start(bf16[2,256,1536]{2,1,0:T(8,128)(2,1)} %collective-permute-done.13.refs_2_), channel_id=1, source_target_pairs={{0,1},{1,0},{2,3},{3,2},{4,5},{5,4},{6,7},{7,6},{8,9},{9,8},{10,11... | collective-permute-start | bytes 4718600 | tf_op jit(solution)/shard_map/ppermute | solution.py:36
  124.4 22.0 %collective-permute-start.18 = (bf16[4,768,256]{2,1,0:T(8,128)(2,1)}, bf16[4,768,256]{2,1,0:T(8,128)(2,1)}, u32[]{:S(2)}, u32[]{:S(2)}) collective-permute-start(bf16[4,768,256]{2,1,0:T(8,128)(2,1)} %get-tuple-element.167.refs_5_), channel_id=1, source_target_pairs={{0,24},{1,25},{2,26},{3,27},{4,28},{5,29},{6,30},{7,31},{8,16},{9,... | collective-permute-start | bytes 4718600 | tf_op jit(solution)/shard_map/ppermute | solution.py:36
  126.6 19.9 %collective-permute-start.19 = (bf16[4,768,256]{2,1,0:T(8,128)(2,1)}, bf16[4,768,256]{2,1,0:T(8,128)(2,1)}, u32[]{:S(2)}, u32[]{:S(2)}) collective-permute-start(bf16[4,768,256]{2,1,0:T(8,128)(2,1)} %get-tuple-element.171.refs_9_), channel_id=1, source_target_pairs={{0,160},{1,161},{2,162},{3,163},{4,164},{5,165},{6,166},{7,167},{8... | collective-permute-start | bytes 4718600 | tf_op jit(solution)/shard_map/ppermute | solution.py:36
  146.5 19.9 %collective-permute-start.20 = (bf16[2,256,1536]{2,1,0:T(8,128)(2,1)}, bf16[2,256,1536]{2,1,0:T(8,128)(2,1)}, u32[]{:S(2)}, u32[]{:S(2)}) collective-permute-start(bf16[2,256,1536]{2,1,0:T(8,128)(2,1)} %collective-permute-done.17.refs_3_), channel_id=1, source_target_pairs={{0,7},{1,2},{2,1},{3,4},{4,3},{5,6},{6,5},{7,0},{8,15},{9,10},{10,... | collective-permute-start | bytes 4718600 | tf_op jit(solution)/shard_map/ppermute | solution.py:36
  147.8 19.9 %collective-permute-start.21 = (bf16[4,768,256]{2,1,0:T(8,128)(2,1)}, bf16[4,768,256]{2,1,0:T(8,128)(2,1)}, u32[]{:S(2)}, u32[]{:S(2)}) collective-permute-start(bf16[4,768,256]{2,1,0:T(8,128)(2,1)} %collective-permute-done.14.refs_6_), channel_id=1, source_target_pairs={{0,24},{1,25},{2,26},{3,27},{4,28},{5,29},{6,30},{7,31},{8,16},{9,... | collective-permute-start | bytes 4718600 | tf_op jit(solution)/shard_map/ppermute | solution.py:36
  147.8 19.9 %collective-permute-start.22 = (bf16[4,768,256]{2,1,0:T(8,128)(2,1)}, bf16[4,768,256]{2,1,0:T(8,128)(2,1)}, u32[]{:S(2)}, u32[]{:S(2)}) collective-permute-start(bf16[4,768,256]{2,1,0:T(8,128)(2,1)} %collective-permute-done.15.refs_10_), channel_id=1, source_target_pairs={{0,160},{1,161},{2,162},{3,163},{4,164},{5,165},{6,166},{7,167},{8... | collective-permute-start | bytes 4718600 | tf_op jit(solution)/shard_map/ppermute | solution.py:36
  150.0 10.0 %copy-start.7 = (s32[32]{0:T(128)}, s32[32]{0:T(128)S(1)}, u32[]{:S(2)}) copy-start(s32[32]{0:T(128)S(1)} %constant_dynamic-update-slice_fusion.4.refs_0_) | copy-start | bytes 388
  160.0 1.0 copy-start
  160.9 1.0 copy-start.2
  174.8 15.7 %collective-permute-start.23 = (f32[512,256]{1,0:T(8,128)}, f32[512,256]{1,0:T(8,128)S(1)}, u32[]{:S(2)}, u32[]{:S(2)}) collective-permute-start(f32[512,256]{1,0:T(8,128)} %get-tuple-element.162), channel_id=1, source_target_pairs={{0,64},{1,65},{8,72},{9,73},{16,80},{17,81},{24,88},{25,89},{32,96... | collective-permute-start | bytes 1572872 | tf_op jit(solution)/shard_map/ppermute | solution.py:36
  191.7 17.5 %copy-start.3 = (f32[512,512]{1,0:T(8,128)S(1)}, f32[512,512]{1,0:T(8,128)}, u32[]{:S(2)}) copy-start(f32[512,512]{1,0:T(8,128)} %copy-done.2) | copy-start | bytes 3145732
  206.3 13.5 %copy-start.1 = (f32[512,512]{1,0:T(8,128)S(1)}, f32[512,512]{1,0:T(8,128)}, u32[]{:S(2)}) copy-start(f32[512,512]{1,0:T(8,128)} %copy-done) | copy-start | bytes 3145732
  206.3 27.9 %collective-permute-start.24 = (f32[8,512,256]{2,1,0:T(8,128)}, f32[8,512,256]{2,1,0:T(8,128)}, u32[]{:S(2)}, u32[]{:S(2)}) collective-permute-start(f32[8,512,256]{2,1,0:T(8,128)} %shard_map.55), channel_id=1, source_target_pairs={{0,64},{1,65},{2,66},{3,67},{4,68},{5,69},{6,70},{7,71},{8,72},{9,... | collective-permute-start | bytes 12582920 | tf_op jit(solution)/shard_map/ppermute | solution.py:36
  207.1 12.7 %collective-permute-start.25 = (f32[512,256]{1,0:T(8,128)S(1)}, f32[512,256]{1,0:T(8,128)}, u32[]{:S(2)}, u32[]{:S(2)}) collective-permute-start(f32[512,256]{1,0:T(8,128)S(1)} %multiply_select_fusion.1), channel_id=1, source_target_pairs={{0,1},{8,9},{16,17},{24,25},{32,33},{40,41},{48,49},{56,57},{64,65... | collective-permute-start | bytes 1572872 | tf_op jit(solution)/shard_map/ppermute | solution.py:36
  221.5 7.5 %collective-permute-start.26 = (f32[64,512]{1,0:T(8,128)S(1)}, f32[64,512]{1,0:T(8,128)S(1)}, u32[]{:S(2)}, u32[]{:S(2)}) collective-permute-start(f32[64,512]{1,0:T(8,128)S(1)} %get-tuple-element.182), channel_id=1, source_target_pairs={{0,1},{1,4},{8,9},{9,12},{16,17},{17,20},{24,25},{25,28},{32,33},{... | collective-permute-start | bytes 393224 | tf_op jit(solution)/shard_map/ppermute | solution.py:36
  225.8 4.9 %collective-permute-start.28 = (f32[64,512]{1,0:T(8,128)S(1)}, f32[64,512]{1,0:T(8,128)S(1)}, u32[]{:S(2)}, u32[]{:S(2)}) collective-permute-start(f32[64,512]{1,0:T(8,128)S(1)} %get-tuple-element.183), channel_id=1, source_target_pairs={{0,3},{1,6},{8,11},{9,14},{16,19},{17,22},{24,27},{25,30},{32,35},... | collective-permute-start | bytes 393224 | tf_op jit(solution)/shard_map/ppermute | solution.py:36
  227.1 3.6 %collective-permute-start.29 = (f32[64,512]{1,0:T(8,128)S(1)}, f32[64,512]{1,0:T(8,128)S(1)}, u32[]{:S(2)}, u32[]{:S(2)}) collective-permute-start(f32[64,512]{1,0:T(8,128)S(1)} %get-tuple-element.184), channel_id=1, source_target_pairs={{1,7},{9,15},{17,23},{25,31},{33,39},{41,47},{49,55},{57,63},{65,7... | collective-permute-start | bytes 393224 | tf_op jit(solution)/shard_map/ppermute | solution.py:36
  227.7 5.7 %collective-permute-start.27 = (f32[64,512]{1,0:T(8,128)S(1)}, f32[64,512]{1,0:T(8,128)S(1)}, u32[]{:S(2)}, u32[]{:S(2)}) collective-permute-start(f32[64,512]{1,0:T(8,128)S(1)} %get-tuple-element.185), channel_id=1, source_target_pairs={{0,2},{1,5},{8,10},{9,13},{16,18},{17,21},{24,26},{25,29},{32,34},... | collective-permute-start | bytes 393224 | tf_op jit(solution)/shard_map/ppermute | solution.py:36

commit v4 on v3

v4 whole, which is shorter than its diff:
```python
import functools

import jax
import jax.numpy as jnp
import numpy as np
from jax import lax
from jax.experimental import pallas as pl
from jax.experimental.pallas import tpu as pltpu
from jax.sharding import PartitionSpec as P

PANEL = 512
reg_alpha = 0.9
AXES = ("cal", "row", "col")
NX, NY, NZ = 4, 4, 8
HIGHEST = lax.Precision.HIGHEST


def flat(x, y, z, core):
    return (((x % 2) * 2 + core) * 8 + (x // 2) * 4 + y) * 8 + z


def devices():
    for x in range(NX):
        for y in range(NY):
            for z in range(NZ):
                for core in range(2):
                    yield x, y, z, core


def move(value, target):
    pairs = []
    for device in devices():
        to = target(*device)
        if to is not None:
            pairs.append((flat(*device), flat(*to)))
    return lax.ppermute(value, AXES, sorted(pairs))


def near(i, size, phase):
    return i ^ 1 if phase == 0 else (i + 1 if i % 2 else i - 1) % size


def x_step(s):
    return lambda x, y, z, c: (near(x, NX, (s + c) % 2), y, z, c)


def y_step(s):
    return lambda x, y, z, c: (x, near(y, NY, (s + c) % 2), z, c)


def z_step(s):
    return lambda x, y, z, c: (x, y, near(z, NZ, (s + c) % 2), c)


def core_swap(x, y, z, c):
    return x, y, z, 1 - c


def row_home(x, y, z, c):
    return (x, y, z, c) if z // 4 == x % 2 else (x ^ 1, y, 7 - z, c)


def tables():
    table = np.zeros((256, 32), np.int32)
    for x, y, z, c in devices():
        def ring4(i):
            p1 = lambda v: near(v, 4, c % 2)
            p2 = lambda v: near(v, 4, (1 + c) % 2)
            return [i, p1(i), p2(i), p1(p2(i))]

        step = lambda v, s: near(v, NZ, (s + c) % 2)
        first = lambda v: [v, step(v, 0)]
        third = lambda v: first(step(step(v, 2), 1))
        slots = first(z) + first(step(z, 1)) + third(z) + third(step(z, 3))
        assert sorted(slots) == list(range(8))
        low = x % 2
        blocks = [(p if p // 4 == low else 7 - p) - 4 * low for p in slots]
        halves = [low if p // 4 == low else 1 - low for p in slots]
        table[flat(x, y, z, c)] = ring4(x) + ring4(y) + blocks + halves + [c, low] + [0] * 6
    return table


TABLE = tables()


def join_kernel(*refs):
    n = len(refs) - 2
    out_ref, sem = refs[n], refs[n + 1]
    copies, at = [], 0
    for i in range(n):
        size = refs[i].shape[0]
        copy = pltpu.make_async_copy(refs[i], out_ref.at[pl.ds(at, size)], sem.at[i])
        copy.start()
        copies.append(copy)
        at += size
    for copy in copies:
        copy.wait()


def join(*parts):
    any_spec = pl.BlockSpec(memory_space=pl.ANY)
    rows = sum(p.shape[0] for p in parts)
    return pl.pallas_call(
        join_kernel,
        out_shape=jax.ShapeDtypeStruct((rows,) + parts[0].shape[1:], parts[0].dtype),
        in_specs=[any_spec] * len(parts),
        out_specs=any_spec,
        scratch_shapes=[pltpu.SemaphoreType.DMA((len(parts),))],
        cost_estimate=pl.CostEstimate(flops=0, bytes_accessed=2**20, transcendentals=0),
    )(*parts)


def transpose_kernel(one_ref, two_ref, out_ref):
    tokens = one_ref.shape[0]
    out_ref[0, :, :tokens] = one_ref[...].T
    out_ref[0, :, tokens:] = two_ref[...].T


def transposed(one, two):
    full = pl.BlockSpec(memory_space=pltpu.VMEM)
    return pl.pallas_call(
        transpose_kernel,
        out_shape=jax.ShapeDtypeStruct((1, one.shape[1], 2 * one.shape[0]), one.dtype),
        in_specs=[full, full],
        out_specs=full,
        cost_estimate=pl.CostEstimate(flops=0, bytes_accessed=2**20, transcendentals=0),
    )(one, two)


def column(meta, j, pair):
    x = jnp.where(meta[24] == 0, meta[2 * pair], meta[pair])
    return (x // 2) * 4 + meta[4 + j]


def column_copies(meta, first_refs, second_refs, cols, sem, j, needed=None):
    half = first_refs[0].shape[1]
    copies = []
    for i in range(4):
        pair = jnp.where(meta[24] == 0, i // 2, i % 2)
        side = meta[i] % 2
        for which, ref in ((0, first_refs[j].at[i]), (1, second_refs[i].at[j])):
            dst = cols.at[
                2 * j + pair,
                pl.ds(pl.multiple_of(side * 2 * half + which * half, half), half),
            ]
            want = True if needed is None else needed(side)
            copies.append((want, pltpu.make_async_copy(ref, dst, sem.at[j, i, which])))
    return copies


def start_all(copies):
    for want, copy in copies:
        pl.when(want)(copy.start)


def wait_all(copies):
    for want, copy in copies:
        pl.when(want)(copy.wait)


def early_kernel(own, *refs):
    meta, row_refs, first_refs, second_refs = refs[0], refs[1:4], refs[4:8], refs[8:12]
    out_ref, rows, cols, acc, row_sem, col_sem, sem = refs[12:]
    tokens = row_refs[0].shape[2]
    wanted = meta[24] if own else 1 - meta[24]

    def place(slot):
        return rows.at[
            pl.ds(pl.multiple_of((meta[8 + slot] % 2) * 256, 256), 256),
            pl.ds(pl.multiple_of(meta[16 + slot] * tokens, tokens), tokens),
        ]

    row_copies = []
    for slot in range(6):
        copy = pltpu.make_async_copy(row_refs[slot // 2].at[slot % 2], place(slot), row_sem.at[slot])
        row_copies.append((meta[8 + slot] // 2 == wanted, copy))
    col_copies = [column_copies(meta, first_refs, second_refs, cols, col_sem, j) for j in range(4)]
    start_all(row_copies)
    start_all(col_copies[0])
    start_all(col_copies[1])
    for slot in (6, 7):
        @pl.when(meta[8 + slot] // 2 == wanted)
        def _(slot=slot):
            place(slot)[...] = jnp.zeros((256, tokens), rows.dtype)
    wait_all(row_copies)
    out_copies = []
    for j in range(4):
        wait_all(col_copies[j])
        if j + 2 < 4:
            start_all(col_copies[j + 2])
        for pair in range(2):
            k = 2 * j + pair
            acc[k] = jnp.dot(rows[...], cols[k], preferred_element_type=jnp.float32)
            copy = pltpu.make_async_copy(acc.at[k], out_ref.at[column(meta, j, pair)], sem.at[k])
            copy.start()
            out_copies.append(copy)
    for copy in out_copies:
        copy.wait()


def early_part(own, meta, rows, first_bufs, second_bufs):
    tokens = rows[0].shape[2]
    any_spec = pl.BlockSpec(memory_space=pl.ANY)
    return pl.pallas_call(
        functools.partial(early_kernel, own),
        out_shape=jax.ShapeDtypeStruct((8, 512, 256), jnp.float32),
        in_specs=[pl.BlockSpec(memory_space=pltpu.SMEM)] + [any_spec] * 11,
        out_specs=any_spec,
        scratch_shapes=[
            pltpu.VMEM((512, 2 * tokens), jnp.bfloat16),
            pltpu.VMEM((8, 2 * tokens, 256), jnp.bfloat16),
            pltpu.VMEM((8, 512, 256), jnp.float32),
            pltpu.SemaphoreType.DMA((6,)),
            pltpu.SemaphoreType.DMA((4, 4, 2)),
            pltpu.SemaphoreType.DMA((8,)),
        ],
        compiler_params=pltpu.CompilerParams(vmem_limit_bytes=62 * 2**20),
        cost_estimate=pl.CostEstimate(flops=2**20, bytes_accessed=2**20, transcendentals=0),
    )(meta, *rows, *first_bufs, *second_bufs)


def late_kernel(own, scale, *refs):
    meta, row_ref, first_refs, second_refs, early_ref = refs[0], refs[1], refs[2:6], refs[6:10], refs[10]
    refs = refs[11:]
    if own:
        other_ref, out_ref, rows, cols, acc, other, row_sem, col_sem, sem, other_sem = refs
    else:
        out_ref, rows, cols, acc, row_sem, col_sem, sem = refs
    tokens = row_ref.shape[2]
    wanted = meta[24] if own else 1 - meta[24]
    mine = [meta[8 + slot] // 2 == wanted for slot in (6, 7)]
    needed = lambda side: (mine[0] & (meta[22] == side)) | (mine[1] & (meta[23] == side))
    row_copies = [
        (mine[i], pltpu.make_async_copy(row_ref.at[i], rows.at[i], row_sem.at[i])) for i in range(2)
    ]
    groups = []
    for j in range(4):
        group = column_copies(meta, first_refs, second_refs, cols, col_sem, j, needed)
        for pair in range(2):
            k, a = 2 * j + pair, column(meta, j, pair)
            group.append((True, pltpu.make_async_copy(early_ref.at[a], acc.at[k], sem.at[k])))
            if own:
                copy = pltpu.make_async_copy(other_ref.at[a], other.at[k], other_sem.at[k])
                group.append((True, copy))
        groups.append(group)
    start_all(row_copies)
    start_all(groups[0])
    start_all(groups[1])
    wait_all(row_copies)
    row_ids = meta[25] + lax.broadcasted_iota(jnp.int32, (512, 128), 0)
    lane = meta[26] + lax.broadcasted_iota(jnp.int32, (512, 128), 1)
    out_copies = []
    for j in range(4):
        wait_all(groups[j])
        if j + 2 < 4:
            start_all(groups[j + 2])
        for i in range(2):
            @pl.when(mine[i])
            def _(i=i):
                at = pl.ds(pl.multiple_of((meta[14 + i] % 2) * 256, 256), 256)
                side = pl.ds(pl.multiple_of(meta[22 + i] * tokens, tokens), tokens)
                for pair in range(2):
                    k = 2 * j + pair
                    acc[k, at, :] += jnp.dot(
                        rows[i], cols[k, side, :], preferred_element_type=jnp.float32
                    )
        for pair in range(2):
            k, a = 2 * j + pair, column(meta, j, pair)
            if own:
                for h in range(2):
                    at = slice(h * 128, (h + 1) * 128)
                    part = (acc[k, :, at] + other[k, :, at]) * scale
                    same = row_ids == lane + (a * 2048 + h * 128)
                    out_ref[pl.ds(2 * a + h, 512, stride=16), :] = jnp.where(
                        same, part, reg_alpha * part
                    )
            else:
                copy = pltpu.make_async_copy(acc.at[k], out_ref.at[a], sem.at[k])
                copy.start()
                out_copies.append(copy)
    for copy in out_copies:
        copy.wait()


def late_part(scale, meta, row, first_bufs, second_bufs, early, other=None):
    own = other is not None
    tokens = row.shape[2]
    any_spec = pl.BlockSpec(memory_space=pl.ANY)
    shape = (512 * 16, 128) if own else (8, 512, 256)
    half = pltpu.VMEM((8, 512, 256), jnp.float32)
    return pl.pallas_call(
        functools.partial(late_kernel, own, scale),
        out_shape=jax.ShapeDtypeStruct(shape, jnp.float32),
        in_specs=[pl.BlockSpec(memory_space=pltpu.SMEM)] + [any_spec] * (10 + own),
        out_specs=pl.BlockSpec(memory_space=pltpu.VMEM) if own else any_spec,
        scratch_shapes=[
            pltpu.VMEM((2, 256, tokens), jnp.bfloat16),
            pltpu.VMEM((8, 2 * tokens, 256), jnp.bfloat16),
        ]
        + [half] * (1 + own)
        + [
            pltpu.SemaphoreType.DMA((2,)),
            pltpu.SemaphoreType.DMA((4, 4, 2)),
            pltpu.SemaphoreType.DMA((8,)),
        ]
        + [pltpu.SemaphoreType.DMA((8,))] * own,
        compiler_params=pltpu.CompilerParams(vmem_limit_bytes=62 * 2**20),
        cost_estimate=pl.CostEstimate(
            flops=2 * 512 * 2048 * 2 * tokens, bytes_accessed=24 * 2**20, transcendentals=0
        ),
    )(meta, row, *first_bufs, *second_bufs, early, *([other] if own else []))


def lead_kernel(*refs):
    meta, row_ref, first_refs, second_refs = refs[0], refs[1], refs[2:6], refs[6:10]
    early_refs, out_refs = refs[10:12], refs[12:14]
    rows, cols, row_sem, col_sem, sem = refs[14:]
    tokens = row_ref.shape[2]
    half = tokens // 2
    copies = [
        (True, pltpu.make_async_copy(row_ref.at[i], rows.at[i], row_sem.at[i])) for i in range(2)
    ]
    for h in range(2):
        copies.append((True, pltpu.make_async_copy(early_refs[h].at[0], out_refs[h], sem.at[h])))
    for j in range(4):
        for i in range(4):
            side = meta[i] % 2
            want = (meta[i] // 2 == 0) & (meta[4 + j] == 0)
            for which, ref in ((0, first_refs[j].at[i]), (1, second_refs[i].at[j])):
                dst = cols.at[pl.ds(pl.multiple_of(side * tokens + which * half, half), half)]
                copies.append((want, pltpu.make_async_copy(ref, dst, col_sem.at[j, i, which])))
    start_all(copies)
    wait_all(copies)
    for i in range(2):
        at = pl.ds(pl.multiple_of((meta[14 + i] % 2) * 256, 256), 256)
        side = pl.ds(pl.multiple_of(meta[22 + i] * tokens, tokens), tokens)
        part = jnp.dot(rows[i], cols[side, :], preferred_element_type=jnp.float32)
        for h in range(2):
            @pl.when((meta[14 + i] // 2 == meta[24]) == (h == 0))
            def _(h=h, at=at, part=part):
                out_refs[h][at, :] += part


def lead_part(meta, row, first_bufs, second_bufs, early_own, early_away):
    tokens = row.shape[2]
    any_spec = pl.BlockSpec(memory_space=pl.ANY)
    vmem = pl.BlockSpec(memory_space=pltpu.VMEM)
    return pl.pallas_call(
        lead_kernel,
        out_shape=(jax.ShapeDtypeStruct((512, 256), jnp.float32),) * 2,
        in_specs=[pl.BlockSpec(memory_space=pltpu.SMEM)] + [any_spec] * 11,
        out_specs=(vmem, vmem),
        scratch_shapes=[
            pltpu.VMEM((2, 256, tokens), jnp.bfloat16),
            pltpu.VMEM((2 * tokens, 256), jnp.bfloat16),
            pltpu.SemaphoreType.DMA((2,)),
            pltpu.SemaphoreType.DMA((4, 4, 2)),
            pltpu.SemaphoreType.DMA((2,)),
        ],
        compiler_params=pltpu.CompilerParams(vmem_limit_bytes=62 * 2**20),
        cost_estimate=pl.CostEstimate(flops=2**30, bytes_accessed=4 * 2**20, transcendentals=0),
    )(meta, row, *first_bufs, *second_bufs, early_own, early_away)


def dot_t(a, b):
    return lax.dot_general(
        a, b, (((0,), (0,)), ((), ())), precision=HIGHEST, preferred_element_type=jnp.float32
    )


def dot_n(a, b):
    return lax.dot_general(
        a, b, (((1,), (0,)), ((), ())), precision=HIGHEST, preferred_element_type=jnp.float32
    )


def factor_block(k, work, u_ref, inv_ref, block, inv):
    n, nb, np_ = 512, 128, 8
    sub = lax.broadcasted_iota(jnp.int32, (np_, nb), 0)
    lane = lax.broadcasted_iota(jnp.int32, (np_, nb), 1)
    lo, hi = k * nb, (k + 1) * nb
    block[...] = work[lo:hi, lo:hi]
    inv[...] = (
        lax.broadcasted_iota(jnp.int32, (nb, nb), 0) == lax.broadcasted_iota(jnp.int32, (nb, nb), 1)
    ).astype(jnp.float32)

    def panel(p, _):
        base = pl.multiple_of(p * np_, np_)
        v = block[pl.ds(base, np_), :]
        xv = inv[pl.ds(base, np_), :]
        rolled = pltpu.roll(v, lax.rem(nb - base, nb), 1)
        pc = [jnp.broadcast_to(rolled[:, i:i + 1], (np_, nb)) for i in range(np_)]
        for i in range(np_):
            s = lax.rsqrt(pc[i][i:i + 1, :])
            u = v[i:i + 1, :] * s
            xu = xv[i:i + 1, :] * s
            below = jnp.where(sub > i, pc[i] * s, 0.0)
            here = sub == i
            for j in range(i + 1, np_):
                pc[j] = pc[j] - below * (pc[j][i:i + 1, :] * s)
            v = jnp.where(here, u, v - below * u)
            xv = jnp.where(here, xu, xv - below * xu)
        v = jnp.where(lane >= base + sub, v, 0.0)
        block[pl.ds(base, np_), :] = v
        inv[pl.ds(base, np_), :] = xv
        later = jnp.where(lane >= base + np_, v, 0.0)
        block[...] -= dot_t(later, v)
        inv[...] -= dot_t(later, xv)
        return 0

    lax.fori_loop(0, nb // np_, panel, 0)
    x = inv[...]
    u_ref[lo:hi, lo:hi] = block[...]
    inv_ref[lo:hi, lo:hi] = x
    if k:
        inner = dot_t(u_ref[0:lo, lo:hi], inv_ref[0:lo, 0:lo])
        inv_ref[lo:hi, 0:lo] = -dot_n(x, inner)
    if hi < n:
        right = dot_n(x, work[lo:hi, hi:n])
        u_ref[lo:hi, hi:n] = right
        work[hi:n, hi:n] -= dot_t(right, right)


def factor_first(scale, sums, work, u_ref, inv_ref, block, inv):
    rid = lax.broadcasted_iota(jnp.int32, (256, 256), 0)
    cid = lax.broadcasted_iota(jnp.int32, (256, 256), 1)

    def regular(part):
        return jnp.where(rid == cid, part * scale, reg_alpha * (part * scale))

    work[...] = jnp.zeros((512, 512), jnp.float32)
    work[:256, :256] = regular(sums[:256])
    work[:256, 256:] = reg_alpha * (sums[256:512] * scale)
    work[256:, 256:] = regular(sums[512:])
    u_ref[...] = jnp.zeros((512, 512), jnp.float32)
    inv_ref[...] = jnp.zeros((512, 512), jnp.float32)
    for k in (0, 1):
        factor_block(k, work, u_ref, inv_ref, block, inv)


def factor_second(work_ref, u_in, inv_in, u_ref, inv_ref, work, block, inv):
    work[...] = work_ref[...]
    u_ref[...] = u_in[...]
    inv_ref[...] = inv_in[...]
    for k in (2, 3):
        factor_block(k, work, u_ref, inv_ref, block, inv)


def factor_part(kernel, n_out, args):
    full = pl.BlockSpec(memory_space=pltpu.VMEM)
    shape = jax.ShapeDtypeStruct((512, 512), jnp.float32)
    small = pltpu.VMEM((128, 128), jnp.float32)
    return pl.pallas_call(
        kernel,
        out_shape=(shape,) * n_out,
        in_specs=[full] * len(args),
        out_specs=(full,) * n_out,
        scratch_shapes=[pltpu.VMEM((512, 512), jnp.float32)] * (3 - n_out) + [small] * 2,
        compiler_params=pltpu.CompilerParams(vmem_limit_bytes=32 * 2**20),
        cost_estimate=pl.CostEstimate(flops=2**20, bytes_accessed=2**20, transcendentals=512),
    )(*args)


def per_device(acts_one, acts_two):
    cal, row, z = (lax.axis_index(a) for a in AXES)
    low, core = cal // 2, cal % 2
    total_tokens = 8 * acts_one.shape[0]
    scale = 1.0 / total_tokens
    device = (cal * 8 + row) * 8 + z
    meta = lax.dynamic_index_in_dim(jnp.asarray(TABLE), device, 0, keepdims=False)
    after = lax.optimization_barrier
    root = lambda x, y, z: (x // 2, y) == (0, 0) and z < 2

    cols = join(acts_one, acts_two)
    piece = transposed(acts_one, acts_two)
    other = move(cols, lambda x, y, z, c: (x, y, 1 - z, c) if root(x, y, z) else None)
    a0, b0 = acts_one[None], acts_two[None]
    a01 = join(a0, move(a0, x_step(0)))
    b01 = join(b0, move(b0, y_step(0)))
    first = join(a01, move(a01, x_step(1)))
    second = join(b01, move(b01, y_step(1)))
    first, second, other, piece = after((first, second, other, piece))

    r0 = move(piece, row_home)
    first1 = move(first, y_step(0))
    second1 = move(second, x_step(0))
    left, right = jnp.where(z == 0, cols, other), jnp.where(z == 0, other, cols)
    part = [
        lax.dot_general(p, q, (((0,), (0,)), ((), ())), preferred_element_type=jnp.float32)
        for p, q in ((left, left), (left, right), (right, right))
    ]
    part = jnp.concatenate(part, 0).reshape(2, 2, 192, 256)
    pick = lambda value, at: lax.dynamic_index_in_dim(value, at, 0, keepdims=False)
    away = move(pick(part, 1 - core), lambda x, y, z, c: (x, y, z, 1 - c) if root(x, y, z) else None)
    lead = pick(part, core) + away
    away = move(pick(lead, 1 - low), lambda x, y, z, c: (x ^ 1, y, z, c) if root(x, y, z) else None)
    lead = jnp.where(row == 0, pick(lead, low) + away, 0.0)
    lead = lead + move(lead, lambda x, y, z, c: (x + 2, y, z, c) if root(x, y, z) else None)
    lead = lead + move(lead, lambda x, y, z, c: (x, 1, z, c) if y == 0 and z < 2 else None)
    lead = lead + move(lead, lambda x, y, z, c: (x, 3 - y, z, c) if y < 2 and z < 2 else None)
    r0, first, first1, second, second1, lead = after((r0, first, first1, second, second1, lead))

    r01 = join(r0, move(r0, z_step(0)))
    theirs = move(lead, lambda x, y, z, c: (x ^ 1, y, z, c) if z < 2 else None)
    lead = jnp.where(low == 0, jnp.stack([lead, theirs]), jnp.stack([theirs, lead]))
    theirs = move(lead, lambda x, y, z, c: (x, y, z, 1 - c) if z < 2 else None)
    lead = jnp.where(core == 0, jnp.stack([lead, theirs]), jnp.stack([theirs, lead]))
    r01, lead, first, first1, second, second1 = after((r01, lead, first, first1, second, second1))

    r2 = move(r01, z_step(1))
    first2 = move(first, y_step(1))
    second2 = move(second, x_step(1))
    state = factor_part(functools.partial(factor_first, scale), 3, (lead.reshape(768, 256),))
    r01, r2, first, first1, first2, second, second1, second2, state = after(
        (r01, r2, first, first1, first2, second, second1, second2, state)
    )

    r3 = move(r2, z_step(2))
    first3 = move(first1, y_step(1))
    second3 = move(second1, x_step(1))
    upper, inverse = factor_part(factor_second, 2, state)
    rows, firsts, seconds, upper, inverse = after(
        (
            (r01, r2, r3),
            (first, first1, first2, first3),
            (second, second1, second2, second3),
            upper,
            inverse,
        )
    )

    row_start = row * 2048 + cal * 512
    meta = meta.at[25].set(row_start).at[26].set(z * 256)
    r4 = move(rows[2], z_step(3))
    early_away = early_part(False, meta, rows, firsts, seconds)
    early_own = early_part(True, meta, rows, firsts, seconds)
    r4, early_away, early_own, firsts, seconds = after((r4, early_away, early_own, firsts, seconds))

    block, away = lead_part(meta, r4, firsts, seconds, early_own, early_away)
    block = block + move(away, lambda x, y, z, c: (x, y, z, 1 - c) if z < 2 else None)
    block = block * scale
    row_ids = row_start + jnp.arange(512, dtype=jnp.int32)[:, None]
    col_ids = z * 256 + jnp.arange(256, dtype=jnp.int32)[None, :]
    block = jnp.where(row_ids == col_ids, block, reg_alpha * block)
    block, r4, early_away, firsts, seconds = after((block, r4, early_away, firsts, seconds))
    left = move(block, lambda x, y, z, c: (x, y, 1, c) if z == 0 else None)
    theirs = late_part(scale, meta, r4, firsts, seconds, early_away)
    left, theirs = after((left, theirs))
    theirs = move(theirs, core_swap)

    def times(weights, rows):
        return lax.dot_general(
            weights, rows, (((1,), (1,)), ((), ())), precision=HIGHEST,
            preferred_element_type=jnp.float32,
        )

    edge = z == 0
    solved = times(jnp.where(edge, inverse[:256, :256], inverse[256:, 256:]), block)
    solved = solved + times(jnp.where(edge, 0.0, inverse[256:, :256]), left)
    head = jnp.where(edge, upper[:256], upper[256:])
    solved = jnp.where((row == 0) & (cal == 0), head, solved).reshape(4, 64, 512)
    share = [jnp.where(edge, solved[0], 0.0)]
    for i in range(4):
        def target(x, y, z, c, i=i):
            if z == 0 and i < 3:
                return x, y, i + 1, c
            return (x, y, i + 4, c) if z == 1 else None

        value = jnp.where(edge, solved[i + 1], solved[i]) if i < 3 else solved[i]
        share.append(move(value, target))

    gram_reg = late_part(scale, meta, r4, firsts, seconds, early_own, other=theirs)
    gram_reg, share = after((gram_reg, share))
    share = functools.reduce(jnp.add, share)
    return gram_reg.reshape(1, 512, 8, 1, 256), share.T.reshape(1, 512, 64)


def solution(mesh):
    return jax.shard_map(
        per_device,
        mesh=mesh,
        in_specs=(P("cal", ("row", "col")), P("cal", ("row", "col"))),
        out_specs=(P("row", "cal", None, "col", None), P("row", "cal", "col")),
        check_vma=False,
    )
```

time: 254 us -> 457 us (1.80)
  Pallas kernels: 79.8 us -> 314 us
  waiting for transfers between devices: 63.3 us -> 29.7 us
  starting transfers between devices: 86.6 us -> 96.4 us
  other arithmetic: 7.9 us -> 3.31 us
    pallas_call x6 -> x13, Pallas kernels: 72.7 us -> 308 us  [the longest x6 221 us: join(): pl.pallas_call(join_kernel, out_shape=jax.ShapeDtypeStruct((rows,) + part...]
    ppermute x30, waiting for transfers between devices: 63.3 us -> 29.7 us  [move(): return lax.ppermute(value, AXES, sorted(pairs))]
    ppermute x30, starting transfers between devices: 86.6 us -> 96.4 us  [move(): return lax.ppermute(value, AXES, sorted(pairs))]
  transfers between devices with their start and end apart: 30 -> 30, of which waited for: 17 -> 10; matrix products, arithmetic and copies ran while one was open for 4% -> 1% of each run, Pallas kernels for 16% -> 57%
where the time goes in v4:
time: 457 us
  Pallas kernels  314 us (69%)
  starting transfers between devices  96.4 us (21%)
  waiting for transfers between devices  29.7 us (6%)
  local copies, waits for them, and re-layouts  7.4 us (2%)
  matrix products  4.85 us (1%)
    pallas_call x6, Pallas kernels, join(): pl.pallas_call(join_kernel, out_shape=jax.ShapeDtypeStruct((rows,) + part...  221 us
    ppermute x30, starting transfers between devices, move(): return lax.ppermute(value, AXES, sorted(pairs))  96.4 us
    pallas_call x2, Pallas kernels, factor_part(): pl.pallas_call(kernel, out_shape=(shape,) * n_out, in_specs=[full] * len(...  38.9 us
    ppermute x30, waiting for transfers between devices, move(): return lax.ppermute(value, AXES, sorted(pairs))  29.7 us
    pallas_call x2, Pallas kernels, early_part(): pl.pallas_call(functools.partial(early_kernel, own), out_shape=jax.ShapeD...  25.5 us
    pallas_call x2, Pallas kernels, late_part(): pl.pallas_call(functools.partial(late_kernel, own, scale), out_shape=jax....  20.4 us
  transfers between devices with their start and end apart: 30, of which 10 were waited for; matrix products, arithmetic and copies ran while one was open for 1% of the time, Pallas kernels for 57%

profile of v4, /device:TPU:1, one launch (start us, length us, event | category | flops | bytes accessed | tf_op | source)
XLA Modules:
  0.0 456.5 jit_solution(4595632100423072053)
XLA Ops:
  0.6 3.4 collective-permute-start
  4.0 2.7 collective-permute-start.2
  6.8 2.6 collective-permute-done.refs_1_
  10.2 24.9 %shard_map.50.refs_0_ = bf16[2,768,256]{2,1,0:T(8,128)(2,1)} custom-call(bf16[1,768,256]{2,1,0:T(8,128)(2,1)} %bitcast.33, bf16[1,768,256]{2,1,0:T(8,128)(2,1)} %copy-done.11), custom_call_target="tpu_custom_call" | custom-call | bytes 1048576 | tf_op jit(solution)/shard_map/pallas_call | solution.py:103
  36.4 24.9 %shard_map.52.refs_0_ = bf16[2,768,256]{2,1,0:T(8,128)(2,1)} custom-call(bf16[1,768,256]{2,1,0:T(8,128)(2,1)} %bitcast.35, bf16[1,768,256]{2,1,0:T(8,128)(2,1)} %copy-done.10), custom_call_target="tpu_custom_call" | custom-call | bytes 1048576 | tf_op jit(solution)/shard_map/pallas_call | solution.py:103
  61.4 1.4 collective-permute-start.3
  62.8 24.9 %shard_map.54 = bf16[1536,256]{1,0:T(8,128)(2,1)} custom-call(bf16[768,256]{1,0:T(8,128)(2,1)} %one_ref.1, bf16[768,256]{1,0:T(8,128)(2,1)} %two_ref.1), custom_call_target="tpu_custom_call" | custom-call | bytes 1048576 | tf_op jit(solution)/shard_map/pallas_call | solution.py:103
  87.7 3.5 collective-permute-start.4
  91.3 2.3 shard_map.55
  94.4 48.8 %shard_map.51.refs_4_.refs_2_ = bf16[4,768,256]{2,1,0:T(8,128)(2,1)} custom-call(bf16[2,768,256]{2,1,0:T(8,128)(2,1)} %shard_map.50.refs_0_, bf16[2,768,256]{2,1,0:T(8,128)(2,1)} %copy-done.7), custom_call_target="tpu_custom_call" | custom-call | bytes 1048576 | tf_op jit(solution)/shard_map/pallas_call | solution.py:103
  144.1 48.8 %shard_map.53.refs_8_.refs_6_ = bf16[4,768,256]{2,1,0:T(8,128)(2,1)} custom-call(bf16[2,768,256]{2,1,0:T(8,128)(2,1)} %shard_map.52.refs_0_, bf16[2,768,256]{2,1,0:T(8,128)(2,1)} %copy-done.8), custom_call_target="tpu_custom_call" | custom-call | bytes 1048576 | tf_op jit(solution)/shard_map/pallas_call | solution.py:103
  194.4 7.1 %collective-permute-start.8 = (f32[2,192,256]{2,1,0:T(8,128)S(1)}, f32[2,192,256]{2,1,0:T(8,128)}, u32[]{:S(2)}, u32[]{:S(2)}) collective-permute-start(f32[2,192,256]{2,1,0:T(8,128)S(1)} %dynamic-slice_bitcast_fusion), channel_id=1, source_target_pairs={{0,64},{1,65},{64,0},{65,1},{128,192},{129,193},{192,128},{193,129}} | collective-permute-start | bytes 1179656 | tf_op jit(solution)/shard_map/ppermute | solution.py:36
  201.8 1.2 collective-permute-done.8
  204.1 1.9 collective-permute-start.9
  206.1 1.5 collective-permute-start.5
  207.6 5.5 %collective-permute-done.9 = f32[192,256]{1,0:T(8,128)S(1)} collective-permute-done((f32[192,256]{1,0:T(8,128)S(1)}, f32[192,256]{1,0:T(8,128)S(1)}, u32[]{:S(2)}, u32[]{:S(2)}) %collective-permute-start.9) | collective-permute-done | bytes 196640 | tf_op jit(solution)/shard_map/ppermute | solution.py:36
  213.1 1.3 collective-permute-start.10
  214.4 4.8 %collective-permute-done.10 = f32[192,256]{1,0:T(8,128)S(1)} collective-permute-done((f32[192,256]{1,0:T(8,128)S(1)}, f32[192,256]{1,0:T(8,128)S(1)}, u32[]{:S(2)}, u32[]{:S(2)}) %collective-permute-start.10) | collective-permute-done | bytes 196640 | tf_op jit(solution)/shard_map/ppermute | solution.py:36
  219.2 1.3 collective-permute-start.11
  220.5 2.6 collective-permute-done.11
  223.1 1.3 collective-permute-start.12
  224.4 2.6 collective-permute-done.12
  227.1 22.3 %collective-permute-start.14 = (f32[192,256]{1,0:T(8,128)S(1)}, f32[192,256]{1,0:T(8,128)S(1)}, u32[]{:S(2)}, u32[]{:S(2)}) collective-permute-start(f32[192,256]{1,0:T(8,128)S(1)} %add.112), channel_id=1, source_target_pairs={{0,128},{1,129},{8,136},{9,137},{16,144},{17,145},{24,152},{25,153... | collective-permute-start | bytes 589832 | tf_op jit(solution)/shard_map/ppermute | solution.py:36
  249.5 2.9 collective-permute-done.14
  252.5 14.3 %collective-permute-start.15 = (f32[2,192,256]{2,1,0:T(8,128)S(1)}, f32[2,192,256]{2,1,0:T(8,128)S(1)}, u32[]{:S(2)}, u32[]{:S(2)}) collective-permute-start(f32[2,192,256]{2,1,0:T(8,128)S(1)} %maximum_select_fusion.2), channel_id=1, source_target_pairs={{0,64},{1,65},{8,72},{9,73},{16,80},{17,81},{24,88},{25,89},{32,96... | collective-permute-start | bytes 1179656 | tf_op jit(solution)/shard_map/ppermute | solution.py:36
  266.8 1.3 collective-permute-done.15
  269.1 48.8 %shard_map.56.refs_1_ = bf16[2,256,1536]{2,1,0:T(8,128)(2,1)} custom-call(bf16[1,256,1536]{2,1,0:T(8,128)(2,1)} %collective-permute-done.5.refs_0_, bf16[1,256,1536]{2,1,0:T(8,128)(2,1)} %copy-done.9), custom_call_target="tpu_custom_call" | custom-call | bytes 1048576 | tf_op jit(solution)/shard_map/pallas_call | solution.py:103
  317.9 1.5 collective-permute-start.16
  319.4 2.2 collective-permute-start.17
  321.6 1.7 collective-permute-start.18
  323.2 19.5 %shard_map.57 = (f32[512,512]{1,0:T(8,128)S(1)}, f32[512,512]{1,0:T(8,128)S(1)}, f32[512,512]{1,0:T(8,128)S(1)}) custom-call(f32[768,256]{1,0:T(8,128)S(1)} %bitcast.30), custom_call_target="tpu_custom_call" | custom-call | flops 1048576 | bytes 1048576 | tf_op jit(solution)/shard_map/pallas_call | solution.py:453
  344.0 19.4 %shard_map.58 = (f32[512,512]{1,0:T(8,128)S(1)}, f32[512,512]{1,0:T(8,128)S(1)}) custom-call(f32[512,512]{1,0:T(8,128)S(1)} %get-tuple-element.130.work_ref, f32[512,512]{1,0:T(8,128)S(1)} %get-tuple-element.131.u_in, f32[512,512]{1,0:T(8,128)S(1)} %get-tuple-element.132.inv_in), custom_call_target="tpu_custom_call" | custom-call | flops 1048576 | bytes 1048576 | tf_op jit(solution)/shard_map/pallas_call | solution.py:453
  365.8 12.5 %shard_map.60.refs_10_ = f32[8,512,256]{2,1,0:T(8,128)} custom-call(s32[32]{0:T(128)} %copy-done.12, bf16[2,256,1536]{2,1,0:T(8,128)(2,1)} %shard_map.56.refs_1_, bf16[2,256,1536]{2,1,0:T(8,128)(2,1)} %copy-done.4, bf16[2,256,1536]{2,1,0:T(8,128)(2,1)} %collective-permute-done.19.refs_3_, bf16[4,768,256]{2,1,0:T(8,128)(2,1)} %shard_map.51.refs_4_.refs_2_, ...), custom_call_target="tpu_custom_call" | custom-call | flops 1048576 | bytes 1048576 | tf_op jit(solution)/shard_map/pallas_call | solution.py:204
  378.4 13.0 %shard_map.59.refs_11_.refs_10_ = f32[8,512,256]{2,1,0:T(8,128)} custom-call(s32[32]{0:T(128)} %copy-done.12, bf16[2,256,1536]{2,1,0:T(8,128)(2,1)} %shard_map.56.refs_1_, bf16[2,256,1536]{2,1,0:T(8,128)(2,1)} %copy-done.4, bf16[2,256,1536]{2,1,0:T(8,128)(2,1)} %collective-permute-done.19.refs_3_, bf16[4,768,256]{2,1,0:T(8,128)(2,1)} %shard_map.51.refs_4_.refs_2_, ...), custom_call_target="tpu_custom_call" | custom-call | flops 1048576 | bytes 1048576 | tf_op jit(solution)/shard_map/pallas_call | solution.py:204
  391.3 5.4 %shard_map.61 = (f32[512,256]{1,0:T(8,128)}, f32[512,256]{1,0:T(8,128)}) custom-call(s32[32]{0:T(128)} %copy-done.12, bf16[2,256,1536]{2,1,0:T(8,128)(2,1)} %collective-permute-done.22.refs_1_, bf16[4,768,256]{2,1,0:T(8,128)(2,1)} %shard_map.51.refs_4_.refs_2_, bf16[4,768,256]{2,1,0:T(8,128)(2,1)} %collective-permute-done.6.refs_5_.refs_3_, ...), custom_call_target="tpu_custom_call" | custom-call | flops 1073741824 | bytes 4194304 | tf_op jit(solution)/shard_map/pallas_call | solution.py:348
  396.7 13.4 %collective-permute-start.23 = (f32[512,256]{1,0:T(8,128)}, f32[512,256]{1,0:T(8,128)S(1)}, u32[]{:S(2)}, u32[]{:S(2)}) collective-permute-start(f32[512,256]{1,0:T(8,128)} %get-tuple-element.158), channel_id=1, source_target_pairs={{0,64},{1,65},{8,72},{9,73},{16,80},{17,81},{24,88},{25,89},{32,96... | collective-permute-start | bytes 1572872 | tf_op jit(solution)/shard_map/ppermute | solution.py:36
  410.2 1.7 collective-permute-done.23
  411.9 1.2 multiply_select_fusion
  413.1 4.9 %collective-permute-start.24 = (f32[512,256]{1,0:T(8,128)S(1)}, f32[512,256]{1,0:T(8,128)}, u32[]{:S(2)}, u32[]{:S(2)}) collective-permute-start(f32[512,256]{1,0:T(8,128)S(1)} %multiply_select_fusion), channel_id=1, source_target_pairs={{0,1},{8,9},{16,17},{24,25},{32,33},{40,41},{48,49},{56,57},{64,65... | collective-permute-start | bytes 1572872 | tf_op jit(solution)/shard_map/ppermute | solution.py:36
  418.0 5.6 %shard_map.62 = f32[8,512,256]{2,1,0:T(8,128)} custom-call(s32[32]{0:T(128)} %copy-done.12, bf16[2,256,1536]{2,1,0:T(8,128)(2,1)} %collective-permute-done.22.refs_1_, bf16[4,768,256]{2,1,0:T(8,128)(2,1)} %shard_map.51.refs_4_.refs_2_, bf16[4,768,256]{2,1,0:T(8,128)(2,1)} %collective-permute-done.6.refs_5_.refs_3_, bf16[4,768,256]{2,1,0:T(8,128)(2,1)} %copy-done.2, ...), custom_call_target="tpu_custom_call" | custom-call | flops 6442450944 | bytes 25165824 | tf_op jit(solution)/shard_map/pallas_call | solution.py:291
  423.6 4.5 collective-permute-done.24
  428.1 1.2 collective-permute-start.25
  429.3 1.7 fusion.7
  431.0 1.8 select_select_fusion
  433.5 1.3 collective-permute-start.28
  434.8 1.3 collective-permute-start.27
  436.1 4.8 %collective-permute-start.26 = (f32[64,512]{1,0:T(8,128)S(1)}, f32[64,512]{1,0:T(8,128)S(1)}, u32[]{:S(2)}, u32[]{:S(2)}) collective-permute-start(f32[64,512]{1,0:T(8,128)S(1)} %get-tuple-element.185), channel_id=1, source_target_pairs={{0,1},{1,4},{8,9},{9,12},{16,17},{17,20},{24,25},{25,28},{32,33},{... | collective-permute-start | bytes 393224 | tf_op jit(solution)/shard_map/ppermute | solution.py:36
  441.0 14.8 %shard_map.63 = f32[8192,128]{1,0:T(8,128)} custom-call(s32[32]{0:T(128)} %copy-done.12, bf16[2,256,1536]{2,1,0:T(8,128)(2,1)} %collective-permute-done.22.refs_1_, bf16[4,768,256]{2,1,0:T(8,128)(2,1)} %shard_map.51.refs_4_.refs_2_, bf16[4,768,256]{2,1,0:T(8,128)(2,1)} %collective-permute-done.6.refs_5_.refs_3_, bf16[4,768,256]{2,1,0:T(8,128)(2,1)} %copy-done.2, ...), custom_call_target="tpu_custom_call" | custom-call | flops 6442450944 | bytes 25165824 | tf_op jit(solution)/shard_map/pallas_call | solution.py:291
  (76 shorter events, 12.8 us)
Async XLA Ops:
  0.6 8.8 %collective-permute-start = (bf16[1,768,256]{2,1,0:T(8,128)(2,1)}, bf16[1,768,256]{2,1,0:T(8,128)(2,1)S(1)}, u32[]{:S(2)}, u32[]{:S(2)}) collective-permute-start(bf16[1,768,256]{2,1,0:T(8,128)(2,1)} %bitcast.32), channel_id=1, source_target_pairs={{0,128},{1,129},{2,130},{3,131},{4,132},{5,133},{6,134},{7,135},{8... | collective-permute-start | bytes 1179656 | tf_op jit(solution)/shard_map/ppermute | solution.py:36
  4.0 31.6 %collective-permute-start.2 = (bf16[1,768,256]{2,1,0:T(8,128)(2,1)}, bf16[1,768,256]{2,1,0:T(8,128)(2,1)S(1)}, u32[]{:S(2)}, u32[]{:S(2)}) collective-permute-start(bf16[1,768,256]{2,1,0:T(8,128)(2,1)} %bitcast.34), channel_id=1, source_target_pairs={{0,8},{1,9},{2,10},{3,11},{4,12},{5,13},{6,14},{7,15},{8,0},{9,1},... | collective-permute-start | bytes 1179656 | tf_op jit(solution)/shard_map/ppermute | solution.py:36
  9.4 0.7 copy-start.11
  35.1 58.4 %collective-permute-start.1 = (bf16[2,768,256]{2,1,0:T(8,128)(2,1)}, bf16[2,768,256]{2,1,0:T(8,128)(2,1)S(1)}, u32[]{:S(2)}, u32[]{:S(2)}) collective-permute-start(bf16[2,768,256]{2,1,0:T(8,128)(2,1)} %shard_map.50.refs_0_), channel_id=1, source_target_pairs={{0,160},{1,161},{2,162},{3,163},{4,164},{5,165},{6,166},{7,167},{8... | collective-permute-start | bytes 2359304 | tf_op jit(solution)/shard_map/ppermute | solution.py:36
  35.7 0.7 copy-start.10
  61.4 81.8 %collective-permute-start.3 = (bf16[2,768,256]{2,1,0:T(8,128)(2,1)}, bf16[2,768,256]{2,1,0:T(8,128)(2,1)S(1)}, u32[]{:S(2)}, u32[]{:S(2)}) collective-permute-start(bf16[2,768,256]{2,1,0:T(8,128)(2,1)} %shard_map.52.refs_0_), channel_id=1, source_target_pairs={{0,24},{1,25},{2,26},{3,27},{4,28},{5,29},{6,30},{7,31},{8,16},{9,... | collective-permute-start | bytes 2359304 | tf_op jit(solution)/shard_map/ppermute | solution.py:36
  87.7 105.2 %collective-permute-start.4 = (bf16[1536,256]{1,0:T(8,128)(2,1)}, bf16[1536,256]{1,0:T(8,128)(2,1)S(1)}, u32[]{:S(2)}, u32[]{:S(2)}) collective-permute-start(bf16[1536,256]{1,0:T(8,128)(2,1)} %shard_map.54), channel_id=1, source_target_pairs={{0,1},{1,0},{64,65},{65,64},{128,129},{129,128},{192,193},{193,192}} | collective-permute-start | bytes 2359304 | tf_op jit(solution)/shard_map/ppermute | solution.py:36
  93.5 0.9 copy-start.7
  143.2 49.7 %copy-start.6 = (bf16[1536,256]{1,0:T(8,128)(2,1)S(1)}, bf16[1536,256]{1,0:T(8,128)(2,1)}, u32[]{:S(2)}) copy-start(bf16[1536,256]{1,0:T(8,128)(2,1)} %shard_map.54) | copy-start | bytes 2359300
  143.2 0.9 copy-start.8
  194.3 7.3 %copy-start.1 = (bf16[4,768,256]{2,1,0:T(8,128)(2,1)S(1)}, bf16[4,768,256]{2,1,0:T(8,128)(2,1)}, u32[]{:S(2)}) copy-start(bf16[4,768,256]{2,1,0:T(8,128)(2,1)} %shard_map.51.refs_4_.refs_2_) | copy-start | bytes 4718596
  194.4 11.7 %copy-start.5 = (bf16[1,256,1536]{2,1,0:T(8,128)(2,1)S(1)}, bf16[1,256,1536]{2,1,0:T(8,128)(2,1)}, u32[]{:S(2)}) copy-start(bf16[1,256,1536]{2,1,0:T(8,128)(2,1)} %shard_map.55) | copy-start | bytes 2359300
  194.4 8.6 %collective-permute-start.8 = (f32[2,192,256]{2,1,0:T(8,128)S(1)}, f32[2,192,256]{2,1,0:T(8,128)}, u32[]{:S(2)}, u32[]{:S(2)}) collective-permute-start(f32[2,192,256]{2,1,0:T(8,128)S(1)} %dynamic-slice_bitcast_fusion), channel_id=1, source_target_pairs={{0,64},{1,65},{64,0},{65,1},{128,192},{129,193},{192,128},{193,129}} | collective-permute-start | bytes 1179656 | tf_op jit(solution)/shard_map/ppermute | solution.py:36
  201.6 25.5 %collective-permute-start.6 = (bf16[4,768,256]{2,1,0:T(8,128)(2,1)S(1)}, bf16[4,768,256]{2,1,0:T(8,128)(2,1)}, u32[]{:S(2)}, u32[]{:S(2)}) collective-permute-start(bf16[4,768,256]{2,1,0:T(8,128)(2,1)S(1)} %copy-done.1), channel_id=1, source_target_pairs={{0,8},{1,9},{2,10},{3,11},{4,12},{5,13},{6,14},{7,15},{8,0},{9,1},... | collective-permute-start | bytes 4718600 | tf_op jit(solution)/shard_map/ppermute | solution.py:36
  201.7 25.4 %collective-permute-start.7 = (bf16[4,768,256]{2,1,0:T(8,128)(2,1)}, bf16[4,768,256]{2,1,0:T(8,128)(2,1)}, u32[]{:S(2)}, u32[]{:S(2)}) collective-permute-start(bf16[4,768,256]{2,1,0:T(8,128)(2,1)} %shard_map.53.refs_8_.refs_6_), channel_id=1, source_target_pairs={{0,128},{1,129},{2,130},{3,131},{4,132},{5,133},{6,134},{7,135},{8... | collective-permute-start | bytes 4718600 | tf_op jit(solution)/shard_map/ppermute | solution.py:36
  204.1 9.0 %collective-permute-start.9 = (f32[192,256]{1,0:T(8,128)S(1)}, f32[192,256]{1,0:T(8,128)S(1)}, u32[]{:S(2)}, u32[]{:S(2)}) collective-permute-start(f32[192,256]{1,0:T(8,128)S(1)} %dynamic-slice_bitcast_fusion.1), channel_id=1, source_target_pairs={{0,128},{1,129},{64,192},{65,193},{128,0},{129,1},{192,64},{193,65}} | collective-permute-start | bytes 589832 | tf_op jit(solution)/shard_map/ppermute | solution.py:36
  206.1 21.0 %collective-permute-start.5 = (bf16[1,256,1536]{2,1,0:T(8,128)(2,1)S(1)}, bf16[1,256,1536]{2,1,0:T(8,128)(2,1)}, u32[]{:S(2)}, u32[]{:S(2)}) collective-permute-start(bf16[1,256,1536]{2,1,0:T(8,128)(2,1)S(1)} %copy-done.5), channel_id=1, source_target_pairs={{0,0},{1,1},{2,2},{3,3},{4,131},{5,130},{6,129},{7,128},{8,8},{9,9... | collective-permute-start | bytes 2359304 | tf_op jit(solution)/shard_map/ppermute | solution.py:36
  213.1 6.1 %collective-permute-start.10 = (f32[192,256]{1,0:T(8,128)S(1)}, f32[192,256]{1,0:T(8,128)S(1)}, u32[]{:S(2)}, u32[]{:S(2)}) collective-permute-start(f32[192,256]{1,0:T(8,128)S(1)} %fusion.11), channel_id=1, source_target_pairs={{0,32},{1,33},{64,96},{65,97},{128,160},{129,161},{192,224},{193,2... | collective-permute-start | bytes 589832 | tf_op jit(solution)/shard_map/ppermute | solution.py:36
  219.2 3.9 collective-permute-start.11
  223.1 3.9 collective-permute-start.12
  227.1 25.4 %collective-permute-start.14 = (f32[192,256]{1,0:T(8,128)S(1)}, f32[192,256]{1,0:T(8,128)S(1)}, u32[]{:S(2)}, u32[]{:S(2)}) collective-permute-start(f32[192,256]{1,0:T(8,128)S(1)} %add.112), channel_id=1, source_target_pairs={{0,128},{1,129},{8,136},{9,137},{16,144},{17,145},{24,152},{25,153... | collective-permute-start | bytes 589832 | tf_op jit(solution)/shard_map/ppermute | solution.py:36
  249.4 18.8 %collective-permute-start.13 = (bf16[1,256,1536]{2,1,0:T(8,128)(2,1)}, bf16[1,256,1536]{2,1,0:T(8,128)(2,1)S(1)}, u32[]{:S(2)}, u32[]{:S(2)}) collective-permute-start(bf16[1,256,1536]{2,1,0:T(8,128)(2,1)} %collective-permute-done.5.refs_0_), channel_id=1, source_target_pairs={{0,1},{1,0},{2,3},{3,2},{4,5},{5,4},{6,7},{7,6},{8,9},{9,8},{10,11... | collective-permute-start | bytes 2359304 | tf_op jit(solution)/shard_map/ppermute | solution.py:36
  252.5 15.6 %collective-permute-start.15 = (f32[2,192,256]{2,1,0:T(8,128)S(1)}, f32[2,192,256]{2,1,0:T(8,128)S(1)}, u32[]{:S(2)}, u32[]{:S(2)}) collective-permute-start(f32[2,192,256]{2,1,0:T(8,128)S(1)} %maximum_select_fusion.2), channel_id=1, source_target_pairs={{0,64},{1,65},{8,72},{9,73},{16,80},{17,81},{24,88},{25,89},{32,96... | collective-permute-start | bytes 1179656 | tf_op jit(solution)/shard_map/ppermute | solution.py:36
  268.2 0.9 copy-start.9
  317.9 24.9 %collective-permute-start.16 = (bf16[2,256,1536]{2,1,0:T(8,128)(2,1)}, bf16[2,256,1536]{2,1,0:T(8,128)(2,1)S(1)}, u32[]{:S(2)}, u32[]{:S(2)}) collective-permute-start(bf16[2,256,1536]{2,1,0:T(8,128)(2,1)} %shard_map.56.refs_1_), channel_id=1, source_target_pairs={{0,7},{1,2},{2,1},{3,4},{4,3},{5,6},{6,5},{7,0},{8,15},{9,10},{10,... | collective-permute-start | bytes 4718600 | tf_op jit(solution)/shard_map/ppermute | solution.py:36
  319.4 23.4 %collective-permute-start.17 = (bf16[4,768,256]{2,1,0:T(8,128)(2,1)S(1)}, bf16[4,768,256]{2,1,0:T(8,128)(2,1)S(1)}, u32[]{:S(2)}, u32[]{:S(2)}) collective-permute-start(bf16[4,768,256]{2,1,0:T(8,128)(2,1)S(1)} %copy-done.1), channel_id=1, source_target_pairs={{0,24},{1,25},{2,26},{3,27},{4,28},{5,29},{6,30},{7,31},{8,16},{9,... | collective-permute-start | bytes 4718600 | tf_op jit(solution)/shard_map/ppermute | solution.py:36
  321.6 21.2 %collective-permute-start.18 = (bf16[4,768,256]{2,1,0:T(8,128)(2,1)}, bf16[4,768,256]{2,1,0:T(8,128)(2,1)S(1)}, u32[]{:S(2)}, u32[]{:S(2)}) collective-permute-start(bf16[4,768,256]{2,1,0:T(8,128)(2,1)} %shard_map.53.refs_8_.refs_6_), channel_id=1, source_target_pairs={{0,160},{1,161},{2,162},{3,163},{4,164},{5,165},{6,166},{7,167},{8... | collective-permute-start | bytes 4718600 | tf_op jit(solution)/shard_map/ppermute | solution.py:36
  342.8 21.6 %copy-start.4 = (bf16[2,256,1536]{2,1,0:T(8,128)(2,1)}, bf16[2,256,1536]{2,1,0:T(8,128)(2,1)S(1)}, u32[]{:S(2)}) copy-start(bf16[2,256,1536]{2,1,0:T(8,128)(2,1)S(1)} %collective-permute-done.16.refs_2_) | copy-start | bytes 4718596
  342.8 1.2 copy-start.2
  342.8 20.6 %copy-start.3 = (bf16[4,768,256]{2,1,0:T(8,128)(2,1)}, bf16[4,768,256]{2,1,0:T(8,128)(2,1)S(1)}, u32[]{:S(2)}) copy-start(bf16[4,768,256]{2,1,0:T(8,128)(2,1)S(1)} %collective-permute-done.18.refs_10_.refs_8_) | copy-start | bytes 4718596
  342.8 21.6 %collective-permute-start.19 = (bf16[2,256,1536]{2,1,0:T(8,128)(2,1)S(1)}, bf16[2,256,1536]{2,1,0:T(8,128)(2,1)}, u32[]{:S(2)}, u32[]{:S(2)}) collective-permute-start(bf16[2,256,1536]{2,1,0:T(8,128)(2,1)S(1)} %collective-permute-done.16.refs_2_), channel_id=1, source_target_pairs={{0,1},{1,0},{2,3},{3,2},{4,5},{5,4},{6,7},{7,6},{8,9},{9,8},{10,11... | collective-permute-start | bytes 4718600 | tf_op jit(solution)/shard_map/ppermute | solution.py:36
  342.9 21.5 %collective-permute-start.20 = (bf16[4,768,256]{2,1,0:T(8,128)(2,1)}, bf16[4,768,256]{2,1,0:T(8,128)(2,1)}, u32[]{:S(2)}, u32[]{:S(2)}) collective-permute-start(bf16[4,768,256]{2,1,0:T(8,128)(2,1)} %collective-permute-done.6.refs_5_.refs_3_), channel_id=1, source_target_pairs={{0,24},{1,25},{2,26},{3,27},{4,28},{5,29},{6,30},{7,31},{8,16},{9,... | collective-permute-start | bytes 4718600 | tf_op jit(solution)/shard_map/ppermute | solution.py:36
  344.0 20.4 %collective-permute-start.21 = (bf16[4,768,256]{2,1,0:T(8,128)(2,1)}, bf16[4,768,256]{2,1,0:T(8,128)(2,1)}, u32[]{:S(2)}, u32[]{:S(2)}) collective-permute-start(bf16[4,768,256]{2,1,0:T(8,128)(2,1)} %collective-permute-done.7.refs_9_.refs_7_), channel_id=1, source_target_pairs={{0,160},{1,161},{2,162},{3,163},{4,164},{5,165},{6,166},{7,167},{8... | collective-permute-start | bytes 4718600 | tf_op jit(solution)/shard_map/ppermute | solution.py:36
  363.4 1.0 copy-start
  364.4 26.9 %collective-permute-start.22 = (bf16[2,256,1536]{2,1,0:T(8,128)(2,1)}, bf16[2,256,1536]{2,1,0:T(8,128)(2,1)}, u32[]{:S(2)}, u32[]{:S(2)}) collective-permute-start(bf16[2,256,1536]{2,1,0:T(8,128)(2,1)} %collective-permute-done.19.refs_3_), channel_id=1, source_target_pairs={{0,7},{1,2},{2,1},{3,4},{4,3},{5,6},{6,5},{7,0},{8,15},{9,10},{10,... | collective-permute-start | bytes 4718600 | tf_op jit(solution)/shard_map/ppermute | solution.py:36
  365.3 0.5 copy-start.12
  396.7 15.2 %collective-permute-start.23 = (f32[512,256]{1,0:T(8,128)}, f32[512,256]{1,0:T(8,128)S(1)}, u32[]{:S(2)}, u32[]{:S(2)}) collective-permute-start(f32[512,256]{1,0:T(8,128)} %get-tuple-element.158), channel_id=1, source_target_pairs={{0,64},{1,65},{8,72},{9,73},{16,80},{17,81},{24,88},{25,89},{32,96... | collective-permute-start | bytes 1572872 | tf_op jit(solution)/shard_map/ppermute | solution.py:36
  413.1 15.0 %collective-permute-start.24 = (f32[512,256]{1,0:T(8,128)S(1)}, f32[512,256]{1,0:T(8,128)}, u32[]{:S(2)}, u32[]{:S(2)}) collective-permute-start(f32[512,256]{1,0:T(8,128)S(1)} %multiply_select_fusion), channel_id=1, source_target_pairs={{0,1},{8,9},{16,17},{24,25},{32,33},{40,41},{48,49},{56,57},{64,65... | collective-permute-start | bytes 1572872 | tf_op jit(solution)/shard_map/ppermute | solution.py:36
  428.1 12.9 %collective-permute-start.25 = (f32[8,512,256]{2,1,0:T(8,128)}, f32[8,512,256]{2,1,0:T(8,128)}, u32[]{:S(2)}, u32[]{:S(2)}) collective-permute-start(f32[8,512,256]{2,1,0:T(8,128)} %shard_map.62), channel_id=1, source_target_pairs={{0,64},{1,65},{2,66},{3,67},{4,68},{5,69},{6,70},{7,71},{8,72},{9,... | collective-permute-start | bytes 12582920 | tf_op jit(solution)/shard_map/ppermute | solution.py:36
  432.9 22.9 %collective-permute-start.29 = (f32[64,512]{1,0:T(8,128)S(1)}, f32[64,512]{1,0:T(8,128)S(1)}, u32[]{:S(2)}, u32[]{:S(2)}) collective-permute-start(f32[64,512]{1,0:T(8,128)S(1)} %get-tuple-element.182), channel_id=1, source_target_pairs={{1,7},{9,15},{17,23},{25,31},{33,39},{41,47},{49,55},{57,63},{65,7... | collective-permute-start | bytes 393224 | tf_op jit(solution)/shard_map/ppermute | solution.py:36
  433.5 22.3 %collective-permute-start.28 = (f32[64,512]{1,0:T(8,128)S(1)}, f32[64,512]{1,0:T(8,128)S(1)}, u32[]{:S(2)}, u32[]{:S(2)}) collective-permute-start(f32[64,512]{1,0:T(8,128)S(1)} %get-tuple-element.183), channel_id=1, source_target_pairs={{0,3},{1,6},{8,11},{9,14},{16,19},{17,22},{24,27},{25,30},{32,35},... | collective-permute-start | bytes 393224 | tf_op jit(solution)/shard_map/ppermute | solution.py:36
  434.8 21.0 %collective-permute-start.27 = (f32[64,512]{1,0:T(8,128)S(1)}, f32[64,512]{1,0:T(8,128)S(1)}, u32[]{:S(2)}, u32[]{:S(2)}) collective-permute-start(f32[64,512]{1,0:T(8,128)S(1)} %get-tuple-element.184), channel_id=1, source_target_pairs={{0,2},{1,5},{8,10},{9,13},{16,18},{17,21},{24,26},{25,29},{32,34},... | collective-permute-start | bytes 393224 | tf_op jit(solution)/shard_map/ppermute | solution.py:36
  436.1 19.7 %collective-permute-start.26 = (f32[64,512]{1,0:T(8,128)S(1)}, f32[64,512]{1,0:T(8,128)S(1)}, u32[]{:S(2)}, u32[]{:S(2)}) collective-permute-start(f32[64,512]{1,0:T(8,128)S(1)} %get-tuple-element.185), channel_id=1, source_target_pairs={{0,1},{1,4},{8,9},{9,12},{16,17},{17,20},{24,25},{25,28},{32,33},{... | collective-permute-start | bytes 393224 | tf_op jit(solution)/shard_map/ppermute | solution.py:36
